TPU v7x, 256 devices: a whole 4x4x8 slice. The times are simulated.
256 devices in a mesh: grp: 8 (over z_lo, core), dev: 32 (over x, y, z_hi).
Axes of the slice: x: 4, y: 4, z: 8 (z_hi: 2, z_lo: 4; z = z_hi * 4 + z_lo), core: 2. Of those that a mesh axis runs over, the one named last changes fastest.
Arguments:
- rollout: bfloat16 [256, 512, 1024], P('dev', 'grp'), may hold values from -6 to 6
- agent_gain: float32 [1024], replicated, may hold values from 0.25 to 1.75
- time_gain: float32 [1024], replicated, may hold values from 0.25 to 1.75
- inner_gain: float32 [1024], replicated, may hold values from 0.25 to 1.75
- agent_pair: bfloat16 [2, 1024, 512], replicated
- agent_value: bfloat16 [1024, 512], replicated, may hold values from -0.1875 to 0.1875
- agent_out: bfloat16 [512, 1024], replicated, may hold values from -0.25 to 0.25
- time_pair: bfloat16 [2, 1024, 512], replicated
- time_value: bfloat16 [1024, 512], replicated, may hold values from -0.1875 to 0.1875
- time_out: bfloat16 [512, 1024], replicated, may hold values from -0.25 to 0.25
- expand_weight: bfloat16 [1024, 2048], P('dev'), may hold values from -0.1875 to 0.1875
- reduce_weight: bfloat16 [2048, 1024], P(None, 'dev'), may hold values from -0.125 to 0.125
- episode_start: int32 [512], P(('grp', 'dev')), may hold values from 0 to 255, as said below
Outputs:
- layer_out: bfloat16 [256, 512, 1024], P('dev', 'grp')
Inputs may be any that keep to these rules, and one draw needn't show every extreme that they name: episode_start[a] is the first step of agent a's current episode; earlier steps belong to its previous episode.
All inputs are finite; a program needn't handle non-finite values.
Results may differ from a plain program's by a relative error of at most 0.017.
Values may be sent and summed in bfloat16 or wider, within the bound.
No kernel may reach another device: no remote copies, remote signals or barrier semaphores. Data moves between devices by JAX's collectives and lax.ppermute only.
A program may use at most 128 MiB of HBM per device.

v0:
```python
import jax
import jax.numpy as jnp
from jax import lax
from jax.sharding import PartitionSpec as P

HDIM = 64


def rms_scale(row_block, gain_vec):
    widened = row_block.astype(jnp.float32)
    inverse = lax.rsqrt(jnp.mean(widened * widened, axis=-1, keepdims=True) + 1e-05)
    return (widened * inverse * gain_vec).astype(jnp.bfloat16)


def linear(row_block, weight):
    row_shape = row_block.shape
    flat_rows = row_block.reshape(-1, row_shape[-1])
    product = jnp.dot(flat_rows, weight, preferred_element_type=jnp.float32)
    return product.reshape(row_shape[:-1] + (weight.shape[1],))


def agent_attend(queries, key_rows, values):
    step_count, query_count, span_width = queries.shape
    head_count = span_width // HDIM
    query_heads = queries.reshape(step_count, query_count, head_count, HDIM)
    key_heads = key_rows.reshape(step_count, key_rows.shape[1], head_count, HDIM)
    value_heads = values.reshape(step_count, values.shape[1], head_count, HDIM)
    scores = jnp.einsum(
        "tihd,tjhd->thij", query_heads, key_heads, preferred_element_type=jnp.float32
    ) * HDIM ** (-0.5)
    peak_score = jnp.max(scores, axis=-1, keepdims=True)
    exponent = jnp.exp(scores - peak_score)
    weight_sum = jnp.sum(exponent, axis=-1)
    rounded = exponent.astype(jnp.bfloat16)
    weighted = jnp.einsum(
        "thij,tjhd->tihd", rounded, value_heads, preferred_element_type=jnp.float32
    )
    context = weighted / jnp.transpose(weight_sum, (0, 2, 1))[..., None]
    return context.reshape(step_count, query_count, span_width).astype(jnp.bfloat16)


def time_attend(queries, key_rows, values, offsets):
    step_count, agent_count, span_width = queries.shape
    head_count = span_width // HDIM
    query_heads = queries.reshape(step_count, agent_count, head_count, HDIM)
    key_heads = key_rows.reshape(step_count, agent_count, head_count, HDIM)
    value_heads = values.reshape(step_count, agent_count, head_count, HDIM)
    scores = jnp.einsum(
        "iahd,jahd->ahij", query_heads, key_heads, preferred_element_type=jnp.float32
    ) * HDIM ** (-0.5)
    places = lax.iota(jnp.int32, step_count)
    causal = places[:, None] >= places[None, :]
    begins = offsets[:, None, None]
    visible = causal[None] & ((places[None, None, :] >= begins) | (places[None, :, None] < begins))
    visible = visible[:, None]
    masked = jnp.where(visible, scores, -1e30)
    peak_score = jnp.max(masked, axis=-1, keepdims=True)
    exponent = jnp.where(visible, jnp.exp(masked - peak_score), 0.0)
    weight_sum = jnp.sum(exponent, axis=-1)
    rounded = exponent.astype(jnp.bfloat16)
    weighted = jnp.einsum(
        "ahij,jahd->iahd", rounded, value_heads, preferred_element_type=jnp.float32
    )
    context = weighted / jnp.transpose(weight_sum, (2, 0, 1))[..., None]
    return context.reshape(step_count, agent_count, span_width).astype(jnp.bfloat16)


def agent_block(row_block, agent_gain, agent_pair, agent_value):
    normed = rms_scale(row_block, agent_gain)
    queries = linear(normed, agent_pair[0]).astype(jnp.bfloat16)
    key_rows = linear(normed, agent_pair[1]).astype(jnp.bfloat16)
    values = linear(normed, agent_value).astype(jnp.bfloat16)
    return (queries, key_rows, values)


def on_device(
    rollout,
    agent_gain,
    time_gain,
    inner_gain,
    agent_pair,
    agent_value,
    agent_out,
    time_pair,
    time_value,
    time_out,
    expand_weight,
    reduce_weight,
    episode_start,
):
    queries, key_rows, values = agent_block(rollout, agent_gain, agent_pair, agent_value)
    all_keys, all_values = (
        lax.all_gather(key_rows, "grp", axis=1, tiled=True),
        lax.all_gather(values, "grp", axis=1, tiled=True),
    )
    context = agent_attend(queries, all_keys, all_values)
    after_agents = (rollout.astype(jnp.float32) + linear(context, agent_out)).astype(jnp.bfloat16)
    series = lax.all_to_all(after_agents, "dev", split_axis=1, concat_axis=0, tiled=True)
    normed_time = rms_scale(series, time_gain)
    time_queries = linear(normed_time, time_pair[0]).astype(jnp.bfloat16)
    time_keys = linear(normed_time, time_pair[1]).astype(jnp.bfloat16)
    time_values = linear(normed_time, time_value).astype(jnp.bfloat16)
    time_context = time_attend(time_queries, time_keys, time_values, episode_start)
    after_time = (series.astype(jnp.float32) + linear(time_context, time_out)).astype(jnp.bfloat16)
    flat_rows = after_time.reshape(-1, after_time.shape[-1])
    inner_rows = rms_scale(flat_rows, inner_gain)
    expanded = jnp.dot(
        inner_rows,
        lax.all_gather(expand_weight, "dev", axis=0, tiled=True),
        preferred_element_type=jnp.float32,
    )
    hidden = jax.nn.gelu(expanded, approximate=True).astype(jnp.bfloat16)
    down_terms = jnp.dot(
        hidden,
        lax.all_gather(reduce_weight, "dev", axis=1, tiled=True),
        preferred_element_type=jnp.float32,
    )
    result = (
        (flat_rows.astype(jnp.float32) + down_terms).astype(jnp.bfloat16).reshape(after_time.shape)
    )
    return lax.all_to_all(result, "dev", split_axis=0, concat_axis=1, tiled=True)


def solution(mesh):
    return jax.shard_map(
        on_device,
        mesh=mesh,
        in_specs=(
            P("dev", "grp", None),
            P(),
            P(),
            P(),
            P(),
            P(),
            P(),
            P(),
            P(),
            P(),
            P("dev", None),
            P(None, "dev"),
            P(("grp", "dev")),
        ),
        out_specs=P("dev", "grp", None),
        check_vma=False,
    )
```

profile of v0, /device:TPU:32, one launch (start us, length us, event | category | flops | bytes accessed | tf_op | source)
XLA Modules:
  0.0 412.0 jit_solution(10141642499916735904)
XLA Ops:
  6.5 1.6 fusion.16
  8.2 3.3 convolution_convert_fusion.3
  11.5 1.6 convolution_convert_fusion.5
  14.5 2.8 convolution_convert_fusion.4
  17.2 1.6 reshape.223
  18.9 45.8 %all-gather.7.cloned.1.call-done = bf16[8,512,512]{2,1,0:T(8,128)(2,1)} async-done(((bf16[8,64,512]{2,1,0:T(8,128)(2,1)}), bf16[8,512,512]{2,1,0:T(8,128)(2,1)}) %all-gather.7.cloned.1.call-update) | async-done | bytes 4194320 | tf_op jit(solution)/shard_map/all_gather | solution.py:93
  64.7 6.5 %copy.92 = bf16[8,512,512]{1,2,0:T(8,128)(2,1)} copy(bf16[8,512,512]{2,1,0:T(8,128)(2,1)} %all-gather.7.cloned.1.call-done) | data formatting | bytes 8388608 | tf_op jit(solution)/shard_map/all_gather | solution.py:93
  71.2 48.7 %all-gather.5.cloned.1.call-done = bf16[8,512,512]{2,1,0:T(8,128)(2,1)} async-done(((bf16[8,64,512]{2,1,0:T(8,128)(2,1)}), bf16[8,512,512]{2,1,0:T(8,128)(2,1)}) %all-gather.5.cloned.1.call-update) | async-done | bytes 4194320 | tf_op jit(solution)/shard_map/all_gather | solution.py:94
  119.9 6.5 %copy.91 = bf16[8,512,512]{1,2,0:T(8,128)(2,1)} copy(bf16[8,512,512]{2,1,0:T(8,128)(2,1)} %all-gather.5.cloned.1.call-done) | data formatting | bytes 8388608 | tf_op jit(solution)/shard_map/all_gather | solution.py:94
  126.3 3.5 multiply_reduce_fusion
  129.9 2.1 fusion.1
  132.0 2.0 fusion.25
  134.1 0.7 fusion.19
  134.8 1.5 copy.95
  136.4 13.7 %all-to-all-start = ((bf16[8,64,1024]{2,0,1:T(8,128)(2,1)}), bf16[8,64,1024]{2,0,1:T(8,128)(2,1)S(1)}, u32[]{:S(2)}, u32[]{:S(2)}) async-start(bf16[8,64,1024]{2,0,1:T(8,128)(2,1)} %copy.95), calls=%async_computation | async-start | bytes 2097152 | tf_op jit(solution)/shard_map/all_to_all | solution.py:98
  150.4 40.7 %all-to-all-done = bf16[8,64,1024]{2,0,1:T(8,128)(2,1)S(1)} async-done(((bf16[8,64,1024]{2,0,1:T(8,128)(2,1)}), bf16[8,64,1024]{2,0,1:T(8,128)(2,1)S(1)}, u32[]{:S(2)}, u32[]{:S(2)}) %all-to-all-start) | async-done | bytes 1048608 | tf_op jit(solution)/shard_map/all_to_all | solution.py:98
  191.7 2.0 convolution_convert_fusion
  193.9 2.8 convolution_convert_fusion.1
  196.7 1.2 copy.103
  198.0 2.8 convolution_convert_fusion.2
  200.8 2.1 copy.100
  202.9 3.3 fusion.87
  206.2 2.2 fusion.46
  208.5 0.8 multiply_reduce_fusion.1
  209.3 1.6 copy.107
  210.9 2.4 reshape.230
  213.7 35.7 %all-gather.11.cloned.1.call-done = bf16[2048,1024]{0,1:T(8,128)(2,1)} async-done(((bf16[2048,32]{0,1:T(8,128)(2,1)}), bf16[2048,1024]{0,1:T(8,128)(2,1)}) %all-gather.11.cloned.1.call-update) | async-done | bytes 4194320 | tf_op jit(solution)/shard_map/all_gather | solution.py:115
  249.4 109.0 %all-gather.9.cloned.1.call-done = bf16[1024,2048]{1,0:T(8,128)(2,1)} async-done(((bf16[32,2048]{1,0:T(8,128)(2,1)}), bf16[1024,2048]{1,0:T(8,128)(2,1)}) %all-gather.9.cloned.1.call-update) | async-done | bytes 4194320 | tf_op jit(solution)/shard_map/all_gather | solution.py:109
  358.4 9.3 %add_convert_fusion = bf16[512,1024]{1,0:T(8,128)(2,1)S(1)} fusion(f32[512,1024]{1,0:T(8,128)} %reshape.230, bf16[2048,1024]{0,1:T(8,128)(2,1)} %all-gather.11.cloned.1.call-done, bf16[1024,2048]{1,0:T(8,128)(2,1)} %all-gather.9.cloned.1.call-done, f32[1024]{0:T(1024)S(1)} %copy-done.8, f32[512]{0:T(512)S(1)} %rsqrt.35), kind=kOutput, calls=%fused_computation.36 | convolution fusion | flops 4307025920 | bytes 11540480 | tf_op jit(solution)/shard_map/dot_general | solution.py:113
  368.2 35.4 %all_to_all.27 = bf16[256,2,1024]{2,1,0:T(2,128)(2,1)S(1)} all-to-all(bf16[256,2,1024]{2,1,0:T(2,128)(2,1)S(1)} %reshape.228), channel_id=1, replica_groups=mesh['grp'=8,'dev'=32] {'dev'}, dimensions={0} | all-to-all | bytes 2097152 | tf_op jit(solution)/shard_map/all_to_all | solution.py:121
  403.6 0.7 copy.133
  404.3 1.2 all_to_all.24
  (41 shorter events, 3.3 us)
Async XLA Ops:
  6.5 201.9 %copy-start = (bf16[512,1024]{1,0:T(8,128)(2,1)S(1)}, bf16[512,1024]{1,0:T(8,128)(2,1)}, u32[]{:S(2)}) copy-start(bf16[512,1024]{1,0:T(8,128)(2,1)} %param.22) | copy-start | bytes 3145732
  6.5 58.2 %all-gather.7.cloned.1.call-start = ((), (), s32[]{:S(2)}) async-start(), calls=%async_computation.3 | async-start | bytes 4718592 | tf_op jit(solution)/shard_map/all_gather | solution.py:93
  8.1 3.4 copy-start.2
  8.2 3.4 copy-start.5
  8.2 3.4 copy-start.6
  11.5 108.4 %all-gather.5.cloned.1.call-start = ((), (), s32[]{:S(2)}) async-start(), calls=%async_computation.2 | async-start | bytes 4718592 | tf_op jit(solution)/shard_map/all_gather | solution.py:94
  13.1 236.2 %all-gather.11.cloned.1.call-start = ((), (), s32[]{:S(2)}) async-start(), calls=%async_computation.5 | async-start | bytes 4325376 | tf_op jit(solution)/shard_map/all_gather | solution.py:115
  13.9 344.6 %all-gather.9.cloned.1.call-start = ((), (), s32[]{:S(2)}) async-start(), calls=%async_computation.4 | async-start | bytes 4325376 | tf_op jit(solution)/shard_map/all_gather | solution.py:109
  129.8 2.2 copy-start.1
  132.0 2.0 copy-start.3
  134.8 15.3 %copy-start.4 = (s32[2]{0:T(128)S(1)}, s32[2]{0:T(128)}, u32[]{:S(2)}) copy-start(s32[2]{0:T(128)} %param.25) | copy-start | bytes 28
  136.4 55.3 %copy-start.7 = (f32[1024]{0:T(1024)S(1)}, f32[1024]{0:T(1024)}, u32[]{:S(2)}) copy-start(f32[1024]{0:T(1024)} %param.15) | copy-start | bytes 12292
  136.4 54.8 %all-to-all-start = ((bf16[8,64,1024]{2,0,1:T(8,128)(2,1)}), bf16[8,64,1024]{2,0,1:T(8,128)(2,1)S(1)}, u32[]{:S(2)}, u32[]{:S(2)}) async-start(bf16[8,64,1024]{2,0,1:T(8,128)(2,1)} %copy.95), calls=%async_computation | async-start | bytes 2097152 | tf_op jit(solution)/shard_map/all_to_all | solution.py:98
  210.9 147.5 %copy-start.8 = (f32[1024]{0:T(1024)S(1)}, f32[1024]{0:T(1024)}, u32[]{:S(2)}) copy-start(f32[1024]{0:T(1024)} %param.16) | copy-start | bytes 12292
Sparse Core Ops, SparseCore 0:
  11.6 53.0 all-gather.6
  66.5 53.2 all-gather.4
  123.3 126.0 all-gather.10
  252.7 105.7 all-gather.8
where the time goes:
time: 413 us; the launch traced here: 412 us
  waiting for transfers between devices  281 us (68%)
  matrix products  37.1 us (9%)
  blocking collectives  35.4 us (9%)
  local copies, waits for them, and re-layouts  26.9 us (7%)
  starting transfers between devices  13.8 us (3%)
  between operations  13.4 us (3%)
  other arithmetic  4.25 us (1%)
    all_gather x1, waiting for transfers between devices, on_device(): lax.all_gather(expand_weight, 'dev', axis=0, tiled=True)  109 us
    all_gather x1, waiting for transfers between devices, on_device(): lax.all_gather(values, 'grp', axis=1, tiled=True)  48.7 us
    all_gather x1, waiting for transfers between devices, on_device(): lax.all_gather(key_rows, 'grp', axis=1, tiled=True)  45.8 us
    all_to_all x1, waiting for transfers between devices, on_device(): lax.all_to_all(after_agents, 'dev', split_axis=1, concat_axis=0, tiled=True)  40.7 us
    all_gather x1, waiting for transfers between devices, on_device(): lax.all_gather(reduce_weight, 'dev', axis=1, tiled=True)  35.7 us
    all_to_all x1, blocking collectives, on_device(): lax.all_to_all(result, 'dev', split_axis=0, concat_axis=1, tiled=True)  35.4 us
    dot_general x8, matrix products, linear(): product = jnp.dot(flat_rows, weight, preferred_element_type=jnp.float32)  16.7 us
    all_to_all x1, starting transfers between devices, on_device(): lax.all_to_all(after_agents, 'dev', split_axis=1, concat_axis=0, tiled=True)  13.7 us
  transfers between devices with their start and end apart: 5, of which 5 were waited for; matrix products, arithmetic and copies ran while one was open for 13% of the time, Pallas kernels for 0%

commit v1 on v0

v1 whole, which is shorter than its diff:
```python
import jax
import jax.numpy as jnp
from jax import lax
from jax.sharding import Mesh, PartitionSpec as P

HDIM = 64
GRP = ("zl", "c")
DEV = ("x", "y", "h")
BF = jnp.bfloat16
F32 = jnp.float32


def rms_scale(row_block, gain_vec):
    widened = row_block.astype(F32)
    inverse = lax.rsqrt(jnp.mean(widened * widened, axis=-1, keepdims=True) + 1e-05)
    return (widened * inverse * gain_vec).astype(BF)


def linear(rows, weight):
    return jnp.dot(rows, weight, preferred_element_type=F32)


def agent_attend(queries, key_rows, values):
    count, width = queries.shape
    heads = width // HDIM
    q = queries.reshape(count, heads, HDIM)
    k = key_rows.reshape(count, heads, HDIM)
    v = values.reshape(count, heads, HDIM)
    scores = jnp.einsum("ihd,jhd->hij", q, k, preferred_element_type=F32) * HDIM ** (-0.5)
    exponent = jnp.exp(scores - jnp.max(scores, axis=-1, keepdims=True))
    total = jnp.sum(exponent, axis=-1)
    weighted = jnp.einsum("hij,jhd->ihd", exponent.astype(BF), v, preferred_element_type=F32)
    context = weighted / jnp.transpose(total)[..., None]
    return context.reshape(count, width).astype(BF)


def time_attend(queries, key_rows, values, offsets, places):
    agents, steps, width = queries.shape
    heads = width // HDIM
    q = queries.reshape(agents, steps, heads, HDIM)
    k = key_rows.reshape(agents, steps, heads, HDIM)
    v = values.reshape(agents, steps, heads, HDIM)
    scores = jnp.einsum("aihd,ajhd->ahij", q, k, preferred_element_type=F32) * HDIM ** (-0.5)
    causal = places[:, None] >= places[None, :]
    begins = offsets[:, None, None]
    visible = causal[None] & ((places[None, None, :] >= begins) | (places[None, :, None] < begins))
    visible = visible[:, None]
    masked = jnp.where(visible, scores, -1e30)
    exponent = jnp.where(visible, jnp.exp(masked - jnp.max(masked, axis=-1, keepdims=True)), 0.0)
    total = jnp.sum(exponent, axis=-1)
    weighted = jnp.einsum("ahij,ajhd->aihd", exponent.astype(BF), v, preferred_element_type=F32)
    context = weighted / jnp.transpose(total, (0, 2, 1))[..., None]
    return context.reshape(agents, steps, width).astype(BF)


def on_device(
    rollout,
    agent_gain,
    time_gain,
    inner_gain,
    agent_pair,
    agent_value,
    agent_out,
    time_pair,
    time_value,
    time_out,
    expand_weight,
    reduce_weight,
    episode_start,
):
    steps_here, agents_here, width = rollout.shape
    n_grp = lax.axis_size(GRP)
    n_dev = lax.axis_size(DEV)
    agents_own = episode_start.shape[0]

    core, high = lax.axis_index("c"), lax.axis_index("h")
    half = expand_weight.shape[1] // 2
    up = lax.dynamic_slice_in_dim(expand_weight, core * half, half, 1)
    down = lax.dynamic_slice_in_dim(reduce_weight.T, core * half, half, 1)
    mine = jnp.stack([up, down])
    other = lax.ppermute(mine, "h", [(0, 1), (1, 0)])
    pair = jnp.where(
        high == 0, jnp.concatenate([mine, other], 1), jnp.concatenate([other, mine], 1)
    )
    near = lax.all_gather(pair, ("x", "y"), axis=1, tiled=True)
    far = lax.ppermute(near, "c", [(0, 1), (1, 0)])

    rows = lax.all_to_all(rollout, GRP, split_axis=0, concat_axis=0, tiled=True)
    rows = rows.reshape(n_grp * agents_here, width)
    normed = rms_scale(rows, agent_gain)
    queries = linear(normed, agent_pair[0]).astype(BF)
    key_rows = linear(normed, agent_pair[1]).astype(BF)
    values = linear(normed, agent_value).astype(BF)
    context = agent_attend(queries, key_rows, values)
    after_agents = (rows.astype(F32) + linear(context, agent_out)).astype(BF)

    pieces = after_agents.reshape(n_grp * n_dev, agents_own, width)
    series = lax.all_to_all(pieces, GRP + DEV, split_axis=0, concat_axis=0, tiled=True)
    series = jnp.swapaxes(series, 0, 1)
    steps = n_grp * n_dev
    index = lax.iota(jnp.int32, steps)
    places = (index % n_dev) * n_grp + index // n_dev
    series = series.reshape(agents_own * steps, width)
    normed_time = rms_scale(series, time_gain)
    shape = (agents_own, steps, -1)
    time_queries = linear(normed_time, time_pair[0]).astype(BF).reshape(shape)
    time_keys = linear(normed_time, time_pair[1]).astype(BF).reshape(shape)
    time_values = linear(normed_time, time_value).astype(BF).reshape(shape)
    time_context = time_attend(time_queries, time_keys, time_values, episode_start, places)
    time_context = time_context.reshape(agents_own * steps, -1)
    after_time = (series.astype(F32) + linear(time_context, time_out)).astype(BF)

    inner = rms_scale(after_time, inner_gain)
    total = after_time.astype(F32)
    for part in (near, far):
        hidden = jax.nn.gelu(linear(inner, part[0]), approximate=True).astype(BF)
        total = total + lax.dot_general(
            hidden, part[1], (((1,), (1,)), ((), ())), preferred_element_type=F32
        )
    result = total.astype(BF).reshape(agents_own, n_grp, n_dev, width)
    result = jnp.transpose(result, (1, 2, 0, 3))
    result = lax.all_to_all(result, DEV, split_axis=1, concat_axis=1, tiled=True)
    return result.reshape(steps_here, agents_here, width)


def solution(mesh):
    fine = Mesh(mesh.devices.reshape(4, 2, 4, 4, 2), ("zl", "c", "x", "y", "h"))
    return jax.shard_map(
        on_device,
        mesh=fine,
        in_specs=(
            P(DEV, GRP, None),
            P(),
            P(),
            P(),
            P(),
            P(),
            P(),
            P(),
            P(),
            P(),
            P(DEV, None),
            P(None, DEV),
            P(GRP + DEV),
        ),
        out_specs=P(DEV, GRP, None),
        check_vma=False,
    )
```

time: 413 us -> 186 us (0.45)
  waiting for transfers between devices: 281 us -> 36.7 us
  blocking collectives: 35.4 us -> 66.4 us
  local copies, waits for them, and re-layouts: 26.9 us -> 14.8 us
  matrix products: 37.1 us -> 27.1 us
  starting transfers between devices: 13.8 us -> 21.1 us
    all_gather x4 -> x1, waiting for transfers between devices: 239 us -> 5.92 us  [on_device(): near = lax.all_gather(pair, ('x', 'y'), axis=1, tiled=True)]
    all_to_all x1 -> x2, blocking collectives: 35.4 us -> 66.4 us  [the longest x1 38.1 us: on_device(): lax.all_to_all(result, DEV, split_axis=1, concat_axis=1, tiled=True)]
    all_to_all x1, waiting for transfers between devices: 40.7 us -> 24.4 us  [on_device(): lax.all_to_all(pieces, GRP + DEV, split_axis=0, concat_axis=0, tiled=True)]
    all_gather x2 -> x0, local copies, waits for them, and re-layouts: 12.9 us -> none  [the longest x1 6.49 us: on_device(): lax.all_gather(values, 'grp', axis=1, tiled=True)]
    convert_element_type x6 -> x1, local copies, waits for them, and re-layouts: 9.13 us -> 0.54 us  [time_attend(): return context.reshape(agents, steps, width).astype(BF)]
    another operation x0 -> x5, local copies, waits for them, and re-layouts: none -> 7.38 us  [the longest x1 2.36 us: time_attend(): k = key_rows.reshape(agents, steps, heads, HDIM)]
    dot_general x12 -> x14, matrix products: 33.8 us -> 27.1 us  [the longest x2 11.4 us: on_device(): lax.dot_general(hidden, part[1], (((1,), (1,)), ((), ())), preferred_elem...]
    ppermute x0 -> x2, starting transfers between devices: none -> 6.38 us  [the longest x1 6.38 us: on_device(): other = lax.ppermute(mine, 'h', [(0, 1), (1, 0)])]
  transfers between devices with their start and end apart: 5 -> 4, of which waited for: 5 -> 3; matrix products, arithmetic and copies ran while one was open for 13% -> 19% of each run, Pallas kernels for 0% -> 0%
where the time goes in v1:
time: 186 us
  blocking collectives  66.4 us (36%)
  waiting for transfers between devices  36.7 us (20%)
  matrix products  27.1 us (15%)
  starting transfers between devices  21.1 us (11%)
  local copies, waits for them, and re-layouts  14.8 us (8%)
  between operations  13.7 us (7%)
  other arithmetic  5.99 us (3%)
    all_to_all x1, blocking collectives, on_device(): lax.all_to_all(result, DEV, split_axis=1, concat_axis=1, tiled=True)  38.1 us
    all_to_all x1, blocking collectives, on_device(): rows = lax.all_to_all(rollout, GRP, split_axis=0, concat_axis=0, tiled=True)  28.4 us
    all_to_all x1, waiting for transfers between devices, on_device(): lax.all_to_all(pieces, GRP + DEV, split_axis=0, concat_axis=0, tiled=True)  24.4 us
    all_to_all x1, starting transfers between devices, on_device(): lax.all_to_all(pieces, GRP + DEV, split_axis=0, concat_axis=0, tiled=True)  14.7 us
    dot_general x2, matrix products, on_device(): lax.dot_general(hidden, part[1], (((1,), (1,)), ((), ())), preferred_elem...  11.4 us
    dot_general x8, matrix products, linear(): return jnp.dot(rows, weight, preferred_element_type=F32)  10.4 us
    ppermute x1, starting transfers between devices, on_device(): other = lax.ppermute(mine, 'h', [(0, 1), (1, 0)])  6.38 us
    ppermute x1, waiting for transfers between devices, on_device(): other = lax.ppermute(mine, 'h', [(0, 1), (1, 0)])  6.35 us
  transfers between devices with their start and end apart: 4, of which 3 were waited for; matrix products, arithmetic and copies ran while one was open for 19% of the time, Pallas kernels for 0%

profile of v1, /device:TPU:32, one launch (start us, length us, event | category | flops | bytes accessed | tf_op | source)
XLA Modules:
  0.0 185.8 jit_solution(14916260190559392782)
XLA Ops:
  6.5 0.9 dynamic-slice_bitcast_fusion
  7.5 0.8 dynamic-slice_bitcast_fusion.1
  8.3 6.4 %collective-permute-start = (bf16[2,32,1024]{2,1,0:T(8,128)(2,1)S(1)}, bf16[2,32,1024]{2,1,0:T(8,128)(2,1)S(1)}, u32[]{:S(2)}, u32[]{:S(2)}) collective-permute-start(bf16[2,32,1024]{2,1,0:T(8,128)(2,1)S(1)} %pad_maximum_fusion), channel_id=1, source_target_pairs={{0,1},{1,0},{2,3},{3,2},{4,5},{5,4},{6,7},{7,6},{8,9},{9,8},{10,11... | collective-permute-start | bytes 393224 | tf_op jit(solution)/shard_map/ppermute | solution.py:81
  14.7 6.4 %collective-permute-done = bf16[2,32,1024]{2,1,0:T(8,128)(2,1)S(1)} collective-permute-done((bf16[2,32,1024]{2,1,0:T(8,128)(2,1)S(1)}, bf16[2,32,1024]{2,1,0:T(8,128)(2,1)S(1)}, u32[]{:S(2)}, u32[]{:S(2)}) %collective-permute-start) | collective-permute-done | bytes 131104 | tf_op jit(solution)/shard_map/ppermute | solution.py:81
  21.1 0.7 maximum_select_fusion
  21.8 28.4 %all_to_all.15 = bf16[8,64,1024]{2,1,0:T(8,128)(2,1)S(1)} all-to-all(bf16[8,64,1024]{2,1,0:T(8,128)(2,1)} %param.13), channel_id=1, replica_groups=mesh['zl'=4,'c'=2,'x'=4,'y'=4,'h'=2] {'zl','c'}, dimensions={0} | all-to-all | bytes 2097152 | tf_op jit(solution)/shard_map/all_to_all | solution.py:88
  51.2 1.0 copy-done.6
  52.2 0.8 convolution_convert_fusion.4
  52.9 0.8 convolution_convert_fusion.3
  54.1 0.8 convolution_convert_fusion.5
  54.9 1.3 multiply_reduce_fusion
  56.2 1.4 fusion.1
  57.6 1.6 divide_convert_fusion
  59.2 0.7 fusion.46
  60.0 1.2 reshape.300
  61.2 14.7 %all-to-all-start.1 = ((bf16[256,2,1024]{2,1,0:T(2,128)(2,1)}), bf16[256,2,1024]{2,1,0:T(2,128)(2,1)S(1)}, u32[]{:S(2)}, u32[]{:S(2)}) async-start(bf16[256,2,1024]{2,1,0:T(2,128)(2,1)} %reshape.300), calls=%async_computation.1 | async-start | bytes 2097152 | tf_op jit(solution)/shard_map/all_to_all | solution.py:98
  76.3 5.9 %all-gather.2.cloned.1.call-done = bf16[2,1024,1024]{2,1,0:T(8,128)(2,1)} async-done(((bf16[2,64,1024]{2,1,0:T(8,128)(2,1)}), bf16[2,1024,1024]{2,1,0:T(8,128)(2,1)}) %all-gather.2.cloned.1.call-update) | async-done | bytes 4194320 | tf_op jit(solution)/shard_map/all_gather | solution.py:85
  82.2 24.4 %all-to-all-done.1 = bf16[256,2,1024]{2,1,0:T(2,128)(2,1)S(1)} async-done(((bf16[256,2,1024]{2,1,0:T(2,128)(2,1)}), bf16[256,2,1024]{2,1,0:T(2,128)(2,1)S(1)}, u32[]{:S(2)}, u32[]{:S(2)}) %all-to-all-start.1) | async-done | bytes 1048608 | tf_op jit(solution)/shard_map/all_to_all | solution.py:98
  107.4 1.9 %convolution_convert_fusion.2 = bf16[512,512]{1,0:T(8,128)(2,1)S(1)} fusion(bf16[512,1024]{1,0:T(8,128)(2,1)S(1)} %fusion.39, bf16[1024,512]{1,0:T(8,128)(2,1)} %param.21), kind=kOutput, calls=%fused_computation.77 | convolution fusion | flops 537133056 | bytes 2621440 | tf_op jit(solution)/shard_map/dot_general | solution.py:20
  109.4 1.6 reshape.305
  111.3 1.0 copy-done.1
  112.9 1.5 convolution_convert_fusion.1
  114.4 1.6 reshape.306
  116.1 3.0 %convolution_convert_fusion = bf16[512,512]{1,0:T(8,128)(2,1)} fusion(bf16[512,1024]{1,0:T(8,128)(2,1)} %bitcast.122, bf16[2,1024,512]{2,1,0:T(8,128)(2,1)} %param.20), kind=kOutput, calls=%fused_computation.75 | convolution fusion | flops 537133056 | bytes 2621440 | tf_op jit(solution)/shard_map/dot_general | solution.py:20
  119.1 2.4 %reshape.307 = bf16[2,256,8,64]{3,2,1,0:T(8,128)(2,1)} reshape(bf16[512,512]{1,0:T(8,128)(2,1)} %convolution_convert_fusion) | data formatting | bytes 1048576 | tf_op jit(solution)/shard_map/reshape;reshape | solution.py:41
  121.5 1.9 %fusion.64 = f32[2,8,256,256]{2,3,1,0:T(8,128)S(1)} fusion(bf16[2,256,8,64]{3,2,1,0:T(8,128)(2,1)} %reshape.307, bf16[2,256,8,64]{3,2,1,0:T(8,128)(2,1)S(1)} %reshape.306), kind=kOutput, calls=%fused_computation.81 | convolution fusion | flops 134217728 | bytes 5242880 | tf_op jit(solution)/shard_map/aihd,ajhd->ahij/dot_general | solution.py:43
  123.4 1.5 fusion.110
  126.4 0.9 fusion.8
  127.3 6.0 %fusion.31 = f32[512,1024]{1,0:T(8,128)} fusion(bf16[2,1024,1024]{2,1,0:T(8,128)(2,1)} %all-gather.2.cloned.1.call-done, bf16[512,1024]{1,0:T(8,128)(2,1)S(1)} %get-tuple-element.14, f32[1024]{0:T(1024)S(1)} %copy-done.10, f32[512]{0:T(512)S(1)} %add_rsqrt_fusion.1), kind=kOutput, calls=%fused_computation.42 | convolution fusion | flops 2154299392 | bytes 7346176 | tf_op jit(solution)/shard_map/dot_general | solution.py:117
  133.4 5.4 %fusion.12 = bf16[512,1024]{1,0:T(8,128)(2,1)S(1)} fusion(f32[512,1024]{1,0:T(8,128)} %fusion.31, bf16[512,1024]{1,0:T(8,128)(2,1)S(1)} %get-tuple-element.14, bf16[2,1024,1024]{2,1,0:T(8,128)(2,1)} %collective-permute-done.1, f32[1024]{0:T(1024)S(1)} %copy-done.10, f32[512]{0:T(512)S(1)} %add_rsqrt_fusion.1), kind=kOutput, calls=%fused_computation.20 | convolution fusion | flops 2156396544 | bytes 9443328 | tf_op jit(solution)/shard_map/dot_general | solution.py:117
  139.3 38.1 %all_to_all.16 = bf16[8,32,2,1024]{3,0,2,1:T(8,128)(2,1)S(1)} all-to-all(bf16[8,32,2,1024]{3,0,2,1:T(8,128)(2,1)S(1)} %bitcast.118), channel_id=1, replica_groups=mesh['zl'=4,'c'=2,'x'=4,'y'=4,'h'=2] {'x','y','h'}, dimensions={1} | all-to-all | bytes 2097152 | tf_op jit(solution)/shard_map/all_to_all | solution.py:122
  177.4 1.5 copy.43
  (45 shorter events, 5.6 us)
Async XLA Ops:
  6.5 119.9 %copy-start = (bf16[512,1024]{1,0:T(8,128)(2,1)S(1)}, bf16[512,1024]{1,0:T(8,128)(2,1)}, u32[]{:S(2)}) copy-start(bf16[512,1024]{1,0:T(8,128)(2,1)} %param.22) | copy-start | bytes 3145732
  6.5 75.7 %all-gather.2.cloned.1.call-start = ((), (), s32[]{:S(2)}) async-start(), calls=%async_computation.3 | async-start | bytes 4456448 | tf_op jit(solution)/shard_map/all_gather | solution.py:85
  8.3 42.2 %copy-start.3 = (f32[1024]{0:T(1024)S(1)}, f32[1024]{0:T(1024)}, u32[]{:S(2)}) copy-start(f32[1024]{0:T(1024)} %param.14) | copy-start | bytes 12292
  8.3 12.7 %collective-permute-start = (bf16[2,32,1024]{2,1,0:T(8,128)(2,1)S(1)}, bf16[2,32,1024]{2,1,0:T(8,128)(2,1)S(1)}, u32[]{:S(2)}, u32[]{:S(2)}) collective-permute-start(bf16[2,32,1024]{2,1,0:T(8,128)(2,1)S(1)} %pad_maximum_fusion), channel_id=1, source_target_pairs={{0,1},{1,0},{2,3},{3,2},{4,5},{5,4},{6,7},{7,6},{8,9},{9,8},{10,11... | collective-permute-start | bytes 393224 | tf_op jit(solution)/shard_map/ppermute | solution.py:81
  50.6 1.6 copy-start.6
  52.9 1.2 copy-start.8
  57.6 1.6 copy-start.9
  60.0 16.0 %copy-start.5 = (s32[2]{0:T(128)S(1)}, s32[2]{0:T(128)}, u32[]{:S(2)}) copy-start(s32[2]{0:T(128)} %param.25) | copy-start | bytes 28
  61.2 45.8 %copy-start.4 = (f32[1024]{0:T(1024)S(1)}, f32[1024]{0:T(1024)}, u32[]{:S(2)}) copy-start(f32[1024]{0:T(1024)} %param.15) | copy-start | bytes 12292
  61.2 45.5 %all-to-all-start.1 = ((bf16[256,2,1024]{2,1,0:T(2,128)(2,1)}), bf16[256,2,1024]{2,1,0:T(2,128)(2,1)S(1)}, u32[]{:S(2)}, u32[]{:S(2)}) async-start(bf16[256,2,1024]{2,1,0:T(2,128)(2,1)} %reshape.300), calls=%async_computation.1 | async-start | bytes 2097152 | tf_op jit(solution)/shard_map/all_to_all | solution.py:98
  82.2 51.2 %collective-permute-start.1 = (bf16[2,1024,1024]{2,1,0:T(8,128)(2,1)}, bf16[2,1024,1024]{2,1,0:T(8,128)(2,1)}, u32[]{:S(2)}, u32[]{:S(2)}) collective-permute-start(bf16[2,1024,1024]{2,1,0:T(8,128)(2,1)} %all-gather.2.cloned.1.call-done), channel_id=1, source_target_pairs={{0,32},{32,0},{1,33},{33,1},{2,34},{34,2},{3,35},{35,3},{4,36},{36... | collective-permute-start | bytes 12582920 | tf_op jit(solution)/shard_map/ppermute | solution.py:86
  111.0 2.0 %copy-start.7 = (bf16[2,1024,512]{2,1,0:T(8,128)(2,1)S(1)}, bf16[2,1024,512]{2,1,0:T(8,128)(2,1)}, u32[]{:S(2)}) copy-start(bf16[2,1024,512]{2,1,0:T(8,128)(2,1)} %param.20) | copy-start | bytes 6291460
  111.3 1.0 copy-start.1
  123.4 1.6 copy-start.2
  126.4 0.9 copy-start.10
Sparse Core Ops, SparseCore 0:
  22.0 60.1 all-gather.1

commit v2 on v1

v2 whole, which is shorter than its diff:
```python
import jax
import jax.numpy as jnp
from jax import lax
from jax.sharding import Mesh, PartitionSpec as P

HDIM = 64
GRP = ("zl", "c")
DEV = ("x", "y", "h")
BF = jnp.bfloat16
F32 = jnp.float32


def rms_scale(row_block, gain_vec):
    widened = row_block.astype(F32)
    inverse = lax.rsqrt(jnp.mean(widened * widened, axis=-1, keepdims=True) + 1e-05)
    return (widened * inverse * gain_vec).astype(BF)


def linear(rows, weight):
    return jnp.dot(rows, weight, preferred_element_type=F32)


def split_heads(rows):
    return rows.reshape(rows.shape[0], -1, HDIM)


def attend(queries, keys, values, visible=None):
    scores = jnp.einsum("ihd,jhd->hij", queries, keys, preferred_element_type=F32)
    scores = scores * HDIM ** (-0.5)
    if visible is not None:
        scores = jnp.where(visible, scores, -jnp.inf)
    exponent = jnp.exp(scores - jnp.max(scores, axis=-1, keepdims=True))
    total = jnp.sum(exponent, axis=-1)
    weighted = jnp.einsum("hij,jhd->ihd", exponent.astype(BF), values, preferred_element_type=F32)
    context = weighted / jnp.transpose(total)[..., None]
    return context.reshape(queries.shape[0], -1).astype(BF)


def swap_core(block):
    return lax.ppermute(block, "c", [(0, 1), (1, 0)])


def swap_z(block, k):
    n = lax.axis_size("zl")
    return lax.ppermute(block, "zl", [(i, i ^ k) for i in range(n)])


def by_xor(block, index):
    count = block.shape[0]
    bits = count.bit_length() - 1
    for bit in range(bits):
        parts = block.reshape((count >> (bit + 1), 2, 1 << bit) + block.shape[1:])
        flip = (index >> bit) & 1 == 1
        low, high = parts[:, :1], parts[:, 1:]
        parts = jnp.concatenate([jnp.where(flip, high, low), jnp.where(flip, low, high)], 1)
        block = parts.reshape(block.shape)
    return block


def on_device(
    rollout,
    agent_gain,
    time_gain,
    inner_gain,
    agent_pair,
    agent_value,
    agent_out,
    time_pair,
    time_value,
    time_out,
    expand_weight,
    reduce_weight,
    episode_start,
):
    steps_here, agents_here, width = rollout.shape
    zl, core, high = lax.axis_index("zl"), lax.axis_index("c"), lax.axis_index("h")
    n_zl, n_core = lax.axis_size("zl"), lax.axis_size("c")

    half = expand_weight.shape[1] // 2
    up = lax.dynamic_slice_in_dim(expand_weight, core * half, half, 1)
    down = lax.dynamic_slice_in_dim(reduce_weight.T, core * half, half, 1)
    mine = jnp.stack([up, down])
    other = lax.ppermute(mine, "h", [(0, 1), (1, 0)])

    by_step = rollout.reshape(n_zl, n_core, agents_here, width)
    keep = lax.dynamic_index_in_dim(by_step, core, 1, keepdims=False)
    give = lax.dynamic_index_in_dim(by_step, 1 - core, 1, keepdims=False)
    both = jnp.stack([keep, swap_core(give)], 1).reshape(n_zl, n_core * agents_here, width)
    chunks = [lax.dynamic_index_in_dim(both, zl ^ k, 0, keepdims=False) for k in range(n_zl)]
    chunks = [chunks[0]] + [swap_z(chunks[k], k) for k in range(1, n_zl)]
    rows = jnp.concatenate(chunks, 0)

    pair = jnp.where(
        high == 0, jnp.concatenate([mine, other], 1), jnp.concatenate([other, mine], 1)
    )
    near = lax.all_gather(pair, ("x", "y"), axis=1, tiled=True)
    far = swap_core(near)

    normed = rms_scale(rows, agent_gain)
    queries = linear(normed, agent_pair[0]).astype(BF)
    keys = split_heads(linear(normed, agent_pair[1]).astype(BF))
    values = split_heads(linear(normed, agent_value).astype(BF))
    size = n_core * agents_here
    back = [None] * n_zl
    for k in reversed(range(n_zl)):
        part = attend(split_heads(queries[k * size : (k + 1) * size]), keys, values)
        back[k] = swap_z(part, k) if k else part
    back = jnp.stack(back).reshape(n_zl, n_core, agents_here, -1)
    own, others = back[:, 0], swap_core(back[:, 1])
    context = jnp.stack([own, others], 1).reshape(steps_here, agents_here, -1)
    context = jnp.swapaxes(by_xor(context, zl * n_core + core), 0, 1)
    residual = jnp.swapaxes(rollout, 0, 1).reshape(-1, width).astype(F32)
    context = context.reshape(agents_here * steps_here, -1)
    after_agents = (residual + linear(context, agent_out)).astype(BF)

    n_dev = lax.axis_size(DEV)
    agents_own = episode_start.shape[0]
    steps = n_dev * steps_here
    pieces = after_agents.reshape(n_dev, agents_own, steps_here, width)
    series = lax.all_to_all(pieces, DEV, split_axis=0, concat_axis=0, tiled=True)
    places = lax.iota(jnp.int32, steps)
    causal = places[:, None] >= places[None, :]
    results = []
    for agent in range(agents_own):
        row_block = series[:, agent].reshape(steps, width)
        begin = episode_start[agent]
        visible = causal & ((places[None, :] >= begin) | (places[:, None] < begin))
        normed_time = rms_scale(row_block, time_gain)
        q = split_heads(linear(normed_time, time_pair[0]).astype(BF))
        k = split_heads(linear(normed_time, time_pair[1]).astype(BF))
        v = split_heads(linear(normed_time, time_value).astype(BF))
        time_context = attend(q, k, v, visible[None])
        results.append((row_block.astype(F32) + linear(time_context, time_out)).astype(BF))
    after_time = jnp.concatenate(results, 0)

    inner = rms_scale(after_time, inner_gain)
    total = after_time.astype(F32)
    for part in (near, far):
        hidden = jax.nn.gelu(linear(inner, part[0]), approximate=True).astype(BF)
        total = total + lax.dot_general(
            hidden, part[1], (((1,), (1,)), ((), ())), preferred_element_type=F32
        )
    result = total.astype(BF).reshape(agents_own, n_dev, steps_here, width)
    result = lax.all_to_all(
        jnp.swapaxes(result, 0, 1), DEV, split_axis=0, concat_axis=0, tiled=True
    )
    return jnp.swapaxes(result.reshape(agents_here, steps_here, width), 0, 1)


def solution(mesh):
    fine = Mesh(mesh.devices.reshape(4, 2, 4, 4, 2), ("zl", "c", "x", "y", "h"))
    return jax.shard_map(
        on_device,
        mesh=fine,
        in_specs=(
            P(DEV, GRP, None),
            P(),
            P(),
            P(),
            P(),
            P(),
            P(),
            P(),
            P(),
            P(),
            P(DEV, None),
            P(None, DEV),
            P(GRP + DEV),
        ),
        out_specs=P(DEV, GRP, None),
        check_vma=False,
    )
```

time: 186 us -> 189 us (1.016)
  blocking collectives: 66.4 us -> 33.7 us
  waiting for transfers between devices: 36.7 us -> 61 us
  matrix products: 27.1 us -> 37 us
  local copies, waits for them, and re-layouts: 14.8 us -> 8.09 us
  starting transfers between devices: 21.1 us -> 27.6 us
    all_to_all x2 -> x1, blocking collectives: 66.4 us -> 33.7 us  [on_device(): lax.all_to_all(jnp.swapaxes(result, 0, 1), DEV, split_axis=0, concat_axis...]
    ppermute x1 -> x9, waiting for transfers between devices: 0.01 us -> 15.3 us  [the longest x6 12.3 us: swap_z(): return lax.ppermute(block, 'zl', [(i, i ^ k) for i in range(n)])]
    ppermute x1 -> x9, starting transfers between devices: 0.01 us -> 10.4 us  [the longest x6 9.88 us: swap_z(): return lax.ppermute(block, 'zl', [(i, i ^ k) for i in range(n)])]
    dot_general x8 -> x12, matrix products: 10.4 us -> 18.5 us  [linear(): return jnp.dot(rows, weight, preferred_element_type=F32)]
    ppermute x1, waiting for transfers between devices: 6.35 us -> 14.2 us  [on_device(): other = lax.ppermute(mine, 'h', [(0, 1), (1, 0)])]
    all_to_all x1, waiting for transfers between devices: 24.4 us -> 31.5 us  [on_device(): lax.all_to_all(pieces, DEV, split_axis=0, concat_axis=0, tiled=True)]
    all_gather x1, waiting for transfers between devices: 5.92 us -> 0.02 us  [on_device(): near = lax.all_gather(pair, ('x', 'y'), axis=1, tiled=True)]
    another operation x3 -> x0, local copies, waits for them, and re-layouts: 5.6 us -> none  [the longest x1 2.36 us: time_attend(): k = key_rows.reshape(agents, steps, heads, HDIM)]
  transfers between devices with their start and end apart: 4 -> 12, of which waited for: 3 -> 7; matrix products, arithmetic and copies ran while one was open for 19% -> 23% of each run, Pallas kernels for 0% -> 0%
where the time goes in v2:
time: 189 us; the launch traced here: 188 us
  waiting for transfers between devices  61 us (32%)
  matrix products  37 us (20%)
  blocking collectives  33.7 us (18%)
  starting transfers between devices  27.6 us (15%)
  between operations  14 us (7%)
  local copies, waits for them, and re-layouts  8.09 us (4%)
  other arithmetic  7.02 us (4%)
    all_to_all x1, blocking collectives, on_device(): lax.all_to_all(jnp.swapaxes(result, 0, 1), DEV, split_axis=0, concat_axis...  33.7 us
    all_to_all x1, waiting for transfers between devices, on_device(): lax.all_to_all(pieces, DEV, split_axis=0, concat_axis=0, tiled=True)  31.5 us
    dot_general x12, matrix products, linear(): return jnp.dot(rows, weight, preferred_element_type=F32)  18.5 us
    ppermute x1, waiting for transfers between devices, on_device(): other = lax.ppermute(mine, 'h', [(0, 1), (1, 0)])  14.2 us
    ppermute x6, waiting for transfers between devices, swap_z(): return lax.ppermute(block, 'zl', [(i, i ^ k) for i in range(n)])  12.3 us
    all_to_all x1, starting transfers between devices, on_device(): lax.all_to_all(pieces, DEV, split_axis=0, concat_axis=0, tiled=True)  12.1 us
    dot_general x2, matrix products, on_device(): lax.dot_general(hidden, part[1], (((1,), (1,)), ((), ())), preferred_elem...  11.4 us
    ppermute x6, starting transfers between devices, swap_z(): return lax.ppermute(block, 'zl', [(i, i ^ k) for i in range(n)])  9.88 us
  transfers between devices with their start and end apart: 12, of which 7 were waited for; matrix products, arithmetic and copies ran while one was open for 23% of the time, Pallas kernels for 0%

profile of v2, /device:TPU:32, one launch (start us, length us, event | category | flops | bytes accessed | tf_op | source)
XLA Modules:
  0.0 188.4 jit_solution(11020111077944560134)
XLA Ops:
  6.6 1.4 constant_dynamic-slice_fusion
  8.2 1.8 collective-permute-done
  10.2 2.0 %collective-permute-start.3 = (bf16[128,1024]{1,0:T(8,128)(2,1)S(1)}, bf16[128,1024]{1,0:T(8,128)(2,1)S(1)}, u32[]{:S(2)}, u32[]{:S(2)}) collective-permute-start(bf16[128,1024]{1,0:T(8,128)(2,1)S(1)} %get-tuple-element.8), channel_id=1, source_target_pairs={{0,192},{64,128},{128,64},{192,0},{1,193},{65,129},{129,65},{193,1... | collective-permute-start | bytes 786440 | tf_op jit(solution)/shard_map/ppermute | solution.py:45
  12.2 2.3 %collective-permute-start.2 = (bf16[128,1024]{1,0:T(8,128)(2,1)S(1)}, bf16[128,1024]{1,0:T(8,128)(2,1)S(1)}, u32[]{:S(2)}, u32[]{:S(2)}) collective-permute-start(bf16[128,1024]{1,0:T(8,128)(2,1)S(1)} %get-tuple-element.9), channel_id=1, source_target_pairs={{0,128},{64,192},{128,0},{192,64},{1,129},{65,193},{129,1},{193,65... | collective-permute-start | bytes 786440 | tf_op jit(solution)/shard_map/ppermute | solution.py:45
  15.0 5.1 %collective-permute-start.8 = (bf16[2,32,1024]{2,1,0:T(8,128)(2,1)S(1)}, bf16[2,32,1024]{2,1,0:T(8,128)(2,1)S(1)}, u32[]{:S(2)}, u32[]{:S(2)}) collective-permute-start(bf16[2,32,1024]{2,1,0:T(8,128)(2,1)S(1)} %pad_maximum_fusion.11), channel_id=1, source_target_pairs={{0,1},{1,0},{2,3},{3,2},{4,5},{5,4},{6,7},{7,6},{8,9},{9,8},{10,11... | collective-permute-start | bytes 393224 | tf_op jit(solution)/shard_map/ppermute | solution.py:83
  20.1 14.2 %collective-permute-done.8 = bf16[2,32,1024]{2,1,0:T(8,128)(2,1)S(1)} collective-permute-done((bf16[2,32,1024]{2,1,0:T(8,128)(2,1)S(1)}, bf16[2,32,1024]{2,1,0:T(8,128)(2,1)S(1)}, u32[]{:S(2)}, u32[]{:S(2)}) %collective-permute-start.8) | collective-permute-done | bytes 131104 | tf_op jit(solution)/shard_map/ppermute | solution.py:83
  34.3 0.7 maximum_select_fusion
  35.1 5.4 %collective-permute-done.2 = bf16[128,1024]{1,0:T(8,128)(2,1)S(1)} collective-permute-done((bf16[128,1024]{1,0:T(8,128)(2,1)S(1)}, bf16[128,1024]{1,0:T(8,128)(2,1)S(1)}, u32[]{:S(2)}, u32[]{:S(2)}) %collective-permute-start.2) | collective-permute-done | bytes 262176 | tf_op jit(solution)/shard_map/ppermute | solution.py:45
  40.8 2.2 %convolution_convert_fusion.1 = bf16[512,512]{0,1:T(8,128)(2,1)S(1)} fusion(bf16[2,1024,512]{2,1,0:T(8,128)(2,1)} %param.17, f32[1024]{0:T(1024)S(1)} %copy-done.9, f32[512]{0:T(512)S(1)} %add_rsqrt_fusion.3, bf16[128,1024]{1,0:T(8,128)(2,1)S(1)} %collective-permute-done.3, bf16[128,1024]{1,0:T(8,128)(2,1)S(1)} %collective-permute-done.2, ...), kind=kOutput, calls=%fused_computation.81 | convolution fusion | flops 542900224 | bytes 2627584 | tf_op jit(solution)/shard_map/dot_general | solution.py:20
  43.2 0.9 convolution_convert_fusion
  45.3 0.8 convolution_convert_fusion.2
  47.0 3.2 %collective-permute-start.4 = (bf16[128,512]{1,0:T(8,128)(2,1)S(1)}, bf16[128,512]{1,0:T(8,128)(2,1)S(1)}, u32[]{:S(2)}, u32[]{:S(2)}) collective-permute-start(bf16[128,512]{1,0:T(8,128)(2,1)S(1)} %copy.42), channel_id=1, source_target_pairs={{0,64},{64,0},{128,192},{192,128},{1,65},{65,1},{129,193},{193,129... | collective-permute-start | bytes 393224 | tf_op jit(solution)/shard_map/ppermute | solution.py:45
  54.6 1.3 collective-permute-start.6
  58.0 3.8 %collective-permute-done.5 = bf16[128,512]{1,0:T(8,128)(2,1)S(1)} collective-permute-done((bf16[128,512]{1,0:T(8,128)(2,1)S(1)}, bf16[128,512]{1,0:T(8,128)(2,1)S(1)}, u32[]{:S(2)}, u32[]{:S(2)}) %collective-permute-start.5) | collective-permute-done | bytes 131104 | tf_op jit(solution)/shard_map/ppermute | solution.py:45
  61.8 3.0 %collective-permute-done.6 = bf16[128,512]{1,0:T(8,128)(2,1)S(1)} collective-permute-done((bf16[128,512]{1,0:T(8,128)(2,1)S(1)}, bf16[128,512]{1,0:T(8,128)(2,1)S(1)}, u32[]{:S(2)}, u32[]{:S(2)}) %collective-permute-start.6) | collective-permute-done | bytes 131104 | tf_op jit(solution)/shard_map/ppermute | solution.py:45
  65.3 1.3 collective-permute-done.7
  67.0 2.7 %fusion.28 = bf16[512,1024]{1,0:T(8,128)(2,1)} fusion(f32[64,8,1024]{2,0,1:T(8,128)S(1)} %convert_bitcast_fusion, bf16[512,1024]{1,0:T(8,128)(2,1)S(1)} %copy-done, bf16[8,64,512]{2,1,0:T(8,128)(2,1)S(1)} %bitcast.219), kind=kOutput, calls=%fused_computation.40 | convolution fusion | flops 537919488 | bytes 4718592 | tf_op jit(solution)/shard_map/dot_general | solution.py:20
  69.7 12.1 %all-to-all-start = ((bf16[32,2,8,1024]{3,2,1,0:T(8,128)(2,1)}), bf16[32,2,8,1024]{3,2,1,0:T(8,128)(2,1)S(1)}, u32[]{:S(2)}, u32[]{:S(2)}) async-start(bf16[32,2,8,1024]{3,2,1,0:T(8,128)(2,1)} %bitcast.40), calls=%async_computation | async-start | bytes 2097152 | tf_op jit(solution)/shard_map/all_to_all | solution.py:120
  83.1 0.7 iota_compare_fusion.1
  84.0 31.5 %all-to-all-done = bf16[32,2,8,1024]{3,2,1,0:T(8,128)(2,1)S(1)} async-done(((bf16[32,2,8,1024]{3,2,1,0:T(8,128)(2,1)}), bf16[32,2,8,1024]{3,2,1,0:T(8,128)(2,1)S(1)}, u32[]{:S(2)}, u32[]{:S(2)}) %all-to-all-start) | async-done | bytes 1048608 | tf_op jit(solution)/shard_map/all_to_all | solution.py:120
  116.0 1.7 convolution_convert_fusion.8
  117.7 0.8 copy.46
  118.5 1.7 convolution_convert_fusion.5
  120.7 1.7 convolution_convert_fusion.3
  122.6 1.7 convolution_convert_fusion.4
  124.4 1.7 convolution_convert_fusion.6
  126.3 2.4 %convolution_convert_fusion.7 = bf16[256,512]{1,0:T(8,128)(2,1)} fusion(bf16[2,1024,512]{2,1,0:T(8,128)(2,1)} %param.20, f32[1024]{0:T(1024)} %param.15, f32[32,8]{1,0:T(8,128)S(1)} %get-tuple-element.40, bf16[32,2,8,1024]{3,2,1,0:T(8,128)(2,1)S(1)} %all-to-all-done), kind=kOutput, calls=%fused_computation.93 | convolution fusion | flops 269615104 | bytes 1855488 | tf_op jit(solution)/shard_map/dot_general | solution.py:20
  128.7 1.1 copy.47
  134.9 6.1 %fusion.26 = f32[512,1024]{1,0:T(8,128)} fusion(bf16[2,1024,1024]{2,1,0:T(8,128)(2,1)} %all-gather.2.cloned.1.call-done, f32[1024]{0:T(1024)S(1)} %copy-done.11, f32[512]{0:T(512)S(1)} %add_rsqrt_fusion.2, bf16[256,1024]{1,0:T(8,128)(2,1)S(1)} %fusion.46, bf16[256,1024]{1,0:T(8,128)(2,1)S(1)} %fusion.45), kind=kOutput, calls=%fused_computation.36 | convolution fusion | flops 2155872256 | bytes 7346176 | tf_op jit(solution)/shard_map/dot_general | solution.py:140
  140.9 5.3 %fusion.7 = bf16[512,1024]{1,0:T(8,128)(2,1)S(1)} fusion(f32[512,1024]{1,0:T(8,128)} %fusion.26, bf16[2,1024,1024]{2,1,0:T(8,128)(2,1)} %collective-permute-done.9, f32[1024]{0:T(1024)S(1)} %copy-done.11, f32[512]{0:T(512)S(1)} %add_rsqrt_fusion.2, bf16[256,1024]{1,0:T(8,128)(2,1)S(1)} %fusion.46, bf16[256,1024]{1,0:T(8,128)(2,1)S(1)} %fusion.45), kind=kOutput, calls=%fused_computation.14 | convolution fusion | flops 2159542272 | bytes 9443328 | tf_op jit(solution)/shard_map/dot_general | solution.py:140
  146.3 33.7 %all_to_all.10 = bf16[32,2,8,1024]{3,2,1,0:T(8,128)(2,1)S(1)} all-to-all(bf16[32,2,8,1024]{3,2,1,0:T(8,128)(2,1)S(1)} %bitcast.217), channel_id=1, replica_groups=mesh['zl'=4,'c'=2,'x'=4,'y'=4,'h'=2] {'x','y','h'}, dimensions={0} | all-to-all | bytes 2097152 | tf_op jit(solution)/shard_map/all_to_all | solution.py:144
  180.0 1.5 copy.66
  (98 shorter events, 18.4 us)
Async XLA Ops:
  6.5 60.4 %copy-start = (bf16[512,1024]{1,0:T(8,128)(2,1)S(1)}, bf16[512,1024]{1,0:T(8,128)(2,1)}, u32[]{:S(2)}) copy-start(bf16[512,1024]{1,0:T(8,128)(2,1)} %param.19) | copy-start | bytes 3145732
  6.5 1.6 copy-start.3
  6.5 1.6 copy-start.4
  6.5 113.8 %all-gather.2.cloned.1.call-start = ((), (), s32[]{:S(2)}) async-start(), calls=%async_computation.2 | async-start | bytes 4456448 | tf_op jit(solution)/shard_map/all_gather | solution.py:96
  8.0 2.0 %collective-permute-start = (bf16[4,64,1024]{2,1,0:T(8,128)(2,1)S(1)}, bf16[4,64,1024]{2,1,0:T(8,128)(2,1)S(1)}, u32[]{:S(2)}, u32[]{:S(2)}) collective-permute-start(bf16[4,64,1024]{2,1,0:T(8,128)(2,1)S(1)} %get-tuple-element.12), channel_id=1, source_target_pairs={{0,32},{32,0},{1,33},{33,1},{2,34},{34,2},{3,35},{35,3},{4,36},{36... | collective-permute-start | bytes 1572872 | tf_op jit(solution)/shard_map/ppermute | solution.py:40
  10.1 30.7 %copy-start.9 = (f32[1024]{0:T(1024)S(1)}, f32[1024]{0:T(1024)}, u32[]{:S(2)}) copy-start(f32[1024]{0:T(1024)} %param.14) | copy-start | bytes 12292
  10.2 24.9 %collective-permute-start.3 = (bf16[128,1024]{1,0:T(8,128)(2,1)S(1)}, bf16[128,1024]{1,0:T(8,128)(2,1)S(1)}, u32[]{:S(2)}, u32[]{:S(2)}) collective-permute-start(bf16[128,1024]{1,0:T(8,128)(2,1)S(1)} %get-tuple-element.8), channel_id=1, source_target_pairs={{0,192},{64,128},{128,64},{192,0},{1,193},{65,129},{129,65},{193,1... | collective-permute-start | bytes 786440 | tf_op jit(solution)/shard_map/ppermute | solution.py:45
  12.2 28.3 %collective-permute-start.2 = (bf16[128,1024]{1,0:T(8,128)(2,1)S(1)}, bf16[128,1024]{1,0:T(8,128)(2,1)S(1)}, u32[]{:S(2)}, u32[]{:S(2)}) collective-permute-start(bf16[128,1024]{1,0:T(8,128)(2,1)S(1)} %get-tuple-element.9), channel_id=1, source_target_pairs={{0,128},{64,192},{128,0},{192,64},{1,129},{65,193},{129,1},{193,65... | collective-permute-start | bytes 786440 | tf_op jit(solution)/shard_map/ppermute | solution.py:45
  14.5 26.1 %collective-permute-start.1 = (bf16[128,1024]{1,0:T(8,128)(2,1)S(1)}, bf16[128,1024]{1,0:T(8,128)(2,1)S(1)}, u32[]{:S(2)}, u32[]{:S(2)}) collective-permute-start(bf16[128,1024]{1,0:T(8,128)(2,1)S(1)} %get-tuple-element.10), channel_id=1, source_target_pairs={{0,64},{64,0},{128,192},{192,128},{1,65},{65,1},{129,193},{193,129... | collective-permute-start | bytes 786440 | tf_op jit(solution)/shard_map/ppermute | solution.py:45
  15.0 19.3 %collective-permute-start.8 = (bf16[2,32,1024]{2,1,0:T(8,128)(2,1)S(1)}, bf16[2,32,1024]{2,1,0:T(8,128)(2,1)S(1)}, u32[]{:S(2)}, u32[]{:S(2)}) collective-permute-start(bf16[2,32,1024]{2,1,0:T(8,128)(2,1)S(1)} %pad_maximum_fusion.11), channel_id=1, source_target_pairs={{0,1},{1,0},{2,3},{3,2},{4,5},{5,4},{6,7},{7,6},{8,9},{9,8},{10,11... | collective-permute-start | bytes 393224 | tf_op jit(solution)/shard_map/ppermute | solution.py:83
  40.8 2.3 %copy-start.6 = (bf16[2,1024,512]{2,1,0:T(8,128)(2,1)S(1)}, bf16[2,1024,512]{2,1,0:T(8,128)(2,1)}, u32[]{:S(2)}) copy-start(bf16[2,1024,512]{2,1,0:T(8,128)(2,1)} %param.17) | copy-start | bytes 6291460
  44.0 1.2 copy-start.7
  46.1 0.8 copy-start.12
  47.0 11.0 %collective-permute-start.4 = (bf16[128,512]{1,0:T(8,128)(2,1)S(1)}, bf16[128,512]{1,0:T(8,128)(2,1)S(1)}, u32[]{:S(2)}, u32[]{:S(2)}) collective-permute-start(bf16[128,512]{1,0:T(8,128)(2,1)S(1)} %copy.42), channel_id=1, source_target_pairs={{0,64},{64,0},{128,192},{192,128},{1,65},{65,1},{129,193},{193,129... | collective-permute-start | bytes 393224 | tf_op jit(solution)/shard_map/ppermute | solution.py:45
  50.2 1.1 copy-start.13
  52.2 9.7 %collective-permute-start.5 = (bf16[128,512]{1,0:T(8,128)(2,1)S(1)}, bf16[128,512]{1,0:T(8,128)(2,1)S(1)}, u32[]{:S(2)}, u32[]{:S(2)}) collective-permute-start(bf16[128,512]{1,0:T(8,128)(2,1)S(1)} %copy.43), channel_id=1, source_target_pairs={{0,128},{64,192},{128,0},{192,64},{1,129},{65,193},{129,1},{193,65... | collective-permute-start | bytes 393224 | tf_op jit(solution)/shard_map/ppermute | solution.py:45
  54.6 10.2 %collective-permute-start.6 = (bf16[128,512]{1,0:T(8,128)(2,1)S(1)}, bf16[128,512]{1,0:T(8,128)(2,1)S(1)}, u32[]{:S(2)}, u32[]{:S(2)}) collective-permute-start(bf16[128,512]{1,0:T(8,128)(2,1)S(1)} %copy.44), channel_id=1, source_target_pairs={{0,192},{64,128},{128,64},{192,0},{1,193},{65,129},{129,65},{193,1... | collective-permute-start | bytes 393224 | tf_op jit(solution)/shard_map/ppermute | solution.py:45
  57.7 7.4 %copy-start.1 = (bf16[8,64,1024]{2,1,0:T(8,128)(2,1)S(1)}, bf16[8,64,1024]{2,1,0:T(8,128)(2,1)}, u32[]{:S(2)}) copy-start(bf16[8,64,1024]{2,1,0:T(8,128)(2,1)} %param.13) | copy-start | bytes 3145732
  64.9 1.6 collective-permute-start.7
  69.7 12.1 %copy-start.5 = (s32[2]{0:T(128)S(1)}, s32[2]{0:T(128)}, u32[]{:S(2)}) copy-start(s32[2]{0:T(128)} %param.25) | copy-start | bytes 28
  69.7 46.3 %copy-start.10 = (f32[1024]{0:T(1024)S(1)}, f32[1024]{0:T(1024)}, u32[]{:S(2)}) copy-start(f32[1024]{0:T(1024)} %param.15) | copy-start | bytes 12292
  69.7 45.8 %all-to-all-start = ((bf16[32,2,8,1024]{3,2,1,0:T(8,128)(2,1)}), bf16[32,2,8,1024]{3,2,1,0:T(8,128)(2,1)S(1)}, u32[]{:S(2)}, u32[]{:S(2)}) async-start(bf16[32,2,8,1024]{3,2,1,0:T(8,128)(2,1)} %bitcast.40), calls=%async_computation | async-start | bytes 2097152 | tf_op jit(solution)/shard_map/all_to_all | solution.py:120
  120.4 20.5 %collective-permute-start.9 = (bf16[2,1024,1024]{2,1,0:T(8,128)(2,1)}, bf16[2,1024,1024]{2,1,0:T(8,128)(2,1)}, u32[]{:S(2)}, u32[]{:S(2)}) collective-permute-start(bf16[2,1024,1024]{2,1,0:T(8,128)(2,1)} %all-gather.2.cloned.1.call-done), channel_id=1, source_target_pairs={{0,32},{32,0},{1,33},{33,1},{2,34},{34,2},{3,35},{35,3},{4,36},{36... | collective-permute-start | bytes 12582920 | tf_op jit(solution)/shard_map/ppermute | solution.py:40
  130.8 1.0 copy-start.2
  131.8 1.2 copy-start.8
  134.1 0.8 copy-start.11
Sparse Core Ops, SparseCore 0:
  35.2 69.2 all-gather.1

commit v3 on v2

v3 whole, which is shorter than its diff:
```python
import jax
import jax.numpy as jnp
from jax import lax
from jax.experimental import pallas as pl
from jax.experimental.pallas import tpu as pltpu
from jax.sharding import Mesh, PartitionSpec as P

HDIM = 64
GRP = ("zl", "c")
DEV = ("x", "y", "h")
BF = jnp.bfloat16
F32 = jnp.float32


def rms_scale(row_block, gain_vec):
    widened = row_block.astype(F32)
    inverse = lax.rsqrt(jnp.mean(widened * widened, axis=-1, keepdims=True) + 1e-05)
    return (widened * inverse * gain_vec).astype(BF)


def linear(rows, weight):
    return jnp.dot(rows, weight, preferred_element_type=F32)


def split_heads(rows):
    return rows.reshape(rows.shape[0], -1, HDIM)


def attend(queries, keys, values):
    scores = jnp.einsum("ihd,jhd->hij", queries, keys, preferred_element_type=F32)
    scores = scores * HDIM ** (-0.5)
    exponent = jnp.exp(scores - jnp.max(scores, axis=-1, keepdims=True))
    total = jnp.sum(exponent, axis=-1)
    weighted = jnp.einsum("hij,jhd->ihd", exponent.astype(BF), values, preferred_element_type=F32)
    context = weighted / jnp.transpose(total)[..., None]
    return context.reshape(queries.shape[0], -1).astype(BF)


LOG2E = 1.4426950408889634


def rms_block(rows, gain):
    inverse = lax.rsqrt(jnp.mean(rows * rows, axis=-1, keepdims=True) + 1e-05)
    return (rows * inverse * gain).astype(BF)


def time_kernel(start_ref, rows_ref, place_ref, place_row_ref, gain_ref, qk_ref, v_ref, o_ref, out_ref):
    agents, steps, width = rows_ref.shape
    later, earlier = place_ref[...], place_row_ref[...]
    for agent in range(agents):
        rows = rows_ref[agent].astype(F32)
        normed = rms_block(rows, gain_ref[...])
        queries = linear(normed, qk_ref[0]).astype(BF)
        keys = linear(normed, qk_ref[1]).astype(BF)
        values = linear(normed, v_ref[...]).astype(BF)
        begin = start_ref[agent]
        visible = (later >= earlier) & ((earlier >= begin) | (later < begin))
        context = []
        for h in range(queries.shape[1] // HDIM):
            part = slice(h * HDIM, (h + 1) * HDIM)
            scores = lax.dot_general(
                queries[:, part], keys[:, part], (((1,), (1,)), ((), ())), preferred_element_type=F32
            )
            scores = jnp.where(visible, scores, -jnp.inf)
            top = jnp.max(scores, axis=-1, keepdims=True)
            exponent = jnp.exp2((scores - top) * (LOG2E * HDIM ** (-0.5)))
            total = jnp.sum(exponent, axis=-1, keepdims=True)
            weighted = linear(exponent.astype(BF), values[:, part])
            context.append((weighted / total).astype(BF))
        context = jnp.concatenate(context, 1)
        out_ref[agent] = (rows + linear(context, o_ref[...])).astype(BF)


def time_block(series, places, starts, gain, pair, value, out):
    agents, steps, width = series.shape
    vmem = pl.BlockSpec(memory_space=pltpu.VMEM)
    return pl.pallas_call(
        time_kernel,
        out_shape=jax.ShapeDtypeStruct(series.shape, BF),
        in_specs=[pl.BlockSpec(memory_space=pltpu.SMEM)] + [vmem] * 7,
        out_specs=vmem,
        compiler_params=pltpu.CompilerParams(vmem_limit_bytes=28 << 20),
        cost_estimate=pl.CostEstimate(flops=3 << 30, bytes_accessed=6 << 20, transcendentals=1 << 20),
        name="time_attention",
    )(starts, series, places[:, None], places[None, :], gain[None, :], pair, value, out)


def gelu(x):
    inner = 0.7978845608028654 * (x + 0.044715 * (x * x * x))
    return (0.5 * x) * (1.0 + jnp.tanh(inner))


def ff_kernel(rows_ref, gain_ref, up_ref, down_ref, out_ref, inner, total):
    step, last = pl.program_id(0), pl.num_programs(0) - 1

    @pl.when(step == 0)
    def _():
        rows = rows_ref[...].astype(F32)
        inner[...] = rms_block(rows, gain_ref[...])
        total[...] = rows

    hidden = gelu(linear(inner[...], up_ref[0, 0])).astype(BF)
    total[...] += lax.dot_general(
        hidden, down_ref[0, 0], (((1,), (1,)), ((), ())), preferred_element_type=F32
    )

    @pl.when(step == last)
    def _():
        out_ref[...] = total[...].astype(BF)


def ff_block(rows, gain, weights):
    count, width = rows.shape
    halves, half = weights.shape[1], weights.shape[3]
    size = 512
    n = half // size
    whole = pl.BlockSpec((count, width), lambda i: (0, 0))
    up = pl.BlockSpec((1, 1, width, size), lambda i: (0, i // n, 0, i % n))
    down = pl.BlockSpec((1, 1, width, size), lambda i: (1, i // n, 0, i % n))
    return pl.pallas_call(
        ff_kernel,
        grid=(halves * n,),
        out_shape=jax.ShapeDtypeStruct((count, width), BF),
        in_specs=[whole, pl.BlockSpec((1, width), lambda i: (0, 0)), up, down],
        out_specs=whole,
        scratch_shapes=[pltpu.VMEM((count, width), BF), pltpu.VMEM((count, width), F32)],
        compiler_params=pltpu.CompilerParams(vmem_limit_bytes=28 << 20),
        cost_estimate=pl.CostEstimate(flops=4 << 30, bytes_accessed=10 << 20, transcendentals=1 << 20),
        name="feed_forward",
    )(rows, gain[None, :], weights, weights)


def swap_core(block):
    return lax.ppermute(block, "c", [(0, 1), (1, 0)])


def swap_z(block, k):
    n = lax.axis_size("zl")
    return lax.ppermute(block, "zl", [(i, i ^ k) for i in range(n)])


def other_half(block, zl, high):
    n = lax.axis_size("zl")
    spot = lambda h, z: z * 2 + h
    edge = [(spot(h, z), spot(1 - h, n - 1 - z)) for h in (0, 1) for z in (0, n - 1)]
    inner = [(spot(h, z), spot(h, w)) for h in (0, 1) for z, w in ((0, 1), (n - 1, n - 2))]
    outer = lax.ppermute(block, ("zl", "h"), edge)
    inward = lax.ppermute(outer, ("zl", "h"), inner)
    return jnp.where((zl == 0) | (zl == n - 1), outer, inward)


def on_device(
    rollout,
    agent_gain,
    time_gain,
    inner_gain,
    agent_pair,
    agent_value,
    agent_out,
    time_pair,
    time_value,
    time_out,
    expand_weight,
    reduce_weight,
    episode_start,
):
    steps_here, agents_here, width = rollout.shape
    zl, core, high = lax.axis_index("zl"), lax.axis_index("c"), lax.axis_index("h")
    n_zl, n_core = lax.axis_size("zl"), lax.axis_size("c")

    half = expand_weight.shape[1] // 2
    up = lax.dynamic_slice_in_dim(expand_weight, core * half, half, 1)
    down = lax.dynamic_slice_in_dim(reduce_weight.T, core * half, half, 1)
    mine = jnp.stack([up, down])
    other = other_half(mine, zl, high)

    by_step = rollout.reshape(n_zl, n_core, agents_here, width)
    chunks = [lax.dynamic_index_in_dim(by_step, zl ^ k, 0, keepdims=False) for k in range(n_zl)]
    chunks = [chunks[0]] + [swap_z(chunks[k], k) for k in range(1, n_zl)]
    keep = jnp.stack([lax.dynamic_index_in_dim(c, core, 0, keepdims=False) for c in chunks])
    give = jnp.stack([lax.dynamic_index_in_dim(c, 1 - core, 0, keepdims=False) for c in chunks])
    got = swap_core(give)
    both = jnp.stack([jnp.where(core == 0, keep, got), jnp.where(core == 0, got, keep)], 1)
    rows = jnp.zeros_like(both)
    for k in range(n_zl):
        rows = lax.dynamic_update_index_in_dim(rows, both[k], zl ^ k, 0)
    rows = rows.reshape(-1, width)

    rows, other = lax.optimization_barrier((rows, other))
    pair = jnp.where(
        high == 0, jnp.concatenate([mine, other], 1), jnp.concatenate([other, mine], 1)
    )
    weights = lax.all_gather(pair, ("c", "x", "y"), axis=1, tiled=True)
    weights = weights.reshape(2, n_core, width, half)

    normed = rms_scale(rows, agent_gain)
    queries = split_heads(linear(normed, agent_pair[0]).astype(BF))
    keys = split_heads(linear(normed, agent_pair[1]).astype(BF))
    values = split_heads(linear(normed, agent_value).astype(BF))
    context = attend(queries, keys, values)
    after_agents = (rows.astype(F32) + linear(context, agent_out)).astype(BF)

    n_grp, n_dev = n_zl * n_core, lax.axis_size(DEV)
    agents_own = episode_start.shape[0]
    steps = n_dev * steps_here
    pieces = after_agents.reshape(n_grp, n_dev, agents_own, width)
    pieces = jnp.swapaxes(pieces, 0, 1).reshape(steps, agents_own, width)
    series = lax.all_to_all(pieces, DEV + GRP, split_axis=0, concat_axis=0, tiled=True)
    series = jnp.swapaxes(series, 0, 1)
    places = lax.iota(jnp.int32, steps)
    after_time = time_block(
        series, places, episode_start, time_gain, time_pair, time_value, time_out
    )
    result = ff_block(after_time.reshape(-1, width), inner_gain, weights)
    result = result.reshape(agents_own, n_dev, steps_here, width)
    result = lax.all_to_all(
        jnp.swapaxes(result, 0, 1), DEV, split_axis=0, concat_axis=0, tiled=True
    )
    return jnp.swapaxes(result.reshape(agents_here, steps_here, width), 0, 1)


def solution(mesh):
    fine = Mesh(mesh.devices.reshape(4, 2, 4, 4, 2), ("zl", "c", "x", "y", "h"))
    return jax.shard_map(
        on_device,
        mesh=fine,
        in_specs=(
            P(DEV, GRP, None),
            P(),
            P(),
            P(),
            P(),
            P(),
            P(),
            P(),
            P(),
            P(),
            P(DEV, None),
            P(None, DEV),
            P(GRP + DEV),
        ),
        out_specs=P(DEV, GRP, None),
        check_vma=False,
    )
```

time: 189 us -> 173 us (0.915)
  blocking collectives: 33.7 us -> 84.4 us
  matrix products: 37 us -> 7.53 us
  waiting for transfers between devices: 61 us -> 33.8 us
  starting transfers between devices: 27.6 us -> 5.98 us
  Pallas kernels: 0 us -> 15 us
  other arithmetic: 7.02 us -> 2.74 us
    all_to_all x0 -> x1, blocking collectives: none -> 41.9 us  [on_device(): lax.all_to_all(pieces, DEV + GRP, split_axis=0, concat_axis=0, tiled=True)]
    all_to_all x1 -> x0, waiting for transfers between devices: 31.5 us -> none  [on_device(): lax.all_to_all(pieces, DEV, split_axis=0, concat_axis=0, tiled=True)]
    pallas_call x0 -> x2, Pallas kernels: none -> 15 us  [the longest x1 8.45 us: time_block(): pl.pallas_call(time_kernel, out_shape=jax.ShapeDtypeStruct(series.shape,...]
    dot_general x12 -> x4, matrix products: 18.5 us -> 4.65 us  [linear(): return jnp.dot(rows, weight, preferred_element_type=F32)]
    all_to_all x1 -> x0, starting transfers between devices: 12.1 us -> none  [on_device(): lax.all_to_all(pieces, DEV, split_axis=0, concat_axis=0, tiled=True)]
    dot_general x2 -> x0, matrix products: 11.4 us -> none  [on_device(): lax.dot_general(hidden, part[1], (((1,), (1,)), ((), ())), preferred_elem...]
    ppermute x6 -> x3, waiting for transfers between devices: 12.3 us -> 21.8 us  [swap_z(): return lax.ppermute(block, 'zl', [(i, i ^ k) for i in range(n)])]
    all_to_all x1, blocking collectives: 33.7 us -> 42.5 us  [on_device(): lax.all_to_all(jnp.swapaxes(result, 0, 1), DEV, split_axis=0, concat_axis...]
  transfers between devices with their start and end apart: 12 -> 7, of which waited for: 7 -> 5; matrix products, arithmetic and copies ran while one was open for 23% -> 7% of each run, Pallas kernels for 0% -> 5%
where the time goes in v3:
time: 173 us
  blocking collectives  84.4 us (49%)
  waiting for transfers between devices  33.8 us (20%)
  Pallas kernels  15 us (9%)
  between operations  13.8 us (8%)
  local copies, waits for them, and re-layouts  9.7 us (6%)
  matrix products  7.53 us (4%)
  starting transfers between devices  5.98 us (3%)
  other arithmetic  2.74 us (2%)
    all_to_all x1, blocking collectives, on_device(): lax.all_to_all(jnp.swapaxes(result, 0, 1), DEV, split_axis=0, concat_axis...  42.5 us
    all_to_all x1, blocking collectives, on_device(): lax.all_to_all(pieces, DEV + GRP, split_axis=0, concat_axis=0, tiled=True)  41.9 us
    ppermute x3, waiting for transfers between devices, swap_z(): return lax.ppermute(block, 'zl', [(i, i ^ k) for i in range(n)])  21.8 us
    ppermute x1, waiting for transfers between devices, other_half(): inward = lax.ppermute(outer, ('zl', 'h'), inner)  10.5 us
    pallas_call x1, Pallas kernels, time_block(): pl.pallas_call(time_kernel, out_shape=jax.ShapeDtypeStruct(series.shape,...  8.45 us
    pallas_call x1, Pallas kernels, ff_block(): pl.pallas_call(ff_kernel, grid=(halves * n,), out_shape=jax.ShapeDtypeStr...  6.53 us
    dot_general x4, matrix products, linear(): return jnp.dot(rows, weight, preferred_element_type=F32)  4.65 us
    ppermute x3, starting transfers between devices, swap_z(): return lax.ppermute(block, 'zl', [(i, i ^ k) for i in range(n)])  3.92 us
  transfers between devices with their start and end apart: 7, of which 5 were waited for; matrix products, arithmetic and copies ran while one was open for 7% of the time, Pallas kernels for 5%

profile of v3, /device:TPU:32, one launch (start us, length us, event | category | flops | bytes accessed | tf_op | source)
XLA Modules:
  0.0 172.9 jit_solution(5036330222678345112)
XLA Ops:
  6.6 1.3 dynamic-slice_bitcast_fusion.2
  7.8 1.9 %collective-permute-start = (bf16[2,64,1024]{2,1,0:T(8,128)(2,1)S(1)}, bf16[2,64,1024]{2,1,0:T(8,128)(2,1)S(1)}, u32[]{:S(2)}, u32[]{:S(2)}) collective-permute-start(bf16[2,64,1024]{2,1,0:T(8,128)(2,1)S(1)} %get-tuple-element.13), channel_id=1, source_target_pairs={{0,64},{64,0},{128,192},{192,128},{1,65},{65,1},{129,193},{193,129... | collective-permute-start | bytes 786440 | tf_op jit(solution)/shard_map/ppermute | solution.py:139
  9.8 1.5 collective-permute-start.1
  11.3 0.5 collective-permute-start.2
  11.8 1.0 dynamic-slice_bitcast_fusion.4
  12.8 5.9 %collective-permute-done = bf16[2,64,1024]{2,1,0:T(8,128)(2,1)S(1)} collective-permute-done((bf16[2,64,1024]{2,1,0:T(8,128)(2,1)S(1)}, bf16[2,64,1024]{2,1,0:T(8,128)(2,1)S(1)}, u32[]{:S(2)}, u32[]{:S(2)}) %collective-permute-start) | collective-permute-done | bytes 262176 | tf_op jit(solution)/shard_map/ppermute | solution.py:139
  18.7 10.5 %collective-permute-done.1 = bf16[2,64,1024]{2,1,0:T(8,128)(2,1)S(1)} collective-permute-done((bf16[2,64,1024]{2,1,0:T(8,128)(2,1)S(1)}, bf16[2,64,1024]{2,1,0:T(8,128)(2,1)S(1)}, u32[]{:S(2)}, u32[]{:S(2)}) %collective-permute-start.1) | collective-permute-done | bytes 262176 | tf_op jit(solution)/shard_map/ppermute | solution.py:139
  29.3 5.4 %collective-permute-done.2 = bf16[2,64,1024]{2,1,0:T(8,128)(2,1)S(1)} collective-permute-done((bf16[2,64,1024]{2,1,0:T(8,128)(2,1)S(1)}, bf16[2,64,1024]{2,1,0:T(8,128)(2,1)S(1)}, u32[]{:S(2)}, u32[]{:S(2)}) %collective-permute-start.2) | collective-permute-done | bytes 262176 | tf_op jit(solution)/shard_map/ppermute | solution.py:139
  34.9 0.7 collective-permute-start.4
  35.6 1.3 collective-permute-start.5
  36.9 10.5 %collective-permute-done.5 = bf16[2,32,1024]{2,1,0:T(8,128)(2,1)S(1)} collective-permute-done((bf16[2,32,1024]{2,1,0:T(8,128)(2,1)S(1)}, bf16[2,32,1024]{2,1,0:T(8,128)(2,1)S(1)}, u32[]{:S(2)}, u32[]{:S(2)}) %collective-permute-start.5) | collective-permute-done | bytes 131104 | tf_op jit(solution)/shard_map/ppermute | solution.py:148
  47.6 0.1 broadcast_in_dim.20
  47.8 0.8 maximum_select_fusion
  48.6 0.3 fusion.6
  48.9 2.2 %convolution_convert_fusion = bf16[512,512]{0,1:T(8,128)(2,1)S(1)} fusion(bf16[2,1024,512]{2,1,0:T(8,128)(2,1)} %param.17, bf16[512,1024]{1,0:T(8,128)(2,1)S(1)} %bitcast.70, f32[1024]{0:T(1024)S(1)} %copy-done.12, f32[512]{0:T(512)S(1)} %add_rsqrt_fusion), kind=kOutput, calls=%fused_computation.21 | convolution fusion | flops 539230208 | bytes 2627584 | tf_op jit(solution)/shard_map/dot_general | solution.py:22
  51.2 0.8 convolution_convert_fusion.1
  52.0 0.4 copy-done.11
  52.4 0.8 convolution_convert_fusion.2
  53.2 1.3 multiply_reduce_fusion
  54.5 1.4 fusion
  55.9 1.6 divide_convert_fusion
  57.5 0.8 fusion.9
  58.3 0.4 reshape.53
  58.7 1.1 copy.20
  59.9 41.9 %all_to_all.10 = bf16[256,2,1024]{2,1,0:T(2,128)(2,1)S(1)} all-to-all(bf16[256,2,1024]{2,1,0:T(2,128)(2,1)S(1)} %bitcast.75), channel_id=1, replica_groups=mesh['zl'=4,'c'=2,'x'=4,'y'=4,'h'=2] {'x','y','h','zl','c'}, dimensions={0} | all-to-all | bytes 2097152 | tf_op jit(solution)/shard_map/all_to_all | solution.py:208
  101.8 0.3 copy.30
  102.2 8.5 %time_attention.1 = bf16[2,256,1024]{2,1,0:T(8,128)(2,1)S(1)} custom-call(s32[2]{0:T(128)S(1)} %copy-done.7, bf16[2,256,1024]{2,1,0:T(8,128)(2,1)S(1)} %bitcast.66, s32[256,1]{1,0:T(8,128)S(1)} %iota.7.place_ref, s32[1,256]{1,0:T(1,128)S(1)} %iota.8.place_row_ref, f32[1,1024]{1,0:T(1,128)S(1)} %bitcast.68, bf16[2,1024,512]{2,1,0:T(8,128)(2,1)S(1)} %copy-done.3, ...), custom_call_target="tpu_custom_call" | custom-call | flops 3221225472 | bytes 6291456 | tf_op jit(solution)/shard_map/time_attention/pallas_call | solution.py:77
  110.6 1.4 all-gather.2.cloned.1.call-done
  112.0 3.4 %copy-done.1 = bf16[2,2048,1024]{2,1,0:T(8,128)(2,1)S(1)} copy-done((bf16[2,2048,1024]{2,1,0:T(8,128)(2,1)S(1)}, bf16[2,2048,1024]{2,1,0:T(8,128)(2,1)}, u32[]{:S(2)}) %copy-start.1) | copy-done | bytes 8388632
  115.4 6.5 %feed_forward.1 = bf16[512,1024]{1,0:T(8,128)(2,1)S(1)} custom-call(bf16[512,1024]{1,0:T(8,128)(2,1)S(1)} %bitcast.65, f32[1,1024]{1,0:T(1,128)S(1)} %bitcast.67, bf16[2,2,1024,1024]{3,2,1,0:T(8,128)(2,1)S(1)} %bitcast.62, bf16[2,2,1024,1024]{3,2,1,0:T(8,128)(2,1)S(1)} %bitcast.63), custom_call_target="tpu_custom_call" | custom-call | flops 4294967296 | bytes 10485760 | tf_op jit(solution)/shard_map/feed_forward/pallas_call | solution.py:120
  122.0 42.5 %all_to_all.11 = bf16[32,2,8,1024]{3,2,1,0:T(8,128)(2,1)S(1)} all-to-all(bf16[32,2,8,1024]{3,2,1,0:T(8,128)(2,1)S(1)} %bitcast.76), channel_id=1, replica_groups=mesh['zl'=4,'c'=2,'x'=4,'y'=4,'h'=2] {'x','y','h'}, dimensions={0} | all-to-all | bytes 2097152 | tf_op jit(solution)/shard_map/all_to_all | solution.py:216
  164.5 1.5 copy.28
  (46 shorter events, 0.7 us)
Async XLA Ops:
  6.5 51.0 %copy-start = (bf16[512,1024]{1,0:T(8,128)(2,1)S(1)}, bf16[512,1024]{1,0:T(8,128)(2,1)}, u32[]{:S(2)}) copy-start(bf16[512,1024]{1,0:T(8,128)(2,1)} %param.19) | copy-start | bytes 3145732
  6.5 6.2 %copy-start.8 = (bf16[2048,32]{0,1:T(8,128)(2,1)S(1)}, bf16[2048,32]{0,1:T(8,128)(2,1)}, u32[]{:S(2)}) copy-start(bf16[2048,32]{0,1:T(8,128)(2,1)} %param.24) | copy-start | bytes 393220
  6.5 6.2 %copy-start.9 = (bf16[32,2048]{1,0:T(8,128)(2,1)S(1)}, bf16[32,2048]{1,0:T(8,128)(2,1)}, u32[]{:S(2)}) copy-start(bf16[32,2048]{1,0:T(8,128)(2,1)} %param.23) | copy-start | bytes 393220
  6.5 105.5 %all-gather.2.cloned.1.call-start = ((), (), s32[]{:S(2)}) async-start(), calls=%async_computation.2 | async-start | bytes 8650752 | tf_op jit(solution)/shard_map/all_gather | solution.py:193
  7.8 10.9 %collective-permute-start = (bf16[2,64,1024]{2,1,0:T(8,128)(2,1)S(1)}, bf16[2,64,1024]{2,1,0:T(8,128)(2,1)S(1)}, u32[]{:S(2)}, u32[]{:S(2)}) collective-permute-start(bf16[2,64,1024]{2,1,0:T(8,128)(2,1)S(1)} %get-tuple-element.13), channel_id=1, source_target_pairs={{0,64},{64,0},{128,192},{192,128},{1,65},{65,1},{129,193},{193,129... | collective-permute-start | bytes 786440 | tf_op jit(solution)/shard_map/ppermute | solution.py:139
  9.8 19.5 %collective-permute-start.1 = (bf16[2,64,1024]{2,1,0:T(8,128)(2,1)S(1)}, bf16[2,64,1024]{2,1,0:T(8,128)(2,1)S(1)}, u32[]{:S(2)}, u32[]{:S(2)}) collective-permute-start(bf16[2,64,1024]{2,1,0:T(8,128)(2,1)S(1)} %get-tuple-element.15), channel_id=1, source_target_pairs={{0,128},{64,192},{128,0},{192,64},{1,129},{65,193},{129,1},{193,65... | collective-permute-start | bytes 786440 | tf_op jit(solution)/shard_map/ppermute | solution.py:139
  11.3 23.4 %collective-permute-start.2 = (bf16[2,64,1024]{2,1,0:T(8,128)(2,1)S(1)}, bf16[2,64,1024]{2,1,0:T(8,128)(2,1)S(1)}, u32[]{:S(2)}, u32[]{:S(2)}) collective-permute-start(bf16[2,64,1024]{2,1,0:T(8,128)(2,1)S(1)} %get-tuple-element.14), channel_id=1, source_target_pairs={{0,192},{64,128},{128,64},{192,0},{1,193},{65,129},{129,65},{193,1... | collective-permute-start | bytes 786440 | tf_op jit(solution)/shard_map/ppermute | solution.py:139
  34.8 12.7 %collective-permute-start.3 = (bf16[4,64,1024]{2,1,0:T(8,128)(2,1)S(1)}, bf16[4,64,1024]{2,1,0:T(8,128)(2,1)S(1)}, u32[]{:S(2)}, u32[]{:S(2)}) collective-permute-start(bf16[4,64,1024]{2,1,0:T(8,128)(2,1)S(1)} %pad_maximum_fusion.1), channel_id=1, source_target_pairs={{0,32},{32,0},{1,33},{33,1},{2,34},{34,2},{3,35},{35,3},{4,36},{36... | collective-permute-start | bytes 1572872 | tf_op jit(solution)/shard_map/ppermute | solution.py:134
  34.9 0.7 collective-permute-start.4
  35.6 11.8 %collective-permute-start.5 = (bf16[2,32,1024]{2,1,0:T(8,128)(2,1)S(1)}, bf16[2,32,1024]{2,1,0:T(8,128)(2,1)S(1)}, u32[]{:S(2)}, u32[]{:S(2)}) collective-permute-start(bf16[2,32,1024]{2,1,0:T(8,128)(2,1)S(1)} %collective-permute-done.4), channel_id=1, source_target_pairs={{0,64},{192,128},{1,65},{193,129},{2,66},{194,130},{3,67},{195,131... | collective-permute-start | bytes 393224 | tf_op jit(solution)/shard_map/ppermute | solution.py:148
  47.7 1.2 copy-start.12
  48.9 2.2 %copy-start.10 = (bf16[2,1024,512]{2,1,0:T(8,128)(2,1)S(1)}, bf16[2,1024,512]{2,1,0:T(8,128)(2,1)}, u32[]{:S(2)}) copy-start(bf16[2,1024,512]{2,1,0:T(8,128)(2,1)} %param.17) | copy-start | bytes 6291460
  51.2 1.2 copy-start.11
  59.8 42.3 %copy-start.3 = (bf16[2,1024,512]{2,1,0:T(8,128)(2,1)S(1)}, bf16[2,1024,512]{2,1,0:T(8,128)(2,1)}, u32[]{:S(2)}) copy-start(bf16[2,1024,512]{2,1,0:T(8,128)(2,1)} %qk_ref.1) | copy-start | bytes 6291460
  59.8 42.3 %copy-start.4 = (bf16[1024,512]{1,0:T(8,128)(2,1)S(1)}, bf16[1024,512]{1,0:T(8,128)(2,1)}, u32[]{:S(2)}) copy-start(bf16[1024,512]{1,0:T(8,128)(2,1)} %v_ref.1) | copy-start | bytes 3145732
  59.8 42.3 %copy-start.5 = (bf16[512,1024]{1,0:T(8,128)(2,1)S(1)}, bf16[512,1024]{1,0:T(8,128)(2,1)}, u32[]{:S(2)}) copy-start(bf16[512,1024]{1,0:T(8,128)(2,1)} %o_ref.1) | copy-start | bytes 3145732
  59.9 42.3 %copy-start.6 = (f32[1024]{0:T(1024)S(1)}, f32[1024]{0:T(1024)}, u32[]{:S(2)}) copy-start(f32[1024]{0:T(1024)} %param.15) | copy-start | bytes 12292
  59.9 42.3 %copy-start.7 = (s32[2]{0:T(128)S(1)}, s32[2]{0:T(128)}, u32[]{:S(2)}) copy-start(s32[2]{0:T(128)} %start_ref.1) | copy-start | bytes 28
  102.1 9.9 %copy-start.2 = (f32[1024]{0:T(1024)S(1)}, f32[1024]{0:T(1024)}, u32[]{:S(2)}) copy-start(f32[1024]{0:T(1024)} %param.16) | copy-start | bytes 12292
  112.0 3.4 %copy-start.1 = (bf16[2,2048,1024]{2,1,0:T(8,128)(2,1)S(1)}, bf16[2,2048,1024]{2,1,0:T(8,128)(2,1)}, u32[]{:S(2)}) copy-start(bf16[2,2048,1024]{2,1,0:T(8,128)(2,1)} %all-gather.2.cloned.1.call-done) | copy-start | bytes 25165828
Sparse Core Ops, SparseCore 0:
  48.7 63.2 all-gather.1

commit v4 on v3

--- a/solution.py
+++ b/solution.py
@@ -8,6 +8,7 @@
 HDIM = 64
 GRP = ("zl", "c")
 DEV = ("x", "y", "h")
+TURNED = ("h", "x", "y")
 BF = jnp.bfloat16
 F32 = jnp.float32
 
@@ -124,7 +125,7 @@
         in_specs=[whole, pl.BlockSpec((1, width), lambda i: (0, 0)), up, down],
         out_specs=whole,
         scratch_shapes=[pltpu.VMEM((count, width), BF), pltpu.VMEM((count, width), F32)],
-        compiler_params=pltpu.CompilerParams(vmem_limit_bytes=28 << 20),
+        compiler_params=pltpu.CompilerParams(vmem_limit_bytes=58 << 20),
         cost_estimate=pl.CostEstimate(flops=4 << 30, bytes_accessed=10 << 20, transcendentals=1 << 20),
         name="feed_forward",
     )(rows, gain[None, :], weights, weights)
@@ -176,7 +177,9 @@
 
     by_step = rollout.reshape(n_zl, n_core, agents_here, width)
     chunks = [lax.dynamic_index_in_dim(by_step, zl ^ k, 0, keepdims=False) for k in range(n_zl)]
-    chunks = [chunks[0]] + [swap_z(chunks[k], k) for k in range(1, n_zl)]
+    arrived = [swap_z(chunks[k], k) for k in range(1, n_zl)]
+    arrived, other = lax.optimization_barrier((arrived, other))
+    chunks = chunks[:1] + arrived
     keep = jnp.stack([lax.dynamic_index_in_dim(c, core, 0, keepdims=False) for c in chunks])
     give = jnp.stack([lax.dynamic_index_in_dim(c, 1 - core, 0, keepdims=False) for c in chunks])
     got = swap_core(give)
@@ -186,7 +189,6 @@
         rows = lax.dynamic_update_index_in_dim(rows, both[k], zl ^ k, 0)
     rows = rows.reshape(-1, width)
 
-    rows, other = lax.optimization_barrier((rows, other))
     pair = jnp.where(
         high == 0, jnp.concatenate([mine, other], 1), jnp.concatenate([other, mine], 1)
     )
@@ -203,20 +205,24 @@
     n_grp, n_dev = n_zl * n_core, lax.axis_size(DEV)
     agents_own = episode_start.shape[0]
     steps = n_dev * steps_here
-    pieces = after_agents.reshape(n_grp, n_dev, agents_own, width)
-    pieces = jnp.swapaxes(pieces, 0, 1).reshape(steps, agents_own, width)
-    series = lax.all_to_all(pieces, DEV + GRP, split_axis=0, concat_axis=0, tiled=True)
+    n_high = lax.axis_size("h")
+    n_flat = n_dev // n_high
+    pieces = after_agents.reshape(n_grp, n_flat, n_high, agents_own, width)
+    pieces = jnp.transpose(pieces, (2, 1, 0, 3, 4)).reshape(steps, agents_own, width)
+    series = lax.all_to_all(pieces, TURNED + GRP, split_axis=0, concat_axis=0, tiled=True)
     series = jnp.swapaxes(series, 0, 1)
-    places = lax.iota(jnp.int32, steps)
+    places = lax.iota(jnp.int32, steps).reshape(n_flat, n_high, n_grp)
+    places = jnp.swapaxes(places, 0, 1).reshape(steps)
     after_time = time_block(
         series, places, episode_start, time_gain, time_pair, time_value, time_out
     )
     result = ff_block(after_time.reshape(-1, width), inner_gain, weights)
     result = result.reshape(agents_own, n_dev, steps_here, width)
     result = lax.all_to_all(
-        jnp.swapaxes(result, 0, 1), DEV, split_axis=0, concat_axis=0, tiled=True
-    )
-    return jnp.swapaxes(result.reshape(agents_here, steps_here, width), 0, 1)
+        jnp.swapaxes(result, 0, 1), TURNED, split_axis=0, concat_axis=0, tiled=True
+    )
+    result = result.reshape(n_high, n_flat, agents_own, steps_here, width)
+    return jnp.transpose(result, (3, 1, 0, 2, 4)).reshape(steps_here, agents_here, width)
 
 
 def solution(mesh):

time: 173 us -> 173 us (level)
  blocking collectives: 84.4 us -> 37.3 us
  starting transfers between devices: 5.98 us -> 27 us
  waiting for transfers between devices: 33.8 us -> 53 us
  local copies, waits for them, and re-layouts: 9.7 us -> 15.1 us
  Pallas kernels: 15 us -> 17.5 us
    all_to_all x2 -> x1, blocking collectives: 84.4 us -> 37.3 us  [on_device(): lax.all_to_all(jnp.swapaxes(result, 0, 1), TURNED, split_axis=0, concat_a...]
    all_to_all x0 -> x1, waiting for transfers between devices: none -> 28.8 us  [on_device(): lax.all_to_all(pieces, TURNED + GRP, split_axis=0, concat_axis=0, tiled=T...]
    all_to_all x0 -> x1, starting transfers between devices: none -> 12.6 us  [on_device(): lax.all_to_all(pieces, TURNED + GRP, split_axis=0, concat_axis=0, tiled=T...]
    ppermute x1, waiting for transfers between devices: 10.5 us -> 1.55 us  [other_half(): inward = lax.ppermute(outer, ('zl', 'h'), inner)]
    ppermute x3, starting transfers between devices: 3.92 us -> 12.3 us  [swap_z(): return lax.ppermute(block, 'zl', [(i, i ^ k) for i in range(n)])]
    pallas_call x1, Pallas kernels: 6.53 us -> 9.07 us  [ff_block(): pl.pallas_call(ff_kernel, grid=(halves * n,), out_shape=jax.ShapeDtypeStr...]
    transpose x1 -> x2, local copies, waits for them, and re-layouts: 1.08 us -> 3.16 us  [the longest x1 2.08 us: on_device(): jnp.transpose(pieces, (2, 1, 0, 3, 4)).reshape(steps, agents_own, width)]
    ppermute x1, waiting for transfers between devices: 0.01 us -> 1.89 us  [swap_core(): return lax.ppermute(block, 'c', [(0, 1), (1, 0)])]
  transfers between devices with their start and end apart: 7 -> 8, of which waited for: 5 -> 6; matrix products, arithmetic and copies ran while one was open for 7% -> 9% of each run, Pallas kernels for 5% -> 5%
where the time goes in v4:
time: 173 us
  waiting for transfers between devices  53 us (31%)
  blocking collectives  37.3 us (22%)
  starting transfers between devices  27 us (16%)
  Pallas kernels  17.5 us (10%)
  local copies, waits for them, and re-layouts  15.1 us (9%)
  between operations  13.7 us (8%)
  matrix products  5.9 us (3%)
  other arithmetic  3.35 us (2%)
    all_to_all x1, blocking collectives, on_device(): lax.all_to_all(jnp.swapaxes(result, 0, 1), TURNED, split_axis=0, concat_a...  37.3 us
    all_to_all x1, waiting for transfers between devices, on_device(): lax.all_to_all(pieces, TURNED + GRP, split_axis=0, concat_axis=0, tiled=T...  28.8 us
    ppermute x3, waiting for transfers between devices, swap_z(): return lax.ppermute(block, 'zl', [(i, i ^ k) for i in range(n)])  20.8 us
    all_to_all x1, starting transfers between devices, on_device(): lax.all_to_all(pieces, TURNED + GRP, split_axis=0, concat_axis=0, tiled=T...  12.6 us
    ppermute x3, starting transfers between devices, swap_z(): return lax.ppermute(block, 'zl', [(i, i ^ k) for i in range(n)])  12.3 us
    pallas_call x1, Pallas kernels, ff_block(): pl.pallas_call(ff_kernel, grid=(halves * n,), out_shape=jax.ShapeDtypeStr...  9.07 us
    pallas_call x1, Pallas kernels, time_block(): pl.pallas_call(time_kernel, out_shape=jax.ShapeDtypeStruct(series.shape,...  8.43 us
  transfers between devices with their start and end apart: 8, of which 6 were waited for; matrix products, arithmetic and copies ran while one was open for 9% of the time, Pallas kernels for 5%

profile of v4, /device:TPU:32, one launch (start us, length us, event | category | flops | bytes accessed | tf_op | source)
XLA Modules:
  0.0 172.9 jit_solution(9195678195407555783)
XLA Ops:
  6.5 0.9 dynamic-slice_bitcast_fusion.5
  7.5 0.8 dynamic-slice_bitcast_fusion.6
  9.0 1.3 collective-permute-start.4
  10.3 1.2 dynamic-slice_bitcast_fusion
  11.5 10.7 %collective-permute-start = (bf16[2,64,1024]{2,1,0:T(8,128)(2,1)S(1)}, bf16[2,64,1024]{2,1,0:T(8,128)(2,1)S(1)}, u32[]{:S(2)}, u32[]{:S(2)}) collective-permute-start(bf16[2,64,1024]{2,1,0:T(8,128)(2,1)S(1)} %get-tuple-element.19), channel_id=1, source_target_pairs={{0,64},{64,0},{128,192},{192,128},{1,65},{65,1},{129,193},{193,129... | collective-permute-start | bytes 786440 | tf_op jit(solution)/shard_map/ppermute | solution.py:140
  22.8 1.0 collective-permute-start.2
  23.8 1.5 collective-permute-done.4
  25.4 7.0 %collective-permute-done = bf16[2,64,1024]{2,1,0:T(8,128)(2,1)S(1)} collective-permute-done((bf16[2,64,1024]{2,1,0:T(8,128)(2,1)S(1)}, bf16[2,64,1024]{2,1,0:T(8,128)(2,1)S(1)}, u32[]{:S(2)}, u32[]{:S(2)}) %collective-permute-start) | collective-permute-done | bytes 262176 | tf_op jit(solution)/shard_map/ppermute | solution.py:140
  32.3 8.4 %collective-permute-done.1 = bf16[2,64,1024]{2,1,0:T(8,128)(2,1)S(1)} collective-permute-done((bf16[2,64,1024]{2,1,0:T(8,128)(2,1)S(1)}, bf16[2,64,1024]{2,1,0:T(8,128)(2,1)S(1)}, u32[]{:S(2)}, u32[]{:S(2)}) %collective-permute-start.1) | collective-permute-done | bytes 262176 | tf_op jit(solution)/shard_map/ppermute | solution.py:140
  40.8 5.4 %collective-permute-done.2 = bf16[2,64,1024]{2,1,0:T(8,128)(2,1)S(1)} collective-permute-done((bf16[2,64,1024]{2,1,0:T(8,128)(2,1)S(1)}, bf16[2,64,1024]{2,1,0:T(8,128)(2,1)S(1)}, u32[]{:S(2)}, u32[]{:S(2)}) %collective-permute-start.2) | collective-permute-done | bytes 262176 | tf_op jit(solution)/shard_map/ppermute | solution.py:140
  46.2 0.8 maximum_select_fusion
  47.0 1.0 dynamic-slice_bitcast_fusion.4
  48.2 1.9 %collective-permute-done.5 = bf16[4,64,1024]{2,1,0:T(8,128)(2,1)S(1)} collective-permute-done((bf16[4,64,1024]{2,1,0:T(8,128)(2,1)S(1)}, bf16[4,64,1024]{2,1,0:T(8,128)(2,1)S(1)}, u32[]{:S(2)}, u32[]{:S(2)}) %collective-permute-start.5) | collective-permute-done | bytes 524320 | tf_op jit(solution)/shard_map/ppermute | solution.py:135
  51.7 1.0 copy-done.8
  52.7 0.8 convolution_convert_fusion.1
  53.5 0.8 convolution_convert_fusion
  54.7 0.8 convolution_convert_fusion.2
  55.5 1.3 multiply_reduce_fusion
  56.8 1.4 fusion
  58.2 1.6 divide_convert_fusion
  59.8 0.8 fusion.11
  61.0 2.1 %copy.25 = bf16[2,16,8,2,1024]{4,3,2,1,0:T(2,128)(2,1)} copy(bf16[2,16,8,2,1024]{4,3,0,1,2:T(2,128)(2,1)S(1)} %bitcast.80) | data formatting | bytes 2097152 | tf_op jit(solution)/shard_map/transpose | solution.py:211
  63.1 12.6 %all-to-all-start = ((bf16[256,2,1024]{2,1,0:T(2,128)(2,1)}), bf16[256,2,1024]{2,1,0:T(2,128)(2,1)}, u32[]{:S(2)}, u32[]{:S(2)}) async-start(bf16[256,2,1024]{2,1,0:T(2,128)(2,1)} %bitcast.79), calls=%async_computation | async-start | bytes 2097152 | tf_op jit(solution)/shard_map/all_to_all | solution.py:212
  75.9 28.8 %all-to-all-done = bf16[256,2,1024]{2,1,0:T(2,128)(2,1)} async-done(((bf16[256,2,1024]{2,1,0:T(2,128)(2,1)}), bf16[256,2,1024]{2,1,0:T(2,128)(2,1)}, u32[]{:S(2)}, u32[]{:S(2)}) %all-to-all-start) | async-done | bytes 1048608 | tf_op jit(solution)/shard_map/all_to_all | solution.py:212
  104.6 1.6 copy.34
  106.7 8.4 %time_attention.1 = bf16[2,256,1024]{2,1,0:T(8,128)(2,1)S(1)} custom-call(s32[2]{0:T(128)S(1)} %copy-done.6, bf16[2,256,1024]{2,1,0:T(8,128)(2,1)S(1)} %bitcast.74, s32[256,1]{1,0:T(8,128)S(1)} %reshape.215.place_ref, s32[1,256]{1,0:T(1,128)S(1)} %reshape.208.place_row_ref, f32[1,1024]{1,0:T(1,128)S(1)} %bitcast.75, bf16[2,1024,512]{2,1,0:T(8,128)(2,1)S(1)} %copy-done.2, ...), custom_call_target="tpu_custom_call" | custom-call | flops 3221225472 | bytes 6291456 | tf_op jit(solution)/shard_map/time_attention/pallas_call | solution.py:78
  115.1 1.0 copy-done.1
  116.1 9.1 %feed_forward.1 = bf16[512,1024]{1,0:T(8,128)(2,1)} custom-call(bf16[512,1024]{1,0:T(8,128)(2,1)} %bitcast.73, f32[1,1024]{1,0:T(1,128)} %bitcast.90, bf16[2,2,1024,1024]{3,2,1,0:T(8,128)(2,1)} %bitcast.76, bf16[2,2,1024,1024]{3,2,1,0:T(8,128)(2,1)} %bitcast.77), custom_call_target="tpu_custom_call" | custom-call | flops 4294967296 | bytes 10485760 | tf_op jit(solution)/shard_map/feed_forward/pallas_call | solution.py:121
  125.1 1.3 copy.33
  126.4 37.3 %all_to_all.10 = bf16[32,2,8,1024]{3,2,1,0:T(8,128)(2,1)S(1)} all-to-all(bf16[32,2,8,1024]{3,2,1,0:T(8,128)(2,1)S(1)} %bitcast.81), channel_id=1, replica_groups=mesh['zl'=4,'c'=2,'x'=4,'y'=4,'h'=2] {'h','x','y'}, dimensions={0} | all-to-all | bytes 2097152 | tf_op jit(solution)/shard_map/all_to_all | solution.py:221
  163.7 1.1 copy.29
  164.8 1.2 reshape.213
  (45 shorter events, 4.5 us)
Async XLA Ops:
  6.5 53.2 %copy-start = (bf16[512,1024]{1,0:T(8,128)(2,1)S(1)}, bf16[512,1024]{1,0:T(8,128)(2,1)}, u32[]{:S(2)}) copy-start(bf16[512,1024]{1,0:T(8,128)(2,1)} %param.19) | copy-start | bytes 3145732
  6.5 109.5 %all-gather.2.cloned.1.call-start = ((), (), s32[]{:S(2)}) async-start(), calls=%async_computation.2 | async-start | bytes 8650752 | tf_op jit(solution)/shard_map/all_gather | solution.py:195
  8.3 0.7 collective-permute-start.3
  9.0 16.3 %collective-permute-start.4 = (bf16[2,32,1024]{2,1,0:T(8,128)(2,1)S(1)}, bf16[2,32,1024]{2,1,0:T(8,128)(2,1)S(1)}, u32[]{:S(2)}, u32[]{:S(2)}) collective-permute-start(bf16[2,32,1024]{2,1,0:T(8,128)(2,1)S(1)} %collective-permute-done.3), channel_id=1, source_target_pairs={{0,64},{192,128},{1,65},{193,129},{2,66},{194,130},{3,67},{195,131... | collective-permute-start | bytes 393224 | tf_op jit(solution)/shard_map/ppermute | solution.py:149
  11.5 20.8 %collective-permute-start = (bf16[2,64,1024]{2,1,0:T(8,128)(2,1)S(1)}, bf16[2,64,1024]{2,1,0:T(8,128)(2,1)S(1)}, u32[]{:S(2)}, u32[]{:S(2)}) collective-permute-start(bf16[2,64,1024]{2,1,0:T(8,128)(2,1)S(1)} %get-tuple-element.19), channel_id=1, source_target_pairs={{0,64},{64,0},{128,192},{192,128},{1,65},{65,1},{129,193},{193,129... | collective-permute-start | bytes 786440 | tf_op jit(solution)/shard_map/ppermute | solution.py:140
  22.3 18.5 %collective-permute-start.1 = (bf16[2,64,1024]{2,1,0:T(8,128)(2,1)S(1)}, bf16[2,64,1024]{2,1,0:T(8,128)(2,1)S(1)}, u32[]{:S(2)}, u32[]{:S(2)}) collective-permute-start(bf16[2,64,1024]{2,1,0:T(8,128)(2,1)S(1)} %get-tuple-element.18), channel_id=1, source_target_pairs={{0,128},{64,192},{128,0},{192,64},{1,129},{65,193},{129,1},{193,65... | collective-permute-start | bytes 786440 | tf_op jit(solution)/shard_map/ppermute | solution.py:140
  22.8 23.4 %collective-permute-start.2 = (bf16[2,64,1024]{2,1,0:T(8,128)(2,1)S(1)}, bf16[2,64,1024]{2,1,0:T(8,128)(2,1)S(1)}, u32[]{:S(2)}, u32[]{:S(2)}) collective-permute-start(bf16[2,64,1024]{2,1,0:T(8,128)(2,1)S(1)} %get-tuple-element.17), channel_id=1, source_target_pairs={{0,192},{64,128},{128,64},{192,0},{1,193},{65,129},{129,65},{193,1... | collective-permute-start | bytes 786440 | tf_op jit(solution)/shard_map/ppermute | solution.py:140
  48.1 2.0 %collective-permute-start.5 = (bf16[4,64,1024]{2,1,0:T(8,128)(2,1)S(1)}, bf16[4,64,1024]{2,1,0:T(8,128)(2,1)S(1)}, u32[]{:S(2)}, u32[]{:S(2)}) collective-permute-start(bf16[4,64,1024]{2,1,0:T(8,128)(2,1)S(1)} %pad_maximum_fusion.1), channel_id=1, source_target_pairs={{0,32},{32,0},{1,33},{33,1},{2,34},{34,2},{3,35},{35,3},{4,36},{36... | collective-permute-start | bytes 1572872 | tf_op jit(solution)/shard_map/ppermute | solution.py:135
  50.4 0.7 copy-start.7
  51.1 1.6 copy-start.8
  53.5 1.2 copy-start.9
  63.0 43.2 %copy-start.2 = (bf16[2,1024,512]{2,1,0:T(8,128)(2,1)S(1)}, bf16[2,1024,512]{2,1,0:T(8,128)(2,1)}, u32[]{:S(2)}) copy-start(bf16[2,1024,512]{2,1,0:T(8,128)(2,1)} %qk_ref.1) | copy-start | bytes 6291460
  63.0 43.3 %copy-start.5 = (f32[1024]{0:T(1024)S(1)}, f32[1024]{0:T(1024)}, u32[]{:S(2)}) copy-start(f32[1024]{0:T(1024)} %param.15) | copy-start | bytes 12292
  63.0 43.3 %copy-start.6 = (s32[2]{0:T(128)S(1)}, s32[2]{0:T(128)}, u32[]{:S(2)}) copy-start(s32[2]{0:T(128)} %start_ref.1) | copy-start | bytes 28
  63.1 41.6 %all-to-all-start = ((bf16[256,2,1024]{2,1,0:T(2,128)(2,1)}), bf16[256,2,1024]{2,1,0:T(2,128)(2,1)}, u32[]{:S(2)}, u32[]{:S(2)}) async-start(bf16[256,2,1024]{2,1,0:T(2,128)(2,1)} %bitcast.79), calls=%async_computation | async-start | bytes 2097152 | tf_op jit(solution)/shard_map/all_to_all | solution.py:212
  104.6 1.7 copy-start.3
  104.6 2.0 %copy-start.4 = (bf16[512,1024]{1,0:T(8,128)(2,1)S(1)}, bf16[512,1024]{1,0:T(8,128)(2,1)}, u32[]{:S(2)}) copy-start(bf16[512,1024]{1,0:T(8,128)(2,1)} %o_ref.1) | copy-start | bytes 3145732
  115.1 1.0 copy-start.1
Sparse Core Ops, SparseCore 0:
  47.1 65.0 all-gather.1

commit v5 on v4

--- a/solution.py
+++ b/solution.py
@@ -46,10 +46,10 @@
 
 
 def time_kernel(start_ref, rows_ref, place_ref, place_row_ref, gain_ref, qk_ref, v_ref, o_ref, out_ref):
-    agents, steps, width = rows_ref.shape
+    agents, steps, width = out_ref.shape
     later, earlier = place_ref[...], place_row_ref[...]
     for agent in range(agents):
-        rows = rows_ref[agent].astype(F32)
+        rows = rows_ref[:, agent].astype(F32).reshape(steps, width)
         normed = rms_block(rows, gain_ref[...])
         queries = linear(normed, qk_ref[0]).astype(BF)
         keys = linear(normed, qk_ref[1]).astype(BF)
@@ -73,11 +73,11 @@
 
 
 def time_block(series, places, starts, gain, pair, value, out):
-    agents, steps, width = series.shape
+    blocks, agents, block, width = series.shape
     vmem = pl.BlockSpec(memory_space=pltpu.VMEM)
     return pl.pallas_call(
         time_kernel,
-        out_shape=jax.ShapeDtypeStruct(series.shape, BF),
+        out_shape=jax.ShapeDtypeStruct((agents, blocks * block, width), BF),
         in_specs=[pl.BlockSpec(memory_space=pltpu.SMEM)] + [vmem] * 7,
         out_specs=vmem,
         compiler_params=pltpu.CompilerParams(vmem_limit_bytes=28 << 20),
@@ -107,10 +107,14 @@
 
     @pl.when(step == last)
     def _():
-        out_ref[...] = total[...].astype(BF)
-
-
-def ff_block(rows, gain, weights):
+        blocks, agents, block, width = out_ref.shape
+        for agent in range(agents):
+            part = total[agent * blocks * block : (agent + 1) * blocks * block]
+            out_ref[:, agent] = part.reshape(blocks, block, width).astype(BF)
+
+
+def ff_block(rows, gain, weights, shape):
+    rows = rows.reshape(-1, rows.shape[-1])
     count, width = rows.shape
     halves, half = weights.shape[1], weights.shape[3]
     size = 512
@@ -121,16 +125,65 @@
     return pl.pallas_call(
         ff_kernel,
         grid=(halves * n,),
-        out_shape=jax.ShapeDtypeStruct((count, width), BF),
+        out_shape=jax.ShapeDtypeStruct(shape, BF),
         in_specs=[whole, pl.BlockSpec((1, width), lambda i: (0, 0)), up, down],
-        out_specs=whole,
+        out_specs=pl.BlockSpec(shape, lambda i: (0, 0, 0, 0)),
         scratch_shapes=[pltpu.VMEM((count, width), BF), pltpu.VMEM((count, width), F32)],
-        compiler_params=pltpu.CompilerParams(vmem_limit_bytes=58 << 20),
+        compiler_params=pltpu.CompilerParams(vmem_limit_bytes=54 << 20),
         cost_estimate=pl.CostEstimate(flops=4 << 30, bytes_accessed=10 << 20, transcendentals=1 << 20),
         name="feed_forward",
     )(rows, gain[None, :], weights, weights)
 
 
+def pick(places, rows):
+    count = rows.shape[0]
+    spot = lax.broadcasted_iota(jnp.int32, (places.shape[0], count), 1)
+    return linear(jnp.where(spot == places, 1.0, 0.0).astype(BF), rows)
+
+
+def home_kernel(rows_place, context_place, rows_ref, own0, own1, own2, own3, got_ref, o_ref, out_ref):
+    width = rows_ref.shape[-1]
+    owns = [own0, own1, own2, own3]
+    half = own0.shape[0] // 2
+    got = got_ref[...].reshape(-1, got_ref.shape[-1])
+    context = jnp.concatenate([own[:half] for own in owns] + [got], 0)
+    residual = pick(rows_place[...], rows_ref[...].reshape(-1, width))
+    context = pick(context_place[...], context).astype(BF)
+    after = residual + linear(context, o_ref[...])
+    out_ref[...] = after.reshape(out_ref.shape).astype(BF)
+
+
+def home_block(rows_place, context_place, rows, back, got, out, shape):
+    vmem = pl.BlockSpec(memory_space=pltpu.VMEM)
+    return pl.pallas_call(
+        home_kernel,
+        out_shape=jax.ShapeDtypeStruct(shape, BF),
+        in_specs=[vmem] * 9,
+        out_specs=vmem,
+        compiler_params=pltpu.CompilerParams(vmem_limit_bytes=24 << 20),
+        cost_estimate=pl.CostEstimate(flops=1 << 30, bytes_accessed=4 << 20, transcendentals=0),
+        name="home",
+    )(rows_place[:, None], context_place[:, None], rows, *back, got, out)
+
+
+def reorder_kernel(place, rows_ref, out_ref):
+    rows = rows_ref[...].astype(F32).reshape(-1, rows_ref.shape[-1]).astype(BF)
+    out_ref[...] = pick(place[...], rows).astype(BF)
+
+
+def reorder(place, rows):
+    vmem = pl.BlockSpec(memory_space=pltpu.VMEM)
+    return pl.pallas_call(
+        reorder_kernel,
+        out_shape=jax.ShapeDtypeStruct((place.shape[0], rows.shape[-1]), BF),
+        in_specs=[vmem] * 2,
+        out_specs=vmem,
+        compiler_params=pltpu.CompilerParams(vmem_limit_bytes=16 << 20),
+        cost_estimate=pl.CostEstimate(flops=1 << 29, bytes_accessed=2 << 20, transcendentals=0),
+        name="reorder",
+    )(place[:, None], rows)
+
+
 def swap_core(block):
     return lax.ppermute(block, "c", [(0, 1), (1, 0)])
 
@@ -138,16 +191,6 @@
 def swap_z(block, k):
     n = lax.axis_size("zl")
     return lax.ppermute(block, "zl", [(i, i ^ k) for i in range(n)])
-
-
-def other_half(block, zl, high):
-    n = lax.axis_size("zl")
-    spot = lambda h, z: z * 2 + h
-    edge = [(spot(h, z), spot(1 - h, n - 1 - z)) for h in (0, 1) for z in (0, n - 1)]
-    inner = [(spot(h, z), spot(h, w)) for h in (0, 1) for z, w in ((0, 1), (n - 1, n - 2))]
-    outer = lax.ppermute(block, ("zl", "h"), edge)
-    inward = lax.ppermute(outer, ("zl", "h"), inner)
-    return jnp.where((zl == 0) | (zl == n - 1), outer, inward)
 
 
 def on_device(
@@ -166,63 +209,62 @@
     episode_start,
 ):
     steps_here, agents_here, width = rollout.shape
-    zl, core, high = lax.axis_index("zl"), lax.axis_index("c"), lax.axis_index("h")
+    zl, core = lax.axis_index("zl"), lax.axis_index("c")
     n_zl, n_core = lax.axis_size("zl"), lax.axis_size("c")
 
     half = expand_weight.shape[1] // 2
     up = lax.dynamic_slice_in_dim(expand_weight, core * half, half, 1)
     down = lax.dynamic_slice_in_dim(reduce_weight.T, core * half, half, 1)
     mine = jnp.stack([up, down])
-    other = other_half(mine, zl, high)
+    pair = lax.all_gather(mine, "h", axis=1, tiled=True)
 
     by_step = rollout.reshape(n_zl, n_core, agents_here, width)
     chunks = [lax.dynamic_index_in_dim(by_step, zl ^ k, 0, keepdims=False) for k in range(n_zl)]
     arrived = [swap_z(chunks[k], k) for k in range(1, n_zl)]
-    arrived, other = lax.optimization_barrier((arrived, other))
+    arrived, pair = lax.optimization_barrier((arrived, pair))
     chunks = chunks[:1] + arrived
     keep = jnp.stack([lax.dynamic_index_in_dim(c, core, 0, keepdims=False) for c in chunks])
     give = jnp.stack([lax.dynamic_index_in_dim(c, 1 - core, 0, keepdims=False) for c in chunks])
     got = swap_core(give)
-    both = jnp.stack([jnp.where(core == 0, keep, got), jnp.where(core == 0, got, keep)], 1)
-    rows = jnp.zeros_like(both)
-    for k in range(n_zl):
-        rows = lax.dynamic_update_index_in_dim(rows, both[k], zl ^ k, 0)
-    rows = rows.reshape(-1, width)
-
-    pair = jnp.where(
-        high == 0, jnp.concatenate([mine, other], 1), jnp.concatenate([other, mine], 1)
-    )
+    size = n_core * agents_here
+    rows = jnp.stack([keep, got], 1).reshape(n_zl * size, width)
+
     weights = lax.all_gather(pair, ("c", "x", "y"), axis=1, tiled=True)
     weights = weights.reshape(2, n_core, width, half)
 
     normed = rms_scale(rows, agent_gain)
-    queries = split_heads(linear(normed, agent_pair[0]).astype(BF))
+    queries = linear(normed, agent_pair[0]).astype(BF)
     keys = split_heads(linear(normed, agent_pair[1]).astype(BF))
     values = split_heads(linear(normed, agent_value).astype(BF))
-    context = attend(queries, keys, values)
-    after_agents = (rows.astype(F32) + linear(context, agent_out)).astype(BF)
-
-    n_grp, n_dev = n_zl * n_core, lax.axis_size(DEV)
+    back = [None] * n_zl
+    for k in reversed(range(n_zl)):
+        part = attend(split_heads(queries[k * size : (k + 1) * size]), keys, values)
+        back[k] = swap_z(part, k) if k else part
+    got = swap_core(jnp.stack([block[agents_here:] for block in back]))
+
+    n_dev, n_high = lax.axis_size(DEV), lax.axis_size("h")
+    n_flat = n_dev // n_high
     agents_own = episode_start.shape[0]
     steps = n_dev * steps_here
-    n_high = lax.axis_size("h")
-    n_flat = n_dev // n_high
-    pieces = after_agents.reshape(n_grp, n_flat, n_high, agents_own, width)
-    pieces = jnp.transpose(pieces, (2, 1, 0, 3, 4)).reshape(steps, agents_own, width)
-    series = lax.all_to_all(pieces, TURNED + GRP, split_axis=0, concat_axis=0, tiled=True)
-    series = jnp.swapaxes(series, 0, 1)
-    places = lax.iota(jnp.int32, steps).reshape(n_flat, n_high, n_grp)
+    at_home = lax.iota(jnp.int32, steps_here * agents_here)
+    turned = at_home.reshape(steps_here, n_flat, n_high, agents_own)
+    turned = jnp.transpose(turned, (2, 1, 3, 0)).reshape(-1)
+    agent, source = turned % agents_here, (turned // agents_here) ^ (zl * n_core + core)
+    in_context = ((source % n_core) * n_zl + source // n_core) * agents_here + agent
+    shape = (n_dev, agents_own, steps_here, width)
+    pieces = home_block(turned, in_context, rollout, back, got, agent_out, shape)
+
+    series = lax.all_to_all(pieces, TURNED, split_axis=0, concat_axis=0, tiled=True)
+    places = lax.iota(jnp.int32, steps).reshape(n_flat, n_high, steps_here)
     places = jnp.swapaxes(places, 0, 1).reshape(steps)
     after_time = time_block(
         series, places, episode_start, time_gain, time_pair, time_value, time_out
     )
-    result = ff_block(after_time.reshape(-1, width), inner_gain, weights)
-    result = result.reshape(agents_own, n_dev, steps_here, width)
-    result = lax.all_to_all(
-        jnp.swapaxes(result, 0, 1), TURNED, split_axis=0, concat_axis=0, tiled=True
-    )
-    result = result.reshape(n_high, n_flat, agents_own, steps_here, width)
-    return jnp.transpose(result, (3, 1, 0, 2, 4)).reshape(steps_here, agents_here, width)
+    result = ff_block(after_time, inner_gain, weights, series.shape)
+    result = lax.all_to_all(result, TURNED, split_axis=0, concat_axis=0, tiled=True)
+    back_home = at_home.reshape(n_high, n_flat, agents_own, steps_here)
+    back_home = jnp.transpose(back_home, (3, 1, 0, 2)).reshape(-1)
+    return reorder(back_home, result).reshape(steps_here, agents_here, width)
 
 
 def solution(mesh):

time: 173 us -> 182 us (1.052)
  blocking collectives: 37.3 us -> 15.4 us
  waiting for transfers between devices: 53 us -> 68 us
  local copies, waits for them, and re-layouts: 15.1 us -> 20.9 us
  Pallas kernels: 17.5 us -> 22.8 us
  other arithmetic: 3.35 us -> 6.94 us
  starting transfers between devices: 27 us -> 25.1 us
    all_to_all x1 -> x0, blocking collectives: 37.3 us -> none  [on_device(): lax.all_to_all(jnp.swapaxes(result, 0, 1), TURNED, split_axis=0, concat_a...]
    all_to_all x1 -> x2, waiting for transfers between devices: 28.8 us -> 54.7 us  [the longest x1 31.5 us: on_device(): lax.all_to_all(pieces, TURNED, split_axis=0, concat_axis=0, tiled=True)]
    all_gather x0 -> x1, blocking collectives: none -> 15.4 us  [on_device(): pair = lax.all_gather(mine, 'h', axis=1, tiled=True)]
    ppermute x3 -> x6, waiting for transfers between devices: 20.8 us -> 11.4 us  [swap_z(): return lax.ppermute(block, 'zl', [(i, i ^ k) for i in range(n)])]
    unnamed x20 -> x44, local copies, waits for them, and re-layouts: 2.97 us -> 8.77 us
    pallas_call x1 -> x3, Pallas kernels: 8.43 us -> 13.7 us  [the longest x1 8.5 us: time_block(): pl.pallas_call(time_kernel, out_shape=jax.ShapeDtypeStruct((agents, block...]
    all_to_all x1 -> x2, starting transfers between devices: 12.6 us -> 17.6 us  [the longest x1 12.8 us: on_device(): lax.all_to_all(pieces, TURNED, split_axis=0, concat_axis=0, tiled=True)]
    ppermute x3 -> x6, starting transfers between devices: 12.3 us -> 7.41 us  [swap_z(): return lax.ppermute(block, 'zl', [(i, i ^ k) for i in range(n)])]
  transfers between devices with their start and end apart: 8 -> 11, of which waited for: 6 -> 5; matrix products, arithmetic and copies ran while one was open for 9% -> 14% of each run, Pallas kernels for 5% -> 7%
where the time goes in v5:
time: 182 us; the launch traced here: 181 us
  waiting for transfers between devices  68 us (37%)
  starting transfers between devices  25.1 us (14%)
  Pallas kernels  22.8 us (13%)
  local copies, waits for them, and re-layouts  20.9 us (11%)
  blocking collectives  15.4 us (8%)
  between operations  13.8 us (8%)
  matrix products  7.67 us (4%)
  other arithmetic  6.94 us (4%)
    all_to_all x1, waiting for transfers between devices, on_device(): lax.all_to_all(pieces, TURNED, split_axis=0, concat_axis=0, tiled=True)  31.5 us
    all_to_all x1, waiting for transfers between devices, on_device(): lax.all_to_all(result, TURNED, split_axis=0, concat_axis=0, tiled=True)  23.2 us
    all_gather x1, blocking collectives, on_device(): pair = lax.all_gather(mine, 'h', axis=1, tiled=True)  15.4 us
    all_to_all x1, starting transfers between devices, on_device(): lax.all_to_all(pieces, TURNED, split_axis=0, concat_axis=0, tiled=True)  12.8 us
    ppermute x6, waiting for transfers between devices, swap_z(): return lax.ppermute(block, 'zl', [(i, i ^ k) for i in range(n)])  11.4 us
    pallas_call x1, Pallas kernels, ff_block(): pl.pallas_call(ff_kernel, grid=(halves * n,), out_shape=jax.ShapeDtypeStr...  9.08 us
    unnamed x44, local copies, waits for them, and re-layouts  8.77 us
    pallas_call x1, Pallas kernels, time_block(): pl.pallas_call(time_kernel, out_shape=jax.ShapeDtypeStruct((agents, block...  8.5 us
  transfers between devices with their start and end apart: 11, of which 5 were waited for; matrix products, arithmetic and copies ran while one was open for 14% of the time, Pallas kernels for 7%

profile of v5, /device:TPU:32, one launch (start us, length us, event | category | flops | bytes accessed | tf_op | source)
XLA Modules:
  0.0 180.6 jit_solution(14523804657327482795)
XLA Ops:
  6.5 1.3 dynamic-slice_bitcast_fusion
  7.9 1.9 %collective-permute-start = (bf16[2,64,1024]{2,1,0:T(8,128)(2,1)S(1)}, bf16[2,64,1024]{2,1,0:T(8,128)(2,1)}, u32[]{:S(2)}, u32[]{:S(2)}) collective-permute-start(bf16[2,64,1024]{2,1,0:T(8,128)(2,1)S(1)} %get-tuple-element.17), channel_id=1, source_target_pairs={{0,64},{64,0},{128,192},{192,128},{1,65},{65,1},{129,193},{193,129... | collective-permute-start | bytes 786440 | tf_op jit(solution)/shard_map/ppermute | solution.py:193
  9.8 1.5 collective-permute-start.1
  13.5 15.4 %all_gather.6 = bf16[2,64,1024]{2,1,0:T(8,128)(2,1)} all-gather(bf16[2,32,1024]{2,1,0:T(8,128)(2,1)S(1)} %pad_maximum_fusion.2), channel_id=1, replica_groups=mesh['zl'=4,'c'=2,'x'=4,'y'=4,'h'=2] {'h'}, dimensions={1}, use_global_device_ids=true | all-gather | bytes 393216 | tf_op jit(solution)/shard_map/all_gather | solution.py:219
  28.9 6.0 %collective-permute-done.1 = bf16[2,64,1024]{2,1,0:T(8,128)(2,1)S(1)} collective-permute-done((bf16[2,64,1024]{2,1,0:T(8,128)(2,1)S(1)}, bf16[2,64,1024]{2,1,0:T(8,128)(2,1)S(1)}, u32[]{:S(2)}, u32[]{:S(2)}) %collective-permute-start.1) | collective-permute-done | bytes 262176 | tf_op jit(solution)/shard_map/ppermute | solution.py:193
  34.9 5.4 %collective-permute-done.2 = bf16[2,64,1024]{2,1,0:T(8,128)(2,1)S(1)} collective-permute-done((bf16[2,64,1024]{2,1,0:T(8,128)(2,1)S(1)}, bf16[2,64,1024]{2,1,0:T(8,128)(2,1)S(1)}, u32[]{:S(2)}, u32[]{:S(2)}) %collective-permute-start.2) | collective-permute-done | bytes 262176 | tf_op jit(solution)/shard_map/ppermute | solution.py:193
  40.4 1.0 constant_dynamic-slice_fusion.5
  41.7 1.8 %collective-permute-done.3 = bf16[4,64,1024]{2,1,0:T(8,128)(2,1)S(1)} collective-permute-done((bf16[4,64,1024]{2,1,0:T(8,128)(2,1)S(1)}, bf16[4,64,1024]{2,1,0:T(8,128)(2,1)S(1)}, u32[]{:S(2)}, u32[]{:S(2)}) %collective-permute-start.3) | collective-permute-done | bytes 524320 | tf_op jit(solution)/shard_map/ppermute | solution.py:188
  44.5 1.0 copy-done.17
  50.8 1.6 collective-permute-start.6
  57.6 1.9 %collective-permute-start.4 = (bf16[128,512]{1,0:T(8,128)(2,1)}, bf16[128,512]{1,0:T(8,128)(2,1)S(1)}, u32[]{:S(2)}, u32[]{:S(2)}) collective-permute-start(bf16[128,512]{1,0:T(8,128)(2,1)} %copy.24), channel_id=1, source_target_pairs={{0,64},{64,0},{128,192},{192,128},{1,65},{65,1},{129,193},{193,129... | collective-permute-start | bytes 393224 | tf_op jit(solution)/shard_map/ppermute | solution.py:193
  60.6 1.3 fusion.14
  61.9 1.7 slice.45
  63.5 1.6 copy.32
  65.2 1.6 pad_maximum_fusion.1
  68.4 1.2 fusion.38.context_place
  69.6 1.0 copy.29.own0
  70.7 0.9 copy-done.4
  71.6 0.9 copy-done.6
  72.5 0.9 copy-done.8
  73.4 0.9 copy-done.10
  74.3 3.5 %home.1 = bf16[32,2,8,1024]{3,2,1,0:T(8,128)(2,1)} custom-call(s32[512,1]{1,0:T(8,128)S(1)} %reshape.682.rows_place, s32[512,1]{1,0:T(8,128)S(1)} %copy-done.4, bf16[8,64,1024]{2,1,0:T(8,128)(2,1)S(1)} %copy-done.1, bf16[128,512]{1,0:T(8,128)(2,1)S(1)} %copy.29.own0, bf16[128,512]{1,0:T(8,128)(2,1)S(1)} %copy-done.10, bf16[128,512]{1,0:T(8,128)(2,1)S(1)} %copy-done.8, ...), custom_call_target="tpu_custom_call" | custom-call | flops 1073741824 | bytes 4194304 | tf_op jit(solution)/shard_map/home/pallas_call | solution.py:158
  77.8 12.8 %all-to-all-start = ((bf16[32,2,8,1024]{3,2,1,0:T(8,128)(2,1)}), bf16[32,2,8,1024]{3,2,1,0:T(8,128)(2,1)S(1)}, u32[]{:S(2)}, u32[]{:S(2)}) async-start(bf16[32,2,8,1024]{3,2,1,0:T(8,128)(2,1)} %home.1), calls=%async_computation | async-start | bytes 2097152 | tf_op jit(solution)/shard_map/all_to_all | solution.py:257
  90.8 31.5 %all-to-all-done.rows_ref = bf16[32,2,8,1024]{3,2,1,0:T(8,128)(2,1)S(1)} async-done(((bf16[32,2,8,1024]{3,2,1,0:T(8,128)(2,1)}), bf16[32,2,8,1024]{3,2,1,0:T(8,128)(2,1)S(1)}, u32[]{:S(2)}, u32[]{:S(2)}) %all-to-all-start) | async-done | bytes 1048608 | tf_op jit(solution)/shard_map/all_to_all | solution.py:257
  122.3 1.6 copy-done.11
  123.9 1.2 copy-done.13
  125.1 8.5 %time_attention.1 = bf16[2,256,1024]{2,1,0:T(8,128)(2,1)S(1)} custom-call(s32[2]{0:T(128)S(1)} %copy-done.15, bf16[32,2,8,1024]{3,2,1,0:T(8,128)(2,1)S(1)} %all-to-all-done.rows_ref, s32[256,1]{1,0:T(8,128)S(1)} %reshape.681.place_ref, s32[1,256]{1,0:T(1,128)S(1)} %reshape.675.place_row_ref, f32[1,1024]{1,0:T(1,128)S(1)} %bitcast.104, ...), custom_call_target="tpu_custom_call" | custom-call | flops 3221225472 | bytes 6291456 | tf_op jit(solution)/shard_map/time_attention/pallas_call | solution.py:78
  133.7 1.0 copy-done.3
  134.6 9.1 %feed_forward.1 = bf16[32,2,8,1024]{3,2,1,0:T(8,128)(2,1)} custom-call(bf16[512,1024]{1,0:T(8,128)(2,1)} %bitcast.103, f32[1,1024]{1,0:T(1,128)} %bitcast.124, bf16[2,2,1024,1024]{3,2,1,0:T(8,128)(2,1)} %bitcast.105, bf16[2,2,1024,1024]{3,2,1,0:T(8,128)(2,1)} %bitcast.106), custom_call_target="tpu_custom_call" | custom-call | flops 4294967296 | bytes 10485760 | tf_op jit(solution)/shard_map/feed_forward/pallas_call | solution.py:125
  143.7 4.8 %all-to-all-start.1 = ((bf16[32,2,8,1024]{3,2,1,0:T(8,128)(2,1)}), bf16[32,2,8,1024]{3,2,1,0:T(8,128)(2,1)S(1)}, u32[]{:S(2)}, u32[]{:S(2)}) async-start(bf16[32,2,8,1024]{3,2,1,0:T(8,128)(2,1)} %feed_forward.1), calls=%async_computation.1 | async-start | bytes 2097152 | tf_op jit(solution)/shard_map/all_to_all | solution.py:264
  148.8 23.2 %all-to-all-done.1.rows_ref = bf16[32,2,8,1024]{3,2,1,0:T(8,128)(2,1)S(1)} async-done(((bf16[32,2,8,1024]{3,2,1,0:T(8,128)(2,1)}), bf16[32,2,8,1024]{3,2,1,0:T(8,128)(2,1)S(1)}, u32[]{:S(2)}, u32[]{:S(2)}) %all-to-all-start.1) | async-done | bytes 1048608 | tf_op jit(solution)/shard_map/all_to_all | solution.py:264
  172.0 1.7 reorder.1
  (89 shorter events, 17.0 us)
Async XLA Ops:
  6.5 42.0 %copy-start = (bf16[1024,512]{1,0:T(8,128)(2,1)S(1)}, bf16[1024,512]{1,0:T(8,128)(2,1)}, u32[]{:S(2)}) copy-start(bf16[1024,512]{1,0:T(8,128)(2,1)} %param.18) | copy-start | bytes 3145732
  6.5 33.8 %copy-start.1 = (bf16[8,64,1024]{2,1,0:T(8,128)(2,1)S(1)}, bf16[8,64,1024]{2,1,0:T(8,128)(2,1)}, u32[]{:S(2)}) copy-start(bf16[8,64,1024]{2,1,0:T(8,128)(2,1)} %rows_ref.1) | copy-start | bytes 3145732
  6.5 128.1 %all-gather.2.cloned.1.call-start = ((), (), s32[]{:S(2)}) async-start(), calls=%async_computation.2 | async-start | bytes 8650752 | tf_op jit(solution)/shard_map/all_gather | solution.py:232
  7.9 21.1 %collective-permute-start = (bf16[2,64,1024]{2,1,0:T(8,128)(2,1)S(1)}, bf16[2,64,1024]{2,1,0:T(8,128)(2,1)}, u32[]{:S(2)}, u32[]{:S(2)}) collective-permute-start(bf16[2,64,1024]{2,1,0:T(8,128)(2,1)S(1)} %get-tuple-element.17), channel_id=1, source_target_pairs={{0,64},{64,0},{128,192},{192,128},{1,65},{65,1},{129,193},{193,129... | collective-permute-start | bytes 786440 | tf_op jit(solution)/shard_map/ppermute | solution.py:193
  9.8 25.1 %collective-permute-start.1 = (bf16[2,64,1024]{2,1,0:T(8,128)(2,1)S(1)}, bf16[2,64,1024]{2,1,0:T(8,128)(2,1)S(1)}, u32[]{:S(2)}, u32[]{:S(2)}) collective-permute-start(bf16[2,64,1024]{2,1,0:T(8,128)(2,1)S(1)} %get-tuple-element.16), channel_id=1, source_target_pairs={{0,128},{64,192},{128,0},{192,64},{1,129},{65,193},{129,1},{193,65... | collective-permute-start | bytes 786440 | tf_op jit(solution)/shard_map/ppermute | solution.py:193
  11.3 29.0 %collective-permute-start.2 = (bf16[2,64,1024]{2,1,0:T(8,128)(2,1)S(1)}, bf16[2,64,1024]{2,1,0:T(8,128)(2,1)S(1)}, u32[]{:S(2)}, u32[]{:S(2)}) collective-permute-start(bf16[2,64,1024]{2,1,0:T(8,128)(2,1)S(1)} %get-tuple-element.15), channel_id=1, source_target_pairs={{0,192},{64,128},{128,64},{192,0},{1,193},{65,129},{129,65},{193,1... | collective-permute-start | bytes 786440 | tf_op jit(solution)/shard_map/ppermute | solution.py:193
  41.5 2.0 %collective-permute-start.3 = (bf16[4,64,1024]{2,1,0:T(8,128)(2,1)S(1)}, bf16[4,64,1024]{2,1,0:T(8,128)(2,1)S(1)}, u32[]{:S(2)}, u32[]{:S(2)}) collective-permute-start(bf16[4,64,1024]{2,1,0:T(8,128)(2,1)S(1)} %pad_maximum_fusion), channel_id=1, source_target_pairs={{0,32},{32,0},{1,33},{33,1},{2,34},{34,2},{3,35},{35,3},{4,36},{36... | collective-permute-start | bytes 1572872 | tf_op jit(solution)/shard_map/ppermute | solution.py:188
  43.9 1.6 copy-start.17
  49.3 0.8 copy-start.18
  50.8 14.3 %collective-permute-start.6 = (bf16[128,512]{1,0:T(8,128)(2,1)}, bf16[128,512]{1,0:T(8,128)(2,1)S(1)}, u32[]{:S(2)}, u32[]{:S(2)}) collective-permute-start(bf16[128,512]{1,0:T(8,128)(2,1)} %copy.26), channel_id=1, source_target_pairs={{0,192},{64,128},{128,64},{192,0},{1,193},{65,129},{129,65},{193,1... | collective-permute-start | bytes 393224 | tf_op jit(solution)/shard_map/ppermute | solution.py:193
  52.5 1.1 copy-start.19
  55.0 10.2 %collective-permute-start.5 = (bf16[128,512]{1,0:T(8,128)(2,1)}, bf16[128,512]{1,0:T(8,128)(2,1)S(1)}, u32[]{:S(2)}, u32[]{:S(2)}) collective-permute-start(bf16[128,512]{1,0:T(8,128)(2,1)} %copy.25), channel_id=1, source_target_pairs={{0,128},{64,192},{128,0},{192,64},{1,129},{65,193},{129,1},{193,65... | collective-permute-start | bytes 393224 | tf_op jit(solution)/shard_map/ppermute | solution.py:193
  55.0 1.1 copy-start.20
  57.6 7.6 %collective-permute-start.4 = (bf16[128,512]{1,0:T(8,128)(2,1)}, bf16[128,512]{1,0:T(8,128)(2,1)S(1)}, u32[]{:S(2)}, u32[]{:S(2)}) collective-permute-start(bf16[128,512]{1,0:T(8,128)(2,1)} %copy.24), channel_id=1, source_target_pairs={{0,64},{64,0},{128,192},{192,128},{1,65},{65,1},{129,193},{193,129... | collective-permute-start | bytes 393224 | tf_op jit(solution)/shard_map/ppermute | solution.py:193
  59.4 1.1 copy-start.21
  60.6 10.1 %copy-start.2 = (bf16[512,1024]{1,0:T(8,128)(2,1)S(1)}, bf16[512,1024]{1,0:T(8,128)(2,1)}, u32[]{:S(2)}) copy-start(bf16[512,1024]{1,0:T(8,128)(2,1)} %o_ref.2) | copy-start | bytes 3145732
  65.1 2.4 %copy-start.5 = (bf16[128,512]{1,0:T(8,128)(2,1)}, bf16[128,512]{1,0:T(8,128)(2,1)S(1)}, u32[]{:S(2)}) copy-start(bf16[128,512]{1,0:T(8,128)(2,1)S(1)} %collective-permute-done.6.own3) | copy-start | bytes 393220
  65.2 2.3 %copy-start.7 = (bf16[128,512]{1,0:T(8,128)(2,1)}, bf16[128,512]{1,0:T(8,128)(2,1)S(1)}, u32[]{:S(2)}) copy-start(bf16[128,512]{1,0:T(8,128)(2,1)S(1)} %collective-permute-done.5.own2) | copy-start | bytes 393220
  65.2 4.4 %copy-start.9 = (bf16[128,512]{1,0:T(8,128)(2,1)}, bf16[128,512]{1,0:T(8,128)(2,1)S(1)}, u32[]{:S(2)}) copy-start(bf16[128,512]{1,0:T(8,128)(2,1)S(1)} %collective-permute-done.4.own1) | copy-start | bytes 393220
  66.9 3.8 %collective-permute-start.7 = (bf16[4,64,512]{2,1,0:T(8,128)(2,1)}, bf16[4,64,512]{2,1,0:T(8,128)(2,1)}, u32[]{:S(2)}, u32[]{:S(2)}) collective-permute-start(bf16[4,64,512]{2,1,0:T(8,128)(2,1)} %pad_maximum_fusion.1), channel_id=1, source_target_pairs={{0,32},{32,0},{1,33},{33,1},{2,34},{34,2},{3,35},{35,3},{4,36},{36... | collective-permute-start | bytes 786440 | tf_op jit(solution)/shard_map/ppermute | solution.py:188
  70.7 1.0 copy-start.4
  71.6 0.9 copy-start.6
  72.5 0.9 copy-start.8
  73.4 0.9 copy-start.10
  77.8 44.5 %copy-start.12 = (bf16[1024,512]{1,0:T(8,128)(2,1)S(1)}, bf16[1024,512]{1,0:T(8,128)(2,1)}, u32[]{:S(2)}) copy-start(bf16[1024,512]{1,0:T(8,128)(2,1)} %v_ref.1) | copy-start | bytes 3145732
  77.8 44.5 %copy-start.14 = (f32[1024]{0:T(1024)S(1)}, f32[1024]{0:T(1024)}, u32[]{:S(2)}) copy-start(f32[1024]{0:T(1024)} %param.15) | copy-start | bytes 12292
  77.8 44.5 %copy-start.15 = (s32[2]{0:T(128)S(1)}, s32[2]{0:T(128)}, u32[]{:S(2)}) copy-start(s32[2]{0:T(128)} %start_ref.1) | copy-start | bytes 28
  77.8 44.5 %all-to-all-start = ((bf16[32,2,8,1024]{3,2,1,0:T(8,128)(2,1)}), bf16[32,2,8,1024]{3,2,1,0:T(8,128)(2,1)S(1)}, u32[]{:S(2)}, u32[]{:S(2)}) async-start(bf16[32,2,8,1024]{3,2,1,0:T(8,128)(2,1)} %home.1), calls=%async_computation | async-start | bytes 2097152 | tf_op jit(solution)/shard_map/all_to_all | solution.py:257
  122.3 1.6 copy-start.11
  123.9 1.2 copy-start.13
  133.6 1.0 copy-start.3
  143.7 28.3 %all-to-all-start.1 = ((bf16[32,2,8,1024]{3,2,1,0:T(8,128)(2,1)}), bf16[32,2,8,1024]{3,2,1,0:T(8,128)(2,1)S(1)}, u32[]{:S(2)}, u32[]{:S(2)}) async-start(bf16[32,2,8,1024]{3,2,1,0:T(8,128)(2,1)} %feed_forward.1), calls=%async_computation.1 | async-start | bytes 2097152 | tf_op jit(solution)/shard_map/all_to_all | solution.py:264
  (1 other events, 0.7 us)
Sparse Core Ops, SparseCore 0:
  40.5 65.2 all-gather.1

commit v6 on v4

--- a/solution.py
+++ b/solution.py
@@ -91,63 +91,75 @@
     return (0.5 * x) * (1.0 + jnp.tanh(inner))
 
 
-def ff_kernel(rows_ref, gain_ref, up_ref, down_ref, out_ref, inner, total):
-    step, last = pl.program_id(0), pl.num_programs(0) - 1
-
-    @pl.when(step == 0)
-    def _():
-        rows = rows_ref[...].astype(F32)
-        inner[...] = rms_block(rows, gain_ref[...])
-        total[...] = rows
-
-    hidden = gelu(linear(inner[...], up_ref[0, 0])).astype(BF)
-    total[...] += lax.dot_general(
-        hidden, down_ref[0, 0], (((1,), (1,)), ((), ())), preferred_element_type=F32
-    )
-
-    @pl.when(step == last)
-    def _():
-        out_ref[...] = total[...].astype(BF)
-
-
-def ff_block(rows, gain, weights):
-    count, width = rows.shape
-    halves, half = weights.shape[1], weights.shape[3]
-    size = 512
-    n = half // size
-    whole = pl.BlockSpec((count, width), lambda i: (0, 0))
-    up = pl.BlockSpec((1, 1, width, size), lambda i: (0, i // n, 0, i % n))
-    down = pl.BlockSpec((1, 1, width, size), lambda i: (1, i // n, 0, i % n))
+def ff_kernel(rows_ref, gain_ref, weights_ref, out_ref, held, arrived):
+    halves, width, half = weights_ref.shape[1:]
+    size = half // 2
+    parts = [(i, j) for i in range(halves) for j in range(half // size)]
+
+    def fetch(n, which):
+        i, j = parts[n]
+        source = weights_ref.at[which, i, :, pl.ds(j * size, size)]
+        return pltpu.make_async_copy(source, held.at[n, which], arrived.at[n, which])
+
+    for n in range(len(parts)):
+        fetch(n, 0).start()
+        fetch(n, 1).start()
+    total = rows_ref[...].astype(F32)
+    inner = rms_block(total, gain_ref[...])
+    for n in range(len(parts)):
+        fetch(n, 0).wait()
+        hidden = gelu(linear(inner, held[n, 0])).astype(BF)
+        fetch(n, 1).wait()
+        total = total + lax.dot_general(
+            hidden, held[n, 1], (((1,), (1,)), ((), ())), preferred_element_type=F32
+        )
+    blocks, agents, block, _ = out_ref.shape
+    for agent in range(agents):
+        part = total[agent * blocks * block : (agent + 1) * blocks * block]
+        out_ref[:, agent] = part.reshape(blocks, block, width).astype(BF)
+
+
+def ff_block(rows, gain, weights, shape):
+    halves, width, half = weights.shape[1:]
+    size = half // 2
+    vmem = pl.BlockSpec(memory_space=pltpu.VMEM)
     return pl.pallas_call(
         ff_kernel,
-        grid=(halves * n,),
-        out_shape=jax.ShapeDtypeStruct((count, width), BF),
-        in_specs=[whole, pl.BlockSpec((1, width), lambda i: (0, 0)), up, down],
-        out_specs=whole,
-        scratch_shapes=[pltpu.VMEM((count, width), BF), pltpu.VMEM((count, width), F32)],
-        compiler_params=pltpu.CompilerParams(vmem_limit_bytes=58 << 20),
+        out_shape=jax.ShapeDtypeStruct(shape, BF),
+        in_specs=[vmem, vmem, pl.BlockSpec(memory_space=pltpu.HBM)],
+        out_specs=vmem,
+        scratch_shapes=[
+            pltpu.VMEM((2 * halves, 2, width, size), BF),
+            pltpu.SemaphoreType.DMA((2 * halves, 2)),
+        ],
+        compiler_params=pltpu.CompilerParams(vmem_limit_bytes=53 << 20),
         cost_estimate=pl.CostEstimate(flops=4 << 30, bytes_accessed=10 << 20, transcendentals=1 << 20),
         name="feed_forward",
-    )(rows, gain[None, :], weights, weights)
-
-
-def swap_core(block):
-    return lax.ppermute(block, "c", [(0, 1), (1, 0)])
-
-
-def swap_z(block, k):
-    n = lax.axis_size("zl")
-    return lax.ppermute(block, "zl", [(i, i ^ k) for i in range(n)])
-
-
-def other_half(block, zl, high):
-    n = lax.axis_size("zl")
-    spot = lambda h, z: z * 2 + h
-    edge = [(spot(h, z), spot(1 - h, n - 1 - z)) for h in (0, 1) for z in (0, n - 1)]
-    inner = [(spot(h, z), spot(h, w)) for h in (0, 1) for z, w in ((0, 1), (n - 1, n - 2))]
-    outer = lax.ppermute(block, ("zl", "h"), edge)
-    inward = lax.ppermute(outer, ("zl", "h"), inner)
-    return jnp.where((zl == 0) | (zl == n - 1), outer, inward)
+    )(rows, gain[None, :], weights)
+
+
+def pick(places, rows):
+    count = rows.shape[0]
+    spot = lax.broadcasted_iota(jnp.int32, (places.shape[0], count), 1)
+    return linear(jnp.where(spot == places, 1.0, 0.0).astype(BF), rows)
+
+
+def reorder_kernel(place, rows_ref, out_ref):
+    rows = rows_ref[...].astype(F32).reshape(-1, rows_ref.shape[-1]).astype(BF)
+    out_ref[...] = pick(place[...], rows).astype(BF)
+
+
+def reorder(place, rows):
+    vmem = pl.BlockSpec(memory_space=pltpu.VMEM)
+    return pl.pallas_call(
+        reorder_kernel,
+        out_shape=jax.ShapeDtypeStruct((place.shape[0], rows.shape[-1]), BF),
+        in_specs=[vmem] * 2,
+        out_specs=vmem,
+        compiler_params=pltpu.CompilerParams(vmem_limit_bytes=16 << 20),
+        cost_estimate=pl.CostEstimate(flops=1 << 29, bytes_accessed=2 << 20, transcendentals=0),
+        name="reorder",
+    )(place[:, None], rows)
 
 
 def on_device(
@@ -166,28 +178,19 @@
     episode_start,
 ):
     steps_here, agents_here, width = rollout.shape
-    zl, core, high = lax.axis_index("zl"), lax.axis_index("c"), lax.axis_index("h")
-    n_zl, n_core = lax.axis_size("zl"), lax.axis_size("c")
+    core, high = lax.axis_index("c"), lax.axis_index("h")
+    n_grp, n_core = lax.axis_size(GRP), lax.axis_size("c")
 
     half = expand_weight.shape[1] // 2
     up = lax.dynamic_slice_in_dim(expand_weight, core * half, half, 1)
     down = lax.dynamic_slice_in_dim(reduce_weight.T, core * half, half, 1)
     mine = jnp.stack([up, down])
-    other = other_half(mine, zl, high)
-
-    by_step = rollout.reshape(n_zl, n_core, agents_here, width)
-    chunks = [lax.dynamic_index_in_dim(by_step, zl ^ k, 0, keepdims=False) for k in range(n_zl)]
-    arrived = [swap_z(chunks[k], k) for k in range(1, n_zl)]
-    arrived, other = lax.optimization_barrier((arrived, other))
-    chunks = chunks[:1] + arrived
-    keep = jnp.stack([lax.dynamic_index_in_dim(c, core, 0, keepdims=False) for c in chunks])
-    give = jnp.stack([lax.dynamic_index_in_dim(c, 1 - core, 0, keepdims=False) for c in chunks])
-    got = swap_core(give)
-    both = jnp.stack([jnp.where(core == 0, keep, got), jnp.where(core == 0, got, keep)], 1)
-    rows = jnp.zeros_like(both)
-    for k in range(n_zl):
-        rows = lax.dynamic_update_index_in_dim(rows, both[k], zl ^ k, 0)
-    rows = rows.reshape(-1, width)
+    rollout, mine = lax.optimization_barrier((rollout, mine))
+    other = lax.ppermute(mine, "h", [(0, 1), (1, 0)])
+
+    rows = lax.all_to_all(rollout, GRP, split_axis=0, concat_axis=0, tiled=True)
+    rows = rows.reshape(n_grp * agents_here, width)
+    rows, other = lax.optimization_barrier((rows, other))
 
     pair = jnp.where(
         high == 0, jnp.concatenate([mine, other], 1), jnp.concatenate([other, mine], 1)
@@ -202,7 +205,7 @@
     context = attend(queries, keys, values)
     after_agents = (rows.astype(F32) + linear(context, agent_out)).astype(BF)
 
-    n_grp, n_dev = n_zl * n_core, lax.axis_size(DEV)
+    n_dev = lax.axis_size(DEV)
     agents_own = episode_start.shape[0]
     steps = n_dev * steps_here
     n_high = lax.axis_size("h")
@@ -216,13 +219,13 @@
     after_time = time_block(
         series, places, episode_start, time_gain, time_pair, time_value, time_out
     )
-    result = ff_block(after_time.reshape(-1, width), inner_gain, weights)
-    result = result.reshape(agents_own, n_dev, steps_here, width)
-    result = lax.all_to_all(
-        jnp.swapaxes(result, 0, 1), TURNED, split_axis=0, concat_axis=0, tiled=True
-    )
-    result = result.reshape(n_high, n_flat, agents_own, steps_here, width)
-    return jnp.transpose(result, (3, 1, 0, 2, 4)).reshape(steps_here, agents_here, width)
+    shape = (n_dev, agents_own, steps_here, width)
+    result = ff_block(after_time.reshape(-1, width), inner_gain, weights, shape)
+    result = lax.all_to_all(result, TURNED, split_axis=0, concat_axis=0, tiled=True)
+    order = lax.iota(jnp.int32, steps_here * agents_here)
+    order = order.reshape(n_high, n_flat, agents_own, steps_here)
+    order = jnp.transpose(order, (3, 1, 0, 2)).reshape(-1)
+    return reorder(order, result).reshape(steps_here, agents_here, width)
 
 
 def solution(mesh):

time: 173 us -> 171 us (0.988)
  blocking collectives: 37.3 us -> 0 us
  waiting for transfers between devices: 53 us -> 84 us
  starting transfers between devices: 27 us -> 34.9 us
  local copies, waits for them, and re-layouts: 15.1 us -> 8 us
  Pallas kernels: 17.5 us -> 20.3 us
    all_to_all x0 -> x2, waiting for transfers between devices: none -> 40.9 us  [the longest x1 31.2 us: on_device(): lax.all_to_all(result, TURNED, split_axis=0, concat_axis=0, tiled=True)]
    all_to_all x1 -> x0, blocking collectives: 37.3 us -> none  [on_device(): lax.all_to_all(jnp.swapaxes(result, 0, 1), TURNED, split_axis=0, concat_a...]
    all_to_all x0 -> x2, starting transfers between devices: none -> 13.8 us  [the longest x1 7.74 us: on_device(): lax.all_to_all(result, TURNED, split_axis=0, concat_axis=0, tiled=True)]
    ppermute x6 -> x1, waiting for transfers between devices: 24.2 us -> 14.3 us  [on_device(): other = lax.ppermute(mine, 'h', [(0, 1), (1, 0)])]
    ppermute x6 -> x1, starting transfers between devices: 14.4 us -> 4.76 us  [on_device(): other = lax.ppermute(mine, 'h', [(0, 1), (1, 0)])]
    all_to_all x1, starting transfers between devices: 12.6 us -> 16.3 us  [on_device(): lax.all_to_all(pieces, TURNED + GRP, split_axis=0, concat_axis=0, tiled=T...]
    pallas_call x1 -> x2, Pallas kernels: 9.07 us -> 11.9 us  [the longest x1 10.2 us: ff_block(): pl.pallas_call(ff_kernel, out_shape=jax.ShapeDtypeStruct(shape, BF), in_s...]
    reshape x2 -> x1, local copies, waits for them, and re-layouts: 2.53 us -> 0.19 us  [on_device(): order = order.reshape(n_high, n_flat, agents_own, steps_here)]
  transfers between devices with their start and end apart: 8 -> 5, of which waited for: 6 -> 4; matrix products, arithmetic and copies ran while one was open for 9% -> 8% of each run, Pallas kernels for 5% -> 5%
where the time goes in v6:
time: 171 us
  waiting for transfers between devices  84 us (49%)
  starting transfers between devices  34.9 us (20%)
  Pallas kernels  20.3 us (12%)
  between operations  13.6 us (8%)
  local copies, waits for them, and re-layouts  8 us (5%)
  matrix products  7.54 us (4%)
  other arithmetic  2.5 us (1%)
    all_to_all x1, waiting for transfers between devices, on_device(): lax.all_to_all(result, TURNED, split_axis=0, concat_axis=0, tiled=True)  31.2 us
    all_to_all x1, waiting for transfers between devices, on_device(): lax.all_to_all(pieces, TURNED + GRP, split_axis=0, concat_axis=0, tiled=T...  28.8 us
    all_to_all x1, starting transfers between devices, on_device(): lax.all_to_all(pieces, TURNED + GRP, split_axis=0, concat_axis=0, tiled=T...  16.3 us
    ppermute x1, waiting for transfers between devices, on_device(): other = lax.ppermute(mine, 'h', [(0, 1), (1, 0)])  14.3 us
    pallas_call x1, Pallas kernels, ff_block(): pl.pallas_call(ff_kernel, out_shape=jax.ShapeDtypeStruct(shape, BF), in_s...  10.2 us
    all_to_all x1, waiting for transfers between devices, on_device(): rows = lax.all_to_all(rollout, GRP, split_axis=0, concat_axis=0, tiled=True)  9.7 us
    pallas_call x1, Pallas kernels, time_block(): pl.pallas_call(time_kernel, out_shape=jax.ShapeDtypeStruct(series.shape,...  8.43 us
    all_to_all x1, starting transfers between devices, on_device(): lax.all_to_all(result, TURNED, split_axis=0, concat_axis=0, tiled=True)  7.74 us
  transfers between devices with their start and end apart: 5, of which 4 were waited for; matrix products, arithmetic and copies ran while one was open for 8% of the time, Pallas kernels for 5%

profile of v6, /device:TPU:32, one launch (start us, length us, event | category | flops | bytes accessed | tf_op | source)
XLA Modules:
  0.0 170.8 jit_solution(5410338144027176146)
XLA Ops:
  6.5 0.9 dynamic-slice_bitcast_fusion
  7.5 0.8 dynamic-slice_bitcast_fusion.1
  8.3 6.0 %all-to-all-start = ((bf16[8,64,1024]{2,1,0:T(8,128)(2,1)}), bf16[8,64,1024]{2,1,0:T(8,128)(2,1)S(1)}, u32[]{:S(2)}, u32[]{:S(2)}) async-start(bf16[8,64,1024]{2,1,0:T(8,128)(2,1)} %param.13), calls=%async_computation | async-start | bytes 2097152 | tf_op jit(solution)/shard_map/all_to_all | solution.py:191
  14.4 4.8 %collective-permute-start = (bf16[2,32,1024]{2,1,0:T(8,128)(2,1)S(1)}, bf16[2,32,1024]{2,1,0:T(8,128)(2,1)S(1)}, u32[]{:S(2)}, u32[]{:S(2)}) collective-permute-start(bf16[2,32,1024]{2,1,0:T(8,128)(2,1)S(1)} %pad_maximum_fusion), channel_id=1, source_target_pairs={{0,1},{1,0},{2,3},{3,2},{4,5},{5,4},{6,7},{7,6},{8,9},{9,8},{10,11... | collective-permute-start | bytes 393224 | tf_op jit(solution)/shard_map/ppermute | solution.py:189
  19.1 14.3 %collective-permute-done = bf16[2,32,1024]{2,1,0:T(8,128)(2,1)S(1)} collective-permute-done((bf16[2,32,1024]{2,1,0:T(8,128)(2,1)S(1)}, bf16[2,32,1024]{2,1,0:T(8,128)(2,1)S(1)}, u32[]{:S(2)}, u32[]{:S(2)}) %collective-permute-start) | collective-permute-done | bytes 131104 | tf_op jit(solution)/shard_map/ppermute | solution.py:189
  33.4 9.7 %all-to-all-done = bf16[8,64,1024]{2,1,0:T(8,128)(2,1)S(1)} async-done(((bf16[8,64,1024]{2,1,0:T(8,128)(2,1)}), bf16[8,64,1024]{2,1,0:T(8,128)(2,1)S(1)}, u32[]{:S(2)}, u32[]{:S(2)}) %all-to-all-start) | async-done | bytes 1048608 | tf_op jit(solution)/shard_map/all_to_all | solution.py:191
  43.1 0.8 maximum_select_fusion
  43.9 0.0 all-gather.2.cloned.1.call-update
  43.9 0.3 fusion.6
  44.2 2.2 %convolution_convert_fusion = bf16[512,512]{0,1:T(8,128)(2,1)S(1)} fusion(bf16[2,1024,512]{2,1,0:T(8,128)(2,1)} %param.17, bf16[512,1024]{1,0:T(8,128)(2,1)S(1)} %bitcast.43, f32[1024]{0:T(1024)S(1)} %copy-done.10, f32[512]{0:T(512)S(1)} %add_rsqrt_fusion), kind=kOutput, calls=%fused_computation.15 | convolution fusion | flops 539230208 | bytes 2627584 | tf_op jit(solution)/shard_map/dot_general | solution.py:23
  46.4 0.8 convolution_convert_fusion.1
  47.3 0.4 copy-done.9
  47.7 0.8 convolution_convert_fusion.2
  48.5 1.3 multiply_reduce_fusion
  49.8 1.4 fusion
  51.2 1.6 divide_convert_fusion
  52.8 0.8 fusion.9
  53.5 0.4 reshape.253
  54.0 2.1 %copy.21 = bf16[2,16,8,2,1024]{4,3,2,1,0:T(2,128)(2,1)} copy(bf16[2,16,8,2,1024]{4,3,0,1,2:T(2,128)(2,1)S(1)} %bitcast.48) | data formatting | bytes 2097152 | tf_op jit(solution)/shard_map/transpose | solution.py:214
  56.1 16.3 %all-to-all-start.1 = ((bf16[256,2,1024]{2,1,0:T(2,128)(2,1)}), bf16[256,2,1024]{2,1,0:T(2,128)(2,1)}, u32[]{:S(2)}, u32[]{:S(2)}) async-start(bf16[256,2,1024]{2,1,0:T(2,128)(2,1)} %bitcast.47), calls=%async_computation.1 | async-start | bytes 2097152 | tf_op jit(solution)/shard_map/all_to_all | solution.py:215
  72.5 0.1 reshape.267.place_ref
  72.6 0.1 reshape.262.place_row_ref
  72.6 28.8 %all-to-all-done.1 = bf16[256,2,1024]{2,1,0:T(2,128)(2,1)} async-done(((bf16[256,2,1024]{2,1,0:T(2,128)(2,1)}), bf16[256,2,1024]{2,1,0:T(2,128)(2,1)}, u32[]{:S(2)}, u32[]{:S(2)}) %all-to-all-start.1) | async-done | bytes 1048608 | tf_op jit(solution)/shard_map/all_to_all | solution.py:215
  101.4 1.6 copy.27
  103.1 0.3 copy-done.3
  103.4 8.4 %time_attention.1 = bf16[2,256,1024]{2,1,0:T(8,128)(2,1)S(1)} custom-call(s32[2]{0:T(128)S(1)} %copy-done.6, bf16[2,256,1024]{2,1,0:T(8,128)(2,1)S(1)} %bitcast.38, s32[256,1]{1,0:T(8,128)S(1)} %reshape.267.place_ref, s32[1,256]{1,0:T(1,128)S(1)} %reshape.262.place_row_ref, f32[1,1024]{1,0:T(1,128)S(1)} %bitcast.39, bf16[2,1024,512]{2,1,0:T(8,128)(2,1)S(1)} %copy-done.1, ...), custom_call_target="tpu_custom_call" | custom-call | flops 3221225472 | bytes 6291456 | tf_op jit(solution)/shard_map/time_attention/pallas_call | solution.py:78
  111.9 1.0 copy-done.7
  112.8 10.2 %feed_forward.1 = bf16[32,2,8,1024]{3,2,1,0:T(8,128)(2,1)} custom-call(bf16[512,1024]{1,0:T(8,128)(2,1)} %bitcast.41, f32[1,1024]{1,0:T(1,128)S(1)} %bitcast.40, bf16[2,2,1024,1024]{3,2,1,0:T(8,128)(2,1)} %bitcast.52), custom_call_target="tpu_custom_call" | custom-call | flops 4294967296 | bytes 10485760 | tf_op jit(solution)/shard_map/feed_forward/pallas_call | solution.py:126
  123.0 7.7 %all-to-all-start.2 = ((bf16[32,2,8,1024]{3,2,1,0:T(8,128)(2,1)}), bf16[32,2,8,1024]{3,2,1,0:T(8,128)(2,1)S(1)}, u32[]{:S(2)}, u32[]{:S(2)}) async-start(bf16[32,2,8,1024]{3,2,1,0:T(8,128)(2,1)} %feed_forward.1), calls=%async_computation.2 | async-start | bytes 2097152 | tf_op jit(solution)/shard_map/all_to_all | solution.py:224
  130.8 0.2 reshape.266.place
  131.0 31.2 %all-to-all-done.2.rows_ref = bf16[32,2,8,1024]{3,2,1,0:T(8,128)(2,1)S(1)} async-done(((bf16[32,2,8,1024]{3,2,1,0:T(8,128)(2,1)}), bf16[32,2,8,1024]{3,2,1,0:T(8,128)(2,1)S(1)}, u32[]{:S(2)}, u32[]{:S(2)}) %all-to-all-start.2) | async-done | bytes 1048608 | tf_op jit(solution)/shard_map/all_to_all | solution.py:224
  162.2 1.7 %reorder.1 = bf16[512,1024]{1,0:T(8,128)(2,1)} custom-call(s32[512,1]{1,0:T(8,128)S(1)} %reshape.266.place, bf16[32,2,8,1024]{3,2,1,0:T(8,128)(2,1)S(1)} %all-to-all-done.2.rows_ref), custom_call_target="tpu_custom_call" | custom-call | flops 536870912 | bytes 2097152 | tf_op jit(solution)/shard_map/reorder/pallas_call | solution.py:154
  (25 shorter events, 0.1 us)
Async XLA Ops:
  6.5 46.3 %copy-start = (bf16[512,1024]{1,0:T(8,128)(2,1)S(1)}, bf16[512,1024]{1,0:T(8,128)(2,1)}, u32[]{:S(2)}) copy-start(bf16[512,1024]{1,0:T(8,128)(2,1)} %param.19) | copy-start | bytes 3145732
  8.3 35.9 %copy-start.10 = (f32[1024]{0:T(1024)S(1)}, f32[1024]{0:T(1024)}, u32[]{:S(2)}) copy-start(f32[1024]{0:T(1024)} %param.14) | copy-start | bytes 12292
  8.3 34.8 %all-to-all-start = ((bf16[8,64,1024]{2,1,0:T(8,128)(2,1)}), bf16[8,64,1024]{2,1,0:T(8,128)(2,1)S(1)}, u32[]{:S(2)}, u32[]{:S(2)}) async-start(bf16[8,64,1024]{2,1,0:T(8,128)(2,1)} %param.13), calls=%async_computation | async-start | bytes 2097152 | tf_op jit(solution)/shard_map/all_to_all | solution.py:191
  14.4 98.5 %all-gather.2.cloned.1.call-start = ((), (), s32[]{:S(2)}) async-start(), calls=%async_computation.3 | async-start | bytes 8650752 | tf_op jit(solution)/shard_map/all_gather | solution.py:198
  14.4 19.0 %collective-permute-start = (bf16[2,32,1024]{2,1,0:T(8,128)(2,1)S(1)}, bf16[2,32,1024]{2,1,0:T(8,128)(2,1)S(1)}, u32[]{:S(2)}, u32[]{:S(2)}) collective-permute-start(bf16[2,32,1024]{2,1,0:T(8,128)(2,1)S(1)} %pad_maximum_fusion), channel_id=1, source_target_pairs={{0,1},{1,0},{2,3},{3,2},{4,5},{5,4},{6,7},{7,6},{8,9},{9,8},{10,11... | collective-permute-start | bytes 393224 | tf_op jit(solution)/shard_map/ppermute | solution.py:189
  44.2 2.2 %copy-start.8 = (bf16[2,1024,512]{2,1,0:T(8,128)(2,1)S(1)}, bf16[2,1024,512]{2,1,0:T(8,128)(2,1)}, u32[]{:S(2)}) copy-start(bf16[2,1024,512]{2,1,0:T(8,128)(2,1)} %param.17) | copy-start | bytes 6291460
  46.4 1.2 copy-start.9
  56.1 47.0 %copy-start.1 = (bf16[2,1024,512]{2,1,0:T(8,128)(2,1)S(1)}, bf16[2,1024,512]{2,1,0:T(8,128)(2,1)}, u32[]{:S(2)}) copy-start(bf16[2,1024,512]{2,1,0:T(8,128)(2,1)} %qk_ref.1) | copy-start | bytes 6291460
  56.1 47.0 %copy-start.4 = (f32[1024]{0:T(1024)S(1)}, f32[1024]{0:T(1024)}, u32[]{:S(2)}) copy-start(f32[1024]{0:T(1024)} %param.15) | copy-start | bytes 12292
  56.1 47.0 %copy-start.6 = (s32[2]{0:T(128)S(1)}, s32[2]{0:T(128)}, u32[]{:S(2)}) copy-start(s32[2]{0:T(128)} %start_ref.1) | copy-start | bytes 28
  56.1 45.3 %all-to-all-start.1 = ((bf16[256,2,1024]{2,1,0:T(2,128)(2,1)}), bf16[256,2,1024]{2,1,0:T(2,128)(2,1)}, u32[]{:S(2)}, u32[]{:S(2)}) async-start(bf16[256,2,1024]{2,1,0:T(2,128)(2,1)} %bitcast.47), calls=%async_computation.1 | async-start | bytes 2097152 | tf_op jit(solution)/shard_map/all_to_all | solution.py:215
  101.4 1.7 copy-start.2
  101.4 2.0 %copy-start.3 = (bf16[512,1024]{1,0:T(8,128)(2,1)S(1)}, bf16[512,1024]{1,0:T(8,128)(2,1)}, u32[]{:S(2)}) copy-start(bf16[512,1024]{1,0:T(8,128)(2,1)} %o_ref.1) | copy-start | bytes 3145732
  103.4 9.4 %copy-start.5 = (f32[1024]{0:T(1024)S(1)}, f32[1024]{0:T(1024)}, u32[]{:S(2)}) copy-start(f32[1024]{0:T(1024)} %param.16) | copy-start | bytes 12292
  111.9 1.0 copy-start.7
  123.0 39.2 %all-to-all-start.2 = ((bf16[32,2,8,1024]{3,2,1,0:T(8,128)(2,1)}), bf16[32,2,8,1024]{3,2,1,0:T(8,128)(2,1)S(1)}, u32[]{:S(2)}, u32[]{:S(2)}) async-start(bf16[32,2,8,1024]{3,2,1,0:T(8,128)(2,1)} %feed_forward.1), calls=%async_computation.2 | async-start | bytes 2097152 | tf_op jit(solution)/shard_map/all_to_all | solution.py:224
Sparse Core Ops, SparseCore 0:
  44.0 67.8 all-gather.1

commit v7 on v4

--- a/solution.py
+++ b/solution.py
@@ -1,3 +1,5 @@
+import functools
+
 import jax
 import jax.numpy as jnp
 from jax import lax
@@ -45,9 +47,16 @@
     return (rows * inverse * gain).astype(BF)
 
 
-def time_kernel(start_ref, rows_ref, place_ref, place_row_ref, gain_ref, qk_ref, v_ref, o_ref, out_ref):
+def step_of(row, n_flat, n_high, block):
+    low, flat = row & (block - 1), (row >> (block.bit_length() - 1)) & (n_flat - 1)
+    high = row >> ((block * n_flat).bit_length() - 1)
+    return (flat * n_high + high) * block + low
+
+
+def time_kernel(sizes, start_ref, rows_ref, gain_ref, qk_ref, v_ref, o_ref, out_ref):
     agents, steps, width = rows_ref.shape
-    later, earlier = place_ref[...], place_row_ref[...]
+    later = step_of(lax.broadcasted_iota(jnp.int32, (steps, 1), 0), *sizes)
+    earlier = step_of(lax.broadcasted_iota(jnp.int32, (1, steps), 1), *sizes)
     for agent in range(agents):
         rows = rows_ref[agent].astype(F32)
         normed = rms_block(rows, gain_ref[...])
@@ -72,18 +81,18 @@
         out_ref[agent] = (rows + linear(context, o_ref[...])).astype(BF)
 
 
-def time_block(series, places, starts, gain, pair, value, out):
+def time_block(series, sizes, starts, gain, pair, value, out):
     agents, steps, width = series.shape
     vmem = pl.BlockSpec(memory_space=pltpu.VMEM)
     return pl.pallas_call(
-        time_kernel,
+        functools.partial(time_kernel, sizes),
         out_shape=jax.ShapeDtypeStruct(series.shape, BF),
-        in_specs=[pl.BlockSpec(memory_space=pltpu.SMEM)] + [vmem] * 7,
+        in_specs=[pl.BlockSpec(memory_space=pltpu.SMEM)] + [vmem] * 5,
         out_specs=vmem,
         compiler_params=pltpu.CompilerParams(vmem_limit_bytes=28 << 20),
         cost_estimate=pl.CostEstimate(flops=3 << 30, bytes_accessed=6 << 20, transcendentals=1 << 20),
         name="time_attention",
-    )(starts, series, places[:, None], places[None, :], gain[None, :], pair, value, out)
+    )(starts, series, gain[None, :], pair, value, out)
 
 
 def gelu(x):
@@ -107,10 +116,14 @@
 
     @pl.when(step == last)
     def _():
-        out_ref[...] = total[...].astype(BF)
-
-
-def ff_block(rows, gain, weights):
+        blocks, agents, block, width = out_ref.shape
+        for agent in range(agents):
+            part = total[agent * blocks * block : (agent + 1) * blocks * block]
+            out_ref[:, agent] = part.reshape(blocks, block, width).astype(BF)
+
+
+def ff_block(rows, gain, weights, shape):
+    rows = rows.reshape(-1, rows.shape[-1])
     count, width = rows.shape
     halves, half = weights.shape[1], weights.shape[3]
     size = 512
@@ -121,23 +134,45 @@
     return pl.pallas_call(
         ff_kernel,
         grid=(halves * n,),
-        out_shape=jax.ShapeDtypeStruct((count, width), BF),
+        out_shape=jax.ShapeDtypeStruct(shape, BF),
         in_specs=[whole, pl.BlockSpec((1, width), lambda i: (0, 0)), up, down],
-        out_specs=whole,
+        out_specs=pl.BlockSpec(shape, lambda i: (0, 0, 0, 0)),
         scratch_shapes=[pltpu.VMEM((count, width), BF), pltpu.VMEM((count, width), F32)],
-        compiler_params=pltpu.CompilerParams(vmem_limit_bytes=58 << 20),
+        compiler_params=pltpu.CompilerParams(vmem_limit_bytes=28 << 20),
         cost_estimate=pl.CostEstimate(flops=4 << 30, bytes_accessed=10 << 20, transcendentals=1 << 20),
         name="feed_forward",
     )(rows, gain[None, :], weights, weights)
 
 
-def swap_core(block):
-    return lax.ppermute(block, "c", [(0, 1), (1, 0)])
-
-
-def swap_z(block, k):
-    n = lax.axis_size("zl")
-    return lax.ppermute(block, "zl", [(i, i ^ k) for i in range(n)])
+def pick(places, rows):
+    count = rows.shape[0]
+    spot = lax.broadcasted_iota(jnp.int32, (places.shape[0], count), 1)
+    return linear(jnp.where(spot == places, 1.0, 0.0).astype(BF), rows)
+
+
+def reorder_kernel(sizes, rows_ref, out_ref):
+    n_flat, n_high, own, steps = sizes
+    to = lax.broadcasted_iota(jnp.int32, (rows_ref.size // rows_ref.shape[-1], 1), 0)
+    bits = lambda n: n.bit_length() - 1
+    agent, to = to & (own - 1), to >> bits(own)
+    high, to = to & (n_high - 1), to >> bits(n_high)
+    flat, step = to & (n_flat - 1), to >> bits(n_flat)
+    place = ((high * n_flat + flat) * own + agent) * steps + step
+    rows = rows_ref[...].astype(F32).reshape(-1, rows_ref.shape[-1]).astype(BF)
+    out_ref[...] = pick(place, rows).reshape(out_ref.shape).astype(BF)
+
+
+def reorder(sizes, rows, shape):
+    vmem = pl.BlockSpec(memory_space=pltpu.VMEM)
+    return pl.pallas_call(
+        functools.partial(reorder_kernel, sizes),
+        out_shape=jax.ShapeDtypeStruct(shape, BF),
+        in_specs=[vmem],
+        out_specs=vmem,
+        compiler_params=pltpu.CompilerParams(vmem_limit_bytes=16 << 20),
+        cost_estimate=pl.CostEstimate(flops=1 << 29, bytes_accessed=2 << 20, transcendentals=0),
+        name="reorder",
+    )(rows)
 
 
 def other_half(block, zl, high):
@@ -167,7 +202,7 @@
 ):
     steps_here, agents_here, width = rollout.shape
     zl, core, high = lax.axis_index("zl"), lax.axis_index("c"), lax.axis_index("h")
-    n_zl, n_core = lax.axis_size("zl"), lax.axis_size("c")
+    n_grp, n_core = lax.axis_size(GRP), lax.axis_size("c")
 
     half = expand_weight.shape[1] // 2
     up = lax.dynamic_slice_in_dim(expand_weight, core * half, half, 1)
@@ -175,26 +210,20 @@
     mine = jnp.stack([up, down])
     other = other_half(mine, zl, high)
 
-    by_step = rollout.reshape(n_zl, n_core, agents_here, width)
-    chunks = [lax.dynamic_index_in_dim(by_step, zl ^ k, 0, keepdims=False) for k in range(n_zl)]
-    arrived = [swap_z(chunks[k], k) for k in range(1, n_zl)]
-    arrived, other = lax.optimization_barrier((arrived, other))
-    chunks = chunks[:1] + arrived
-    keep = jnp.stack([lax.dynamic_index_in_dim(c, core, 0, keepdims=False) for c in chunks])
-    give = jnp.stack([lax.dynamic_index_in_dim(c, 1 - core, 0, keepdims=False) for c in chunks])
-    got = swap_core(give)
-    both = jnp.stack([jnp.where(core == 0, keep, got), jnp.where(core == 0, got, keep)], 1)
-    rows = jnp.zeros_like(both)
-    for k in range(n_zl):
-        rows = lax.dynamic_update_index_in_dim(rows, both[k], zl ^ k, 0)
-    rows = rows.reshape(-1, width)
-
+    rows = lax.all_to_all(rollout, GRP, split_axis=0, concat_axis=0, tiled=True)
+    rows = rows.reshape(n_grp * agents_here, width)
     pair = jnp.where(
         high == 0, jnp.concatenate([mine, other], 1), jnp.concatenate([other, mine], 1)
     )
+    rows, pair = lax.optimization_barrier((rows, pair))
     weights = lax.all_gather(pair, ("c", "x", "y"), axis=1, tiled=True)
     weights = weights.reshape(2, n_core, width, half)
 
+    n_dev = lax.axis_size(DEV)
+    agents_own = episode_start.shape[0]
+    steps = n_dev * steps_here
+    n_high = lax.axis_size("h")
+    n_flat = n_dev // n_high
     normed = rms_scale(rows, agent_gain)
     queries = split_heads(linear(normed, agent_pair[0]).astype(BF))
     keys = split_heads(linear(normed, agent_pair[1]).astype(BF))
@@ -202,27 +231,18 @@
     context = attend(queries, keys, values)
     after_agents = (rows.astype(F32) + linear(context, agent_out)).astype(BF)
 
-    n_grp, n_dev = n_zl * n_core, lax.axis_size(DEV)
-    agents_own = episode_start.shape[0]
-    steps = n_dev * steps_here
-    n_high = lax.axis_size("h")
-    n_flat = n_dev // n_high
     pieces = after_agents.reshape(n_grp, n_flat, n_high, agents_own, width)
     pieces = jnp.transpose(pieces, (2, 1, 0, 3, 4)).reshape(steps, agents_own, width)
     series = lax.all_to_all(pieces, TURNED + GRP, split_axis=0, concat_axis=0, tiled=True)
     series = jnp.swapaxes(series, 0, 1)
-    places = lax.iota(jnp.int32, steps).reshape(n_flat, n_high, n_grp)
-    places = jnp.swapaxes(places, 0, 1).reshape(steps)
+    sizes = (n_flat, n_high, steps_here)
     after_time = time_block(
-        series, places, episode_start, time_gain, time_pair, time_value, time_out
-    )
-    result = ff_block(after_time.reshape(-1, width), inner_gain, weights)
-    result = result.reshape(agents_own, n_dev, steps_here, width)
-    result = lax.all_to_all(
-        jnp.swapaxes(result, 0, 1), TURNED, split_axis=0, concat_axis=0, tiled=True
-    )
-    result = result.reshape(n_high, n_flat, agents_own, steps_here, width)
-    return jnp.transpose(result, (3, 1, 0, 2, 4)).reshape(steps_here, agents_here, width)
+        series, sizes, episode_start, time_gain, time_pair, time_value, time_out
+    )
+    shape = (n_dev, agents_own, steps_here, width)
+    result = ff_block(after_time, inner_gain, weights, shape)
+    result = lax.all_to_all(result, TURNED, split_axis=0, concat_axis=0, tiled=True)
+    return reorder((n_flat, n_high, agents_own, steps_here), result, rollout.shape)
 
 
 def solution(mesh):

time: 173 us -> 162 us (0.936)
  blocking collectives: 37.3 us -> 84.9 us
  waiting for transfers between devices: 53 us -> 23 us
  starting transfers between devices: 27 us -> 8.11 us
  local copies, waits for them, and re-layouts: 15.1 us -> 5.62 us
    all_to_all x1 -> x2, blocking collectives: 37.3 us -> 84.9 us  [the longest x1 45 us: on_device(): lax.all_to_all(pieces, TURNED + GRP, split_axis=0, concat_axis=0, tiled=T...]
    all_to_all x1, waiting for transfers between devices: 28.8 us -> 1.07 us  [on_device(): rows = lax.all_to_all(rollout, GRP, split_axis=0, concat_axis=0, tiled=True)]
    ppermute x4 -> x0, waiting for transfers between devices: 22.7 us -> none  [the longest x3 20.8 us: swap_z(): return lax.ppermute(block, 'zl', [(i, i ^ k) for i in range(n)])]
    ppermute x1, waiting for transfers between devices: 1.55 us -> 19.2 us  [other_half(): inward = lax.ppermute(outer, ('zl', 'h'), inner)]
    ppermute x4 -> x0, starting transfers between devices: 12.4 us -> none  [the longest x3 12.3 us: swap_z(): return lax.ppermute(block, 'zl', [(i, i ^ k) for i in range(n)])]
    all_to_all x1, starting transfers between devices: 12.6 us -> 6.14 us  [on_device(): rows = lax.all_to_all(rollout, GRP, split_axis=0, concat_axis=0, tiled=True)]
    all_gather x1, waiting for transfers between devices: 0.01 us -> 2.74 us  [on_device(): weights = lax.all_gather(pair, ('c', 'x', 'y'), axis=1, tiled=True)]
    reshape x4 -> x0, local copies, waits for them, and re-layouts: 2.71 us -> none  [the longest x1 1.31 us: on_device(): result = result.reshape(agents_own, n_dev, steps_here, width)]
  transfers between devices with their start and end apart: 8 -> 4, of which waited for: 6 -> 3; matrix products, arithmetic and copies ran while one was open for 9% -> 7% of each run, Pallas kernels for 5% -> 5%
where the time goes in v7:
time: 162 us
  blocking collectives  84.9 us (52%)
  waiting for transfers between devices  23 us (14%)
  Pallas kernels  16.3 us (10%)
  between operations  13.7 us (8%)
  starting transfers between devices  8.11 us (5%)
  matrix products  7.54 us (5%)
  local copies, waits for them, and re-layouts  5.62 us (3%)
  other arithmetic  2.47 us (2%)
    all_to_all x1, blocking collectives, on_device(): lax.all_to_all(pieces, TURNED + GRP, split_axis=0, concat_axis=0, tiled=T...  45 us
    all_to_all x1, blocking collectives, on_device(): lax.all_to_all(result, TURNED, split_axis=0, concat_axis=0, tiled=True)  39.9 us
    ppermute x1, waiting for transfers between devices, other_half(): inward = lax.ppermute(outer, ('zl', 'h'), inner)  19.2 us
    pallas_call x1, Pallas kernels, time_block(): pl.pallas_call(functools.partial(time_kernel, sizes), out_shape=jax.Shape...  8.01 us
    pallas_call x1, Pallas kernels, ff_block(): pl.pallas_call(ff_kernel, grid=(halves * n,), out_shape=jax.ShapeDtypeStr...  6.54 us
    all_to_all x1, starting transfers between devices, on_device(): rows = lax.all_to_all(rollout, GRP, split_axis=0, concat_axis=0, tiled=True)  6.14 us
    dot_general x4, matrix products, linear(): return jnp.dot(rows, weight, preferred_element_type=F32)  4.65 us
    unnamed x26, local copies, waits for them, and re-layouts  3.81 us
  transfers between devices with their start and end apart: 4, of which 3 were waited for; matrix products, arithmetic and copies ran while one was open for 7% of the time, Pallas kernels for 5%

profile of v7, /device:TPU:32, one launch (start us, length us, event | category | flops | bytes accessed | tf_op | source)
XLA Modules:
  0.0 161.6 jit_solution(1720726781950772852)
XLA Ops:
  6.5 6.1 %all-to-all-start = ((bf16[8,64,1024]{2,1,0:T(8,128)(2,1)}), bf16[8,64,1024]{2,1,0:T(8,128)(2,1)S(1)}, u32[]{:S(2)}, u32[]{:S(2)}) async-start(bf16[8,64,1024]{2,1,0:T(8,128)(2,1)} %param.13), calls=%async_computation | async-start | bytes 2097152 | tf_op jit(solution)/shard_map/all_to_all | solution.py:213
  12.8 0.7 collective-permute-start
  13.5 1.3 collective-permute-start.1
  14.8 19.2 %collective-permute-done.1 = bf16[2,32,1024]{2,1,0:T(8,128)(2,1)S(1)} collective-permute-done((bf16[2,32,1024]{2,1,0:T(8,128)(2,1)S(1)}, bf16[2,32,1024]{2,1,0:T(8,128)(2,1)S(1)}, u32[]{:S(2)}, u32[]{:S(2)}) %collective-permute-start.1) | collective-permute-done | bytes 131104 | tf_op jit(solution)/shard_map/ppermute | solution.py:184
  34.0 0.8 maximum_select_fusion
  34.7 1.1 all-to-all-done
  35.8 0.0 all-gather.2.cloned.1.call-update
  35.8 0.3 fusion.6
  36.1 0.0 copy-start.10
  36.1 2.2 %convolution_convert_fusion = bf16[512,512]{0,1:T(8,128)(2,1)S(1)} fusion(bf16[2,1024,512]{2,1,0:T(8,128)(2,1)} %param.17, bf16[512,1024]{1,0:T(8,128)(2,1)S(1)} %bitcast.44, f32[1024]{0:T(1024)S(1)} %copy-done.12, f32[512]{0:T(512)S(1)} %add_rsqrt_fusion), kind=kOutput, calls=%fused_computation.15 | convolution fusion | flops 539230208 | bytes 2627584 | tf_op jit(solution)/shard_map/dot_general | solution.py:25
  38.4 0.0 copy-start.11
  38.4 0.8 convolution_convert_fusion.1
  39.2 0.4 copy-done.11
  39.6 0.8 convolution_convert_fusion.2
  40.5 1.3 multiply_reduce_fusion
  41.8 1.4 fusion
  43.2 1.6 divide_convert_fusion
  44.7 0.8 fusion.9
  45.5 0.4 reshape.41
  46.0 1.1 copy.17
  47.0 0.0 copy-start.6
  47.1 0.0 copy-start.3
  47.1 0.0 copy-start.4
  47.1 0.0 copy-start.5
  47.1 45.0 %all_to_all.15 = bf16[256,2,1024]{2,1,0:T(2,128)(2,1)S(1)} all-to-all(bf16[256,2,1024]{2,1,0:T(2,128)(2,1)S(1)} %bitcast.49), channel_id=1, replica_groups=mesh['zl'=4,'c'=2,'x'=4,'y'=4,'h'=2] {'h','x','y','zl','c'}, dimensions={0} | all-to-all | bytes 2097152 | tf_op jit(solution)/shard_map/all_to_all | solution.py:236
  92.1 0.3 copy.21
  92.5 8.0 %time_attention.1 = bf16[2,256,1024]{2,1,0:T(8,128)(2,1)S(1)} custom-call(s32[2]{0:T(128)S(1)} %copy-done.7, bf16[2,256,1024]{2,1,0:T(8,128)(2,1)S(1)} %bitcast.40, f32[1,1024]{1,0:T(1,128)S(1)} %bitcast.42, bf16[2,1024,512]{2,1,0:T(8,128)(2,1)S(1)} %copy-done.3, bf16[1024,512]{1,0:T(8,128)(2,1)S(1)} %copy-done.4, bf16[512,1024]{1,0:T(8,128)(2,1)S(1)} %copy-done.5), custom_call_target="tpu_custom_call" | custom-call | flops 3221225472 | bytes 6291456 | tf_op jit(solution)/shard_map/time_attention/pallas_call | solution.py:87
  100.5 2.7 %all-gather.2.cloned.1.call-done = bf16[2,2048,1024]{2,1,0:T(8,128)(2,1)} async-done(((bf16[2,64,1024]{2,1,0:T(8,128)(2,1)}), bf16[2,2048,1024]{2,1,0:T(8,128)(2,1)}) %all-gather.2.cloned.1.call-update) | async-done | bytes 8388624 | tf_op jit(solution)/shard_map/all_gather | solution.py:219
  103.2 3.4 %copy-done.1 = bf16[2,2048,1024]{2,1,0:T(8,128)(2,1)S(1)} copy-done((bf16[2,2048,1024]{2,1,0:T(8,128)(2,1)S(1)}, bf16[2,2048,1024]{2,1,0:T(8,128)(2,1)}, u32[]{:S(2)}) %copy-start.1) | copy-done | bytes 8388632
  106.6 6.5 %feed_forward.1 = bf16[32,2,8,1024]{3,2,1,0:T(8,128)(2,1)S(1)} custom-call(bf16[512,1024]{1,0:T(8,128)(2,1)S(1)} %bitcast.39, f32[1,1024]{1,0:T(1,128)S(1)} %bitcast.41, bf16[2,2,1024,1024]{3,2,1,0:T(8,128)(2,1)S(1)} %bitcast.37, bf16[2,2,1024,1024]{3,2,1,0:T(8,128)(2,1)S(1)} %bitcast.38), custom_call_target="tpu_custom_call" | custom-call | flops 4294967296 | bytes 10485760 | tf_op jit(solution)/shard_map/feed_forward/pallas_call | solution.py:134
  113.1 39.9 %all_to_all.16.rows_ref = bf16[32,2,8,1024]{3,2,1,0:T(8,128)(2,1)S(1)} all-to-all(bf16[32,2,8,1024]{3,2,1,0:T(8,128)(2,1)S(1)} %feed_forward.1), channel_id=1, replica_groups=mesh['zl'=4,'c'=2,'x'=4,'y'=4,'h'=2] {'h','x','y'}, dimensions={0} | all-to-all | bytes 2097152 | tf_op jit(solution)/shard_map/all_to_all | solution.py:244
  153.1 1.7 %reorder.1 = bf16[8,64,1024]{2,1,0:T(8,128)(2,1)} custom-call(bf16[32,2,8,1024]{3,2,1,0:T(8,128)(2,1)S(1)} %all_to_all.16.rows_ref), custom_call_target="tpu_custom_call" | custom-call | flops 536870912 | bytes 2097152 | tf_op jit(solution)/shard_map/reorder/pallas_call | solution.py:167
  (25 shorter events, 0.1 us)
Async XLA Ops:
  6.5 38.2 %copy-start = (bf16[512,1024]{1,0:T(8,128)(2,1)S(1)}, bf16[512,1024]{1,0:T(8,128)(2,1)}, u32[]{:S(2)}) copy-start(bf16[512,1024]{1,0:T(8,128)(2,1)} %param.19) | copy-start | bytes 3145732
  6.5 6.2 %copy-start.8 = (bf16[2048,32]{0,1:T(8,128)(2,1)S(1)}, bf16[2048,32]{0,1:T(8,128)(2,1)}, u32[]{:S(2)}) copy-start(bf16[2048,32]{0,1:T(8,128)(2,1)} %param.24) | copy-start | bytes 393220
  6.5 6.2 %copy-start.9 = (bf16[32,2048]{1,0:T(8,128)(2,1)S(1)}, bf16[32,2048]{1,0:T(8,128)(2,1)}, u32[]{:S(2)}) copy-start(bf16[32,2048]{1,0:T(8,128)(2,1)} %param.23) | copy-start | bytes 393220
  6.5 29.6 %copy-start.12 = (f32[1024]{0:T(1024)S(1)}, f32[1024]{0:T(1024)}, u32[]{:S(2)}) copy-start(f32[1024]{0:T(1024)} %param.14) | copy-start | bytes 12292
  6.5 29.3 %all-to-all-start = ((bf16[8,64,1024]{2,1,0:T(8,128)(2,1)}), bf16[8,64,1024]{2,1,0:T(8,128)(2,1)S(1)}, u32[]{:S(2)}, u32[]{:S(2)}) async-start(bf16[8,64,1024]{2,1,0:T(8,128)(2,1)} %param.13), calls=%async_computation | async-start | bytes 2097152 | tf_op jit(solution)/shard_map/all_to_all | solution.py:213
  12.7 90.5 %all-gather.2.cloned.1.call-start = ((), (), s32[]{:S(2)}) async-start(), calls=%async_computation.3 | async-start | bytes 8650752 | tf_op jit(solution)/shard_map/all_gather | solution.py:219
  12.8 0.7 collective-permute-start
  13.5 20.5 %collective-permute-start.1 = (bf16[2,32,1024]{2,1,0:T(8,128)(2,1)S(1)}, bf16[2,32,1024]{2,1,0:T(8,128)(2,1)S(1)}, u32[]{:S(2)}, u32[]{:S(2)}) collective-permute-start(bf16[2,32,1024]{2,1,0:T(8,128)(2,1)S(1)} %collective-permute-done), channel_id=1, source_target_pairs={{0,64},{192,128},{1,65},{193,129},{2,66},{194,130},{3,67},{195,131... | collective-permute-start | bytes 393224 | tf_op jit(solution)/shard_map/ppermute | solution.py:184
  36.1 2.2 %copy-start.10 = (bf16[2,1024,512]{2,1,0:T(8,128)(2,1)S(1)}, bf16[2,1024,512]{2,1,0:T(8,128)(2,1)}, u32[]{:S(2)}) copy-start(bf16[2,1024,512]{2,1,0:T(8,128)(2,1)} %param.17) | copy-start | bytes 6291460
  38.4 1.2 copy-start.11
  47.0 45.3 %copy-start.6 = (f32[1024]{0:T(1024)S(1)}, f32[1024]{0:T(1024)}, u32[]{:S(2)}) copy-start(f32[1024]{0:T(1024)} %param.15) | copy-start | bytes 12292
  47.1 45.3 %copy-start.3 = (bf16[2,1024,512]{2,1,0:T(8,128)(2,1)S(1)}, bf16[2,1024,512]{2,1,0:T(8,128)(2,1)}, u32[]{:S(2)}) copy-start(bf16[2,1024,512]{2,1,0:T(8,128)(2,1)} %qk_ref.1) | copy-start | bytes 6291460
  47.1 45.3 %copy-start.4 = (bf16[1024,512]{1,0:T(8,128)(2,1)S(1)}, bf16[1024,512]{1,0:T(8,128)(2,1)}, u32[]{:S(2)}) copy-start(bf16[1024,512]{1,0:T(8,128)(2,1)} %v_ref.1) | copy-start | bytes 3145732
  47.1 45.3 %copy-start.5 = (bf16[512,1024]{1,0:T(8,128)(2,1)S(1)}, bf16[512,1024]{1,0:T(8,128)(2,1)}, u32[]{:S(2)}) copy-start(bf16[512,1024]{1,0:T(8,128)(2,1)} %o_ref.1) | copy-start | bytes 3145732
  47.1 45.3 %copy-start.7 = (s32[2]{0:T(128)S(1)}, s32[2]{0:T(128)}, u32[]{:S(2)}) copy-start(s32[2]{0:T(128)} %start_ref.1) | copy-start | bytes 28
  92.4 10.8 %copy-start.2 = (f32[1024]{0:T(1024)S(1)}, f32[1024]{0:T(1024)}, u32[]{:S(2)}) copy-start(f32[1024]{0:T(1024)} %param.16) | copy-start | bytes 12292
  103.2 3.4 %copy-start.1 = (bf16[2,2048,1024]{2,1,0:T(8,128)(2,1)S(1)}, bf16[2,2048,1024]{2,1,0:T(8,128)(2,1)}, u32[]{:S(2)}) copy-start(bf16[2,2048,1024]{2,1,0:T(8,128)(2,1)} %all-gather.2.cloned.1.call-done) | copy-start | bytes 25165828
Sparse Core Ops, SparseCore 0:
  36.0 67.2 all-gather.1

commit v8 on v7

--- a/solution.py
+++ b/solution.py
@@ -175,14 +175,11 @@
     )(rows)
 
 
-def other_half(block, zl, high):
+def other_half(block):
     n = lax.axis_size("zl")
     spot = lambda h, z: z * 2 + h
-    edge = [(spot(h, z), spot(1 - h, n - 1 - z)) for h in (0, 1) for z in (0, n - 1)]
-    inner = [(spot(h, z), spot(h, w)) for h in (0, 1) for z, w in ((0, 1), (n - 1, n - 2))]
-    outer = lax.ppermute(block, ("zl", "h"), edge)
-    inward = lax.ppermute(outer, ("zl", "h"), inner)
-    return jnp.where((zl == 0) | (zl == n - 1), outer, inward)
+    mirror = [(spot(h, z), spot(1 - h, n - 1 - z)) for h in (0, 1) for z in range(n)]
+    return lax.ppermute(block, ("zl", "h"), mirror)
 
 
 def on_device(
@@ -201,14 +198,14 @@
     episode_start,
 ):
     steps_here, agents_here, width = rollout.shape
-    zl, core, high = lax.axis_index("zl"), lax.axis_index("c"), lax.axis_index("h")
+    core, high = lax.axis_index("c"), lax.axis_index("h")
     n_grp, n_core = lax.axis_size(GRP), lax.axis_size("c")
 
     half = expand_weight.shape[1] // 2
     up = lax.dynamic_slice_in_dim(expand_weight, core * half, half, 1)
     down = lax.dynamic_slice_in_dim(reduce_weight.T, core * half, half, 1)
     mine = jnp.stack([up, down])
-    other = other_half(mine, zl, high)
+    other = other_half(mine)
 
     rows = lax.all_to_all(rollout, GRP, split_axis=0, concat_axis=0, tiled=True)
     rows = rows.reshape(n_grp * agents_here, width)
@@ -234,6 +231,7 @@
     pieces = after_agents.reshape(n_grp, n_flat, n_high, agents_own, width)
     pieces = jnp.transpose(pieces, (2, 1, 0, 3, 4)).reshape(steps, agents_own, width)
     series = lax.all_to_all(pieces, TURNED + GRP, split_axis=0, concat_axis=0, tiled=True)
+    series, weights = lax.optimization_barrier((series, weights))
     series = jnp.swapaxes(series, 0, 1)
     sizes = (n_flat, n_high, steps_here)
     after_time = time_block(

time: 162 us -> 168 us (1.037)
  waiting for transfers between devices: 23 us -> 28.9 us
  starting transfers between devices: 8.11 us -> 11 us
  local copies, waits for them, and re-layouts: 5.62 us -> 3.77 us
    all_gather x1, waiting for transfers between devices: 2.74 us -> 10.9 us  [on_device(): weights = lax.all_gather(pair, ('c', 'x', 'y'), axis=1, tiled=True)]
    unnamed x26, local copies, waits for them, and re-layouts: 3.81 us -> 0.59 us
    ppermute x2 -> x1, starting transfers between devices: 1.96 us -> 4.86 us  [other_half(): return lax.ppermute(block, ('zl', 'h'), mirror)]
    ppermute x2 -> x1, waiting for transfers between devices: 19.2 us -> 18 us  [other_half(): return lax.ppermute(block, ('zl', 'h'), mirror)]
  transfers between devices with their start and end apart: 4 -> 3, of which waited for: 3 -> 2; matrix products, arithmetic and copies ran while one was open for 7% -> 7% of each run, Pallas kernels for 5% -> 0%
where the time goes in v8:
time: 168 us
  blocking collectives  84.4 us (50%)
  waiting for transfers between devices  28.9 us (17%)
  Pallas kernels  16.2 us (10%)
  between operations  13.6 us (8%)
  starting transfers between devices  11 us (7%)
  matrix products  7.53 us (4%)
  local copies, waits for them, and re-layouts  3.77 us (2%)
  other arithmetic  2.45 us (1%)
    all_to_all x1, blocking collectives, on_device(): lax.all_to_all(pieces, TURNED + GRP, split_axis=0, concat_axis=0, tiled=T...  44.5 us
    all_to_all x1, blocking collectives, on_device(): lax.all_to_all(result, TURNED, split_axis=0, concat_axis=0, tiled=True)  39.9 us
    ppermute x1, waiting for transfers between devices, other_half(): return lax.ppermute(block, ('zl', 'h'), mirror)  18 us
    all_gather x1, waiting for transfers between devices, on_device(): weights = lax.all_gather(pair, ('c', 'x', 'y'), axis=1, tiled=True)  10.9 us
    pallas_call x1, Pallas kernels, time_block(): pl.pallas_call(functools.partial(time_kernel, sizes), out_shape=jax.Shape...  7.94 us
    pallas_call x1, Pallas kernels, ff_block(): pl.pallas_call(ff_kernel, grid=(halves * n,), out_shape=jax.ShapeDtypeStr...  6.56 us
    all_to_all x1, starting transfers between devices, on_device(): rows = lax.all_to_all(rollout, GRP, split_axis=0, concat_axis=0, tiled=True)  6.14 us
    ppermute x1, starting transfers between devices, other_half(): return lax.ppermute(block, ('zl', 'h'), mirror)  4.86 us
  transfers between devices with their start and end apart: 3, of which 2 were waited for; matrix products, arithmetic and copies ran while one was open for 7% of the time, Pallas kernels for 0%

profile of v8, /device:TPU:32, one launch (start us, length us, event | category | flops | bytes accessed | tf_op | source)
XLA Modules:
  0.0 168.0 jit_solution(5126442254283737113)
XLA Ops:
  6.5 6.1 %all-to-all-start = ((bf16[8,64,1024]{2,1,0:T(8,128)(2,1)}), bf16[8,64,1024]{2,1,0:T(8,128)(2,1)S(1)}, u32[]{:S(2)}, u32[]{:S(2)}) async-start(bf16[8,64,1024]{2,1,0:T(8,128)(2,1)} %param.13), calls=%async_computation | async-start | bytes 2097152 | tf_op jit(solution)/shard_map/all_to_all | solution.py:210
  12.7 0.0 copy-done.8
  12.7 0.0 copy-done.9
  12.8 4.9 %collective-permute-start = (bf16[2,32,1024]{2,1,0:T(8,128)(2,1)S(1)}, bf16[2,32,1024]{2,1,0:T(8,128)(2,1)S(1)}, u32[]{:S(2)}, u32[]{:S(2)}) collective-permute-start(bf16[2,32,1024]{2,1,0:T(8,128)(2,1)S(1)} %pad_maximum_fusion), channel_id=1, source_target_pairs={{0,193},{64,129},{128,65},{192,1},{1,192},{65,128},{129,64},{193,0... | collective-permute-start | bytes 393224 | tf_op jit(solution)/shard_map/ppermute | solution.py:182
  17.6 18.0 %collective-permute-done = bf16[2,32,1024]{2,1,0:T(8,128)(2,1)S(1)} collective-permute-done((bf16[2,32,1024]{2,1,0:T(8,128)(2,1)S(1)}, bf16[2,32,1024]{2,1,0:T(8,128)(2,1)S(1)}, u32[]{:S(2)}, u32[]{:S(2)}) %collective-permute-start) | collective-permute-done | bytes 131104 | tf_op jit(solution)/shard_map/ppermute | solution.py:182
  35.7 0.8 maximum_select_fusion
  36.4 0.0 all-to-all-done
  36.4 0.0 all-gather.2.cloned.1.call-update
  36.4 0.3 fusion.6
  36.7 0.0 copy-start.10
  36.8 2.2 %convolution_convert_fusion = bf16[512,512]{0,1:T(8,128)(2,1)S(1)} fusion(bf16[2,1024,512]{2,1,0:T(8,128)(2,1)} %param.17, bf16[512,1024]{1,0:T(8,128)(2,1)S(1)} %bitcast.44, f32[1024]{0:T(1024)S(1)} %copy-done.12, f32[512]{0:T(512)S(1)} %add_rsqrt_fusion), kind=kOutput, calls=%fused_computation.15 | convolution fusion | flops 539230208 | bytes 2627584 | tf_op jit(solution)/shard_map/dot_general | solution.py:25
  39.0 0.0 copy-start.11
  39.0 0.8 convolution_convert_fusion.1
  39.9 0.4 copy-done.11
  40.2 0.8 convolution_convert_fusion.2
  41.1 1.3 multiply_reduce_fusion
  42.4 1.4 fusion
  43.8 1.6 divide_convert_fusion
  45.4 0.8 fusion.9
  46.1 0.4 reshape.41
  46.6 1.1 copy.17
  47.7 0.0 copy-start.3
  47.7 0.0 copy-start.6
  47.7 0.0 copy-start.7
  47.7 44.5 %all_to_all.15 = bf16[256,2,1024]{2,1,0:T(2,128)(2,1)} all-to-all(bf16[256,2,1024]{2,1,0:T(2,128)(2,1)S(1)} %bitcast.49), channel_id=1, replica_groups=mesh['zl'=4,'c'=2,'x'=4,'y'=4,'h'=2] {'h','x','y','zl','c'}, dimensions={0} | all-to-all | bytes 2097152 | tf_op jit(solution)/shard_map/all_to_all | solution.py:233
  92.2 10.9 %all-gather.2.cloned.1.call-done = bf16[2,2048,1024]{2,1,0:T(8,128)(2,1)} async-done(((bf16[2,64,1024]{2,1,0:T(8,128)(2,1)}), bf16[2,2048,1024]{2,1,0:T(8,128)(2,1)}) %all-gather.2.cloned.1.call-update) | async-done | bytes 8388624 | tf_op jit(solution)/shard_map/all_gather | solution.py:216
  103.1 1.6 copy.21
  104.7 0.2 copy-done.5
  104.9 7.9 %time_attention.1 = bf16[2,256,1024]{2,1,0:T(8,128)(2,1)S(1)} custom-call(s32[2]{0:T(128)S(1)} %copy-done.7, bf16[2,256,1024]{2,1,0:T(8,128)(2,1)S(1)} %bitcast.40, f32[1,1024]{1,0:T(1,128)S(1)} %bitcast.42, bf16[2,1024,512]{2,1,0:T(8,128)(2,1)S(1)} %copy-done.3, bf16[1024,512]{1,0:T(8,128)(2,1)S(1)} %copy-done.4, bf16[512,1024]{1,0:T(8,128)(2,1)S(1)} %copy-done.5), custom_call_target="tpu_custom_call" | custom-call | flops 3221225472 | bytes 6291456 | tf_op jit(solution)/shard_map/time_attention/pallas_call | solution.py:87
  112.9 6.6 %feed_forward.1 = bf16[32,2,8,1024]{3,2,1,0:T(8,128)(2,1)S(1)} custom-call(bf16[512,1024]{1,0:T(8,128)(2,1)S(1)} %bitcast.39, f32[1,1024]{1,0:T(1,128)S(1)} %bitcast.41, bf16[2,2,1024,1024]{3,2,1,0:T(8,128)(2,1)S(1)} %bitcast.37, bf16[2,2,1024,1024]{3,2,1,0:T(8,128)(2,1)S(1)} %bitcast.38), custom_call_target="tpu_custom_call" | custom-call | flops 4294967296 | bytes 10485760 | tf_op jit(solution)/shard_map/feed_forward/pallas_call | solution.py:134
  119.5 39.9 %all_to_all.16.rows_ref = bf16[32,2,8,1024]{3,2,1,0:T(8,128)(2,1)S(1)} all-to-all(bf16[32,2,8,1024]{3,2,1,0:T(8,128)(2,1)S(1)} %feed_forward.1), channel_id=1, replica_groups=mesh['zl'=4,'c'=2,'x'=4,'y'=4,'h'=2] {'h','x','y'}, dimensions={0} | all-to-all | bytes 2097152 | tf_op jit(solution)/shard_map/all_to_all | solution.py:242
  159.4 1.7 %reorder.1 = bf16[8,64,1024]{2,1,0:T(8,128)(2,1)} custom-call(bf16[32,2,8,1024]{3,2,1,0:T(8,128)(2,1)S(1)} %all_to_all.16.rows_ref), custom_call_target="tpu_custom_call" | custom-call | flops 536870912 | bytes 2097152 | tf_op jit(solution)/shard_map/reorder/pallas_call | solution.py:167
  (22 shorter events, 0.1 us)
Async XLA Ops:
  6.5 38.8 %copy-start = (bf16[512,1024]{1,0:T(8,128)(2,1)S(1)}, bf16[512,1024]{1,0:T(8,128)(2,1)}, u32[]{:S(2)}) copy-start(bf16[512,1024]{1,0:T(8,128)(2,1)} %param.19) | copy-start | bytes 3145732
  6.5 6.2 %copy-start.8 = (bf16[2048,32]{0,1:T(8,128)(2,1)S(1)}, bf16[2048,32]{0,1:T(8,128)(2,1)}, u32[]{:S(2)}) copy-start(bf16[2048,32]{0,1:T(8,128)(2,1)} %param.24) | copy-start | bytes 393220
  6.5 6.2 %copy-start.9 = (bf16[32,2048]{1,0:T(8,128)(2,1)S(1)}, bf16[32,2048]{1,0:T(8,128)(2,1)}, u32[]{:S(2)}) copy-start(bf16[32,2048]{1,0:T(8,128)(2,1)} %param.23) | copy-start | bytes 393220
  6.5 30.2 %copy-start.12 = (f32[1024]{0:T(1024)S(1)}, f32[1024]{0:T(1024)}, u32[]{:S(2)}) copy-start(f32[1024]{0:T(1024)} %param.14) | copy-start | bytes 12292
  6.5 29.9 %all-to-all-start = ((bf16[8,64,1024]{2,1,0:T(8,128)(2,1)}), bf16[8,64,1024]{2,1,0:T(8,128)(2,1)S(1)}, u32[]{:S(2)}, u32[]{:S(2)}) async-start(bf16[8,64,1024]{2,1,0:T(8,128)(2,1)} %param.13), calls=%async_computation | async-start | bytes 2097152 | tf_op jit(solution)/shard_map/all_to_all | solution.py:210
  12.7 90.4 %all-gather.2.cloned.1.call-start = ((), (), s32[]{:S(2)}) async-start(), calls=%async_computation.3 | async-start | bytes 8650752 | tf_op jit(solution)/shard_map/all_gather | solution.py:216
  12.8 22.9 %collective-permute-start = (bf16[2,32,1024]{2,1,0:T(8,128)(2,1)S(1)}, bf16[2,32,1024]{2,1,0:T(8,128)(2,1)S(1)}, u32[]{:S(2)}, u32[]{:S(2)}) collective-permute-start(bf16[2,32,1024]{2,1,0:T(8,128)(2,1)S(1)} %pad_maximum_fusion), channel_id=1, source_target_pairs={{0,193},{64,129},{128,65},{192,1},{1,192},{65,128},{129,64},{193,0... | collective-permute-start | bytes 393224 | tf_op jit(solution)/shard_map/ppermute | solution.py:182
  36.7 2.2 %copy-start.10 = (bf16[2,1024,512]{2,1,0:T(8,128)(2,1)S(1)}, bf16[2,1024,512]{2,1,0:T(8,128)(2,1)}, u32[]{:S(2)}) copy-start(bf16[2,1024,512]{2,1,0:T(8,128)(2,1)} %param.17) | copy-start | bytes 6291460
  39.0 1.2 copy-start.11
  47.7 57.1 %copy-start.3 = (bf16[2,1024,512]{2,1,0:T(8,128)(2,1)S(1)}, bf16[2,1024,512]{2,1,0:T(8,128)(2,1)}, u32[]{:S(2)}) copy-start(bf16[2,1024,512]{2,1,0:T(8,128)(2,1)} %qk_ref.1) | copy-start | bytes 6291460
  47.7 57.1 %copy-start.6 = (f32[1024]{0:T(1024)S(1)}, f32[1024]{0:T(1024)}, u32[]{:S(2)}) copy-start(f32[1024]{0:T(1024)} %param.15) | copy-start | bytes 12292
  47.7 57.1 %copy-start.7 = (s32[2]{0:T(128)S(1)}, s32[2]{0:T(128)}, u32[]{:S(2)}) copy-start(s32[2]{0:T(128)} %start_ref.1) | copy-start | bytes 28
  103.1 1.7 %copy-start.4 = (bf16[1024,512]{1,0:T(8,128)(2,1)S(1)}, bf16[1024,512]{1,0:T(8,128)(2,1)}, u32[]{:S(2)}) copy-start(bf16[1024,512]{1,0:T(8,128)(2,1)} %v_ref.1) | copy-start | bytes 3145732
  103.1 1.9 %copy-start.5 = (bf16[512,1024]{1,0:T(8,128)(2,1)S(1)}, bf16[512,1024]{1,0:T(8,128)(2,1)}, u32[]{:S(2)}) copy-start(bf16[512,1024]{1,0:T(8,128)(2,1)} %o_ref.1) | copy-start | bytes 3145732
  104.9 8.0 %copy-start.1 = (bf16[2,2048,1024]{2,1,0:T(8,128)(2,1)S(1)}, bf16[2,2048,1024]{2,1,0:T(8,128)(2,1)}, u32[]{:S(2)}) copy-start(bf16[2,2048,1024]{2,1,0:T(8,128)(2,1)} %all-gather.2.cloned.1.call-done) | copy-start | bytes 25165828
  104.9 8.0 %copy-start.2 = (f32[1024]{0:T(1024)S(1)}, f32[1024]{0:T(1024)}, u32[]{:S(2)}) copy-start(f32[1024]{0:T(1024)} %param.16) | copy-start | bytes 12292
Sparse Core Ops, SparseCore 0:
  36.6 66.4 all-gather.1

commit v9 on v8

--- a/solution.py
+++ b/solution.py
@@ -207,12 +207,13 @@
     mine = jnp.stack([up, down])
     other = other_half(mine)
 
-    rows = lax.all_to_all(rollout, GRP, split_axis=0, concat_axis=0, tiled=True)
+    odd = mine[0, 0, 0] != mine[0, 0, 0]
+    rows = jnp.where(odd, -rollout, rollout)
+    rows = lax.all_to_all(rows, GRP, split_axis=0, concat_axis=0, tiled=True)
     rows = rows.reshape(n_grp * agents_here, width)
     pair = jnp.where(
         high == 0, jnp.concatenate([mine, other], 1), jnp.concatenate([other, mine], 1)
     )
-    rows, pair = lax.optimization_barrier((rows, pair))
     weights = lax.all_gather(pair, ("c", "x", "y"), axis=1, tiled=True)
     weights = weights.reshape(2, n_core, width, half)
 

time: 168 us -> 169 us (level)
  blocking collectives: 84.4 us -> 111 us
  waiting for transfers between devices: 28.9 us -> 3.62 us
  starting transfers between devices: 11 us -> 5.93 us
  local copies, waits for them, and re-layouts: 3.77 us -> 7.22 us
  other arithmetic: 2.45 us -> 4.36 us
    all_to_all x0 -> x1, blocking collectives: none -> 30 us  [on_device(): rows = lax.all_to_all(rows, GRP, split_axis=0, concat_axis=0, tiled=True)]
    ppermute x1, waiting for transfers between devices: 18 us -> 3.61 us  [other_half(): return lax.ppermute(block, ('zl', 'h'), mirror)]
    all_gather x1, waiting for transfers between devices: 10.9 us -> 0.01 us  [on_device(): weights = lax.all_gather(pair, ('c', 'x', 'y'), axis=1, tiled=True)]
    all_to_all x1 -> x0, starting transfers between devices: 6.14 us -> none  [on_device(): rows = lax.all_to_all(rollout, GRP, split_axis=0, concat_axis=0, tiled=True)]
    all_to_all x1, blocking collectives: 39.9 us -> 37.3 us  [on_device(): lax.all_to_all(result, TURNED, split_axis=0, concat_axis=0, tiled=True)]
    another operation x2, local copies, waits for them, and re-layouts: 0.03 us -> 1.78 us  [on_device(): mine = jnp.stack([up, down])]
  transfers between devices with their start and end apart: 3 -> 2, of which waited for: 2 -> 1; matrix products, arithmetic and copies ran while one was open for 7% -> 7% of each run, Pallas kernels for 0% -> 0%
where the time goes in v9:
time: 169 us
  blocking collectives  111 us (66%)
  Pallas kernels  16.2 us (10%)
  between operations  14.9 us (9%)
  local copies, waits for them, and re-layouts  7.22 us (4%)
  starting transfers between devices  5.93 us (4%)
  matrix products  5.9 us (3%)
  other arithmetic  4.36 us (3%)
  waiting for transfers between devices  3.62 us (2%)
    all_to_all x1, blocking collectives, on_device(): lax.all_to_all(pieces, TURNED + GRP, split_axis=0, concat_axis=0, tiled=T...  43.6 us
    all_to_all x1, blocking collectives, on_device(): lax.all_to_all(result, TURNED, split_axis=0, concat_axis=0, tiled=True)  37.3 us
    all_to_all x1, blocking collectives, on_device(): rows = lax.all_to_all(rows, GRP, split_axis=0, concat_axis=0, tiled=True)  30 us
    pallas_call x1, Pallas kernels, time_block(): pl.pallas_call(functools.partial(time_kernel, sizes), out_shape=jax.Shape...  7.91 us
    pallas_call x1, Pallas kernels, ff_block(): pl.pallas_call(ff_kernel, grid=(halves * n,), out_shape=jax.ShapeDtypeStr...  6.56 us
    ppermute x1, starting transfers between devices, other_half(): return lax.ppermute(block, ('zl', 'h'), mirror)  5.93 us
    ppermute x1, waiting for transfers between devices, other_half(): return lax.ppermute(block, ('zl', 'h'), mirror)  3.61 us
  transfers between devices with their start and end apart: 2, of which 1 were waited for; matrix products, arithmetic and copies ran while one was open for 7% of the time, Pallas kernels for 0%

profile of v9, /device:TPU:32, one launch (start us, length us, event | category | flops | bytes accessed | tf_op | source)
XLA Modules:
  0.0 169.0 jit_solution(2402832747342650731)
XLA Ops:
  6.5 0.9 dynamic-slice_bitcast_fusion.1
  7.5 0.8 dynamic-slice_bitcast_fusion
  8.3 5.9 %collective-permute-start = (bf16[2,32,1024]{2,1,0:T(8,128)(2,1)S(1)}, bf16[2,32,1024]{2,1,0:T(8,128)(2,1)S(1)}, u32[]{:S(2)}, u32[]{:S(2)}) collective-permute-start(bf16[2,32,1024]{2,1,0:T(8,128)(2,1)S(1)} %pad_maximum_fusion), channel_id=1, source_target_pairs={{0,193},{64,129},{128,65},{192,1},{1,192},{65,128},{129,64},{193,0... | collective-permute-start | bytes 393224 | tf_op jit(solution)/shard_map/ppermute | solution.py:182
  14.3 3.6 %collective-permute-done = bf16[2,32,1024]{2,1,0:T(8,128)(2,1)S(1)} collective-permute-done((bf16[2,32,1024]{2,1,0:T(8,128)(2,1)S(1)}, bf16[2,32,1024]{2,1,0:T(8,128)(2,1)S(1)}, u32[]{:S(2)}, u32[]{:S(2)}) %collective-permute-start) | collective-permute-done | bytes 131104 | tf_op jit(solution)/shard_map/ppermute | solution.py:182
  17.9 0.8 maximum_select_fusion
  18.6 0.0 all-gather.2.cloned.1.call-update
  18.7 0.6 slice.13
  20.6 1.3 negate_select_fusion
  21.9 30.0 %all_to_all.15 = bf16[8,64,1024]{2,1,0:T(8,128)(2,1)S(1)} all-to-all(bf16[8,64,1024]{2,1,0:T(8,128)(2,1)S(1)} %negate_select_fusion), channel_id=1, replica_groups=mesh['zl'=4,'c'=2,'x'=4,'y'=4,'h'=2] {'zl','c'}, dimensions={0} | all-to-all | bytes 2097152 | tf_op jit(solution)/shard_map/all_to_all | solution.py:212
  51.9 0.3 fusion.6
  52.2 0.1 rsqrt.13
  52.3 0.3 fusion.10
  52.6 0.3 fusion.8
  52.9 1.0 copy-done.9
  53.9 0.8 convolution_convert_fusion.1
  54.6 0.0 copy-start.10
  54.6 0.8 convolution_convert_fusion
  55.4 0.5 copy-done.10
  55.8 0.8 convolution_convert_fusion.2
  56.6 1.3 multiply_reduce_fusion
  57.9 1.4 fusion
  59.3 1.6 divide_convert_fusion
  60.9 0.8 fusion.11
  61.7 0.4 reshape.70
  62.1 1.1 copy.17
  63.2 43.6 %all_to_all.16 = bf16[256,2,1024]{2,1,0:T(2,128)(2,1)} all-to-all(bf16[256,2,1024]{2,1,0:T(2,128)(2,1)S(1)} %bitcast.57), channel_id=1, replica_groups=mesh['zl'=4,'c'=2,'x'=4,'y'=4,'h'=2] {'h','x','y','zl','c'}, dimensions={0} | all-to-all | bytes 2097152 | tf_op jit(solution)/shard_map/all_to_all | solution.py:234
  106.8 1.6 copy.21
  108.5 0.2 copy-done.5
  108.7 7.9 %time_attention.1 = bf16[2,256,1024]{2,1,0:T(8,128)(2,1)S(1)} custom-call(s32[2]{0:T(128)S(1)} %copy-done.7, bf16[2,256,1024]{2,1,0:T(8,128)(2,1)S(1)} %bitcast.53, f32[1,1024]{1,0:T(1,128)S(1)} %bitcast.55, bf16[2,1024,512]{2,1,0:T(8,128)(2,1)S(1)} %copy-done.3, bf16[1024,512]{1,0:T(8,128)(2,1)S(1)} %copy-done.4, bf16[512,1024]{1,0:T(8,128)(2,1)S(1)} %copy-done.5), custom_call_target="tpu_custom_call" | custom-call | flops 3221225472 | bytes 6291456 | tf_op jit(solution)/shard_map/time_attention/pallas_call | solution.py:87
  116.6 6.6 %feed_forward.1 = bf16[32,2,8,1024]{3,2,1,0:T(8,128)(2,1)S(1)} custom-call(bf16[512,1024]{1,0:T(8,128)(2,1)S(1)} %bitcast.52, f32[1,1024]{1,0:T(1,128)S(1)} %bitcast.54, bf16[2,2,1024,1024]{3,2,1,0:T(8,128)(2,1)S(1)} %bitcast.50, bf16[2,2,1024,1024]{3,2,1,0:T(8,128)(2,1)S(1)} %bitcast.51), custom_call_target="tpu_custom_call" | custom-call | flops 4294967296 | bytes 10485760 | tf_op jit(solution)/shard_map/feed_forward/pallas_call | solution.py:134
  123.2 37.3 %all_to_all.17.rows_ref = bf16[32,2,8,1024]{3,2,1,0:T(8,128)(2,1)S(1)} all-to-all(bf16[32,2,8,1024]{3,2,1,0:T(8,128)(2,1)S(1)} %feed_forward.1), channel_id=1, replica_groups=mesh['zl'=4,'c'=2,'x'=4,'y'=4,'h'=2] {'h','x','y'}, dimensions={0} | all-to-all | bytes 2097152 | tf_op jit(solution)/shard_map/all_to_all | solution.py:243
  160.4 1.7 %reorder.1 = bf16[8,64,1024]{2,1,0:T(8,128)(2,1)} custom-call(bf16[32,2,8,1024]{3,2,1,0:T(8,128)(2,1)S(1)} %all_to_all.17.rows_ref), custom_call_target="tpu_custom_call" | custom-call | flops 536870912 | bytes 2097152 | tf_op jit(solution)/shard_map/reorder/pallas_call | solution.py:167
  (22 shorter events, 0.1 us)
Async XLA Ops:
  6.5 54.4 %copy-start = (bf16[512,1024]{1,0:T(8,128)(2,1)S(1)}, bf16[512,1024]{1,0:T(8,128)(2,1)}, u32[]{:S(2)}) copy-start(bf16[512,1024]{1,0:T(8,128)(2,1)} %param.19) | copy-start | bytes 3145732
  6.5 100.3 %all-gather.2.cloned.1.call-start = ((), (), s32[]{:S(2)}) async-start(), calls=%async_computation.3 | async-start | bytes 8650752 | tf_op jit(solution)/shard_map/all_gather | solution.py:217
  8.3 9.5 %collective-permute-start = (bf16[2,32,1024]{2,1,0:T(8,128)(2,1)S(1)}, bf16[2,32,1024]{2,1,0:T(8,128)(2,1)S(1)}, u32[]{:S(2)}, u32[]{:S(2)}) collective-permute-start(bf16[2,32,1024]{2,1,0:T(8,128)(2,1)S(1)} %pad_maximum_fusion), channel_id=1, source_target_pairs={{0,193},{64,129},{128,65},{192,1},{1,192},{65,128},{129,64},{193,0... | collective-permute-start | bytes 393224 | tf_op jit(solution)/shard_map/ppermute | solution.py:182
  21.9 30.4 %copy-start.8 = (f32[1024]{0:T(1024)S(1)}, f32[1024]{0:T(1024)}, u32[]{:S(2)}) copy-start(f32[1024]{0:T(1024)} %param.14) | copy-start | bytes 12292
  52.3 1.6 copy-start.9
  54.6 1.2 copy-start.10
  63.2 45.3 %copy-start.3 = (bf16[2,1024,512]{2,1,0:T(8,128)(2,1)S(1)}, bf16[2,1024,512]{2,1,0:T(8,128)(2,1)}, u32[]{:S(2)}) copy-start(bf16[2,1024,512]{2,1,0:T(8,128)(2,1)} %qk_ref.1) | copy-start | bytes 6291460
  63.2 45.3 %copy-start.6 = (f32[1024]{0:T(1024)S(1)}, f32[1024]{0:T(1024)}, u32[]{:S(2)}) copy-start(f32[1024]{0:T(1024)} %param.15) | copy-start | bytes 12292
  63.2 45.3 %copy-start.7 = (s32[2]{0:T(128)S(1)}, s32[2]{0:T(128)}, u32[]{:S(2)}) copy-start(s32[2]{0:T(128)} %start_ref.1) | copy-start | bytes 28
  106.8 1.7 copy-start.4
  106.8 1.9 %copy-start.5 = (bf16[512,1024]{1,0:T(8,128)(2,1)S(1)}, bf16[512,1024]{1,0:T(8,128)(2,1)}, u32[]{:S(2)}) copy-start(bf16[512,1024]{1,0:T(8,128)(2,1)} %o_ref.1) | copy-start | bytes 3145732
  108.7 7.9 %copy-start.1 = (bf16[2,2048,1024]{2,1,0:T(8,128)(2,1)S(1)}, bf16[2,2048,1024]{2,1,0:T(8,128)(2,1)}, u32[]{:S(2)}) copy-start(bf16[2,2048,1024]{2,1,0:T(8,128)(2,1)} %all-gather.2.cloned.1.call-done) | copy-start | bytes 25165828
  108.7 7.9 %copy-start.2 = (f32[1024]{0:T(1024)S(1)}, f32[1024]{0:T(1024)}, u32[]{:S(2)}) copy-start(f32[1024]{0:T(1024)} %param.16) | copy-start | bytes 12292
Sparse Core Ops, SparseCore 0:
  18.8 60.3 all-gather.1

commit v10 on v8

--- a/solution.py
+++ b/solution.py
@@ -57,28 +57,32 @@
     agents, steps, width = rows_ref.shape
     later = step_of(lax.broadcasted_iota(jnp.int32, (steps, 1), 0), *sizes)
     earlier = step_of(lax.broadcasted_iota(jnp.int32, (1, steps), 1), *sizes)
+    rows = jnp.concatenate([rows_ref[agent].astype(F32) for agent in range(agents)], 0)
+    normed = rms_block(rows, gain_ref[...])
+    queries = linear(normed, qk_ref[0]).astype(BF)
+    keys = linear(normed, qk_ref[1]).astype(BF)
+    values = linear(normed, v_ref[...]).astype(BF)
+    context = []
     for agent in range(agents):
-        rows = rows_ref[agent].astype(F32)
-        normed = rms_block(rows, gain_ref[...])
-        queries = linear(normed, qk_ref[0]).astype(BF)
-        keys = linear(normed, qk_ref[1]).astype(BF)
-        values = linear(normed, v_ref[...]).astype(BF)
         begin = start_ref[agent]
         visible = (later >= earlier) & ((earlier >= begin) | (later < begin))
-        context = []
+        own = slice(agent * steps, (agent + 1) * steps)
+        parts = []
         for h in range(queries.shape[1] // HDIM):
             part = slice(h * HDIM, (h + 1) * HDIM)
             scores = lax.dot_general(
-                queries[:, part], keys[:, part], (((1,), (1,)), ((), ())), preferred_element_type=F32
+                queries[own, part], keys[own, part], (((1,), (1,)), ((), ())), preferred_element_type=F32
             )
             scores = jnp.where(visible, scores, -jnp.inf)
             top = jnp.max(scores, axis=-1, keepdims=True)
             exponent = jnp.exp2((scores - top) * (LOG2E * HDIM ** (-0.5)))
             total = jnp.sum(exponent, axis=-1, keepdims=True)
-            weighted = linear(exponent.astype(BF), values[:, part])
-            context.append((weighted / total).astype(BF))
-        context = jnp.concatenate(context, 1)
-        out_ref[agent] = (rows + linear(context, o_ref[...])).astype(BF)
+            weighted = linear(exponent.astype(BF), values[own, part])
+            parts.append((weighted / total).astype(BF))
+        context.append(jnp.concatenate(parts, 1))
+    result = (rows + linear(jnp.concatenate(context, 0), o_ref[...])).astype(BF)
+    for agent in range(agents):
+        out_ref[agent] = result[agent * steps : (agent + 1) * steps]
 
 
 def time_block(series, sizes, starts, gain, pair, value, out):
@@ -212,9 +216,9 @@
     pair = jnp.where(
         high == 0, jnp.concatenate([mine, other], 1), jnp.concatenate([other, mine], 1)
     )
-    rows, pair = lax.optimization_barrier((rows, pair))
     weights = lax.all_gather(pair, ("c", "x", "y"), axis=1, tiled=True)
     weights = weights.reshape(2, n_core, width, half)
+    rows, other = lax.optimization_barrier((rows, other))
 
     n_dev = lax.axis_size(DEV)
     agents_own = episode_start.shape[0]
@@ -231,7 +235,6 @@
     pieces = after_agents.reshape(n_grp, n_flat, n_high, agents_own, width)
     pieces = jnp.transpose(pieces, (2, 1, 0, 3, 4)).reshape(steps, agents_own, width)
     series = lax.all_to_all(pieces, TURNED + GRP, split_axis=0, concat_axis=0, tiled=True)
-    series, weights = lax.optimization_barrier((series, weights))
     series = jnp.swapaxes(series, 0, 1)
     sizes = (n_flat, n_high, steps_here)
     after_time = time_block(

time: 168 us -> 166 us (0.988)
  blocking collectives: 84.4 us -> 111 us
  waiting for transfers between devices: 28.9 us -> 3.64 us
  starting transfers between devices: 11 us -> 5.93 us
  local copies, waits for them, and re-layouts: 3.77 us -> 7.34 us
    all_to_all x0 -> x1, blocking collectives: none -> 30.5 us  [on_device(): rows = lax.all_to_all(rollout, GRP, split_axis=0, concat_axis=0, tiled=True)]
    ppermute x1, waiting for transfers between devices: 18 us -> 3.61 us  [other_half(): return lax.ppermute(block, ('zl', 'h'), mirror)]
    all_gather x1, waiting for transfers between devices: 10.9 us -> 0.02 us  [on_device(): weights = lax.all_gather(pair, ('c', 'x', 'y'), axis=1, tiled=True)]
    all_to_all x1 -> x0, starting transfers between devices: 6.14 us -> none  [on_device(): rows = lax.all_to_all(rollout, GRP, split_axis=0, concat_axis=0, tiled=True)]
    unnamed x26 -> x22, local copies, waits for them, and re-layouts: 0.59 us -> 3.78 us
    all_to_all x1, blocking collectives: 39.9 us -> 37.3 us  [on_device(): lax.all_to_all(result, TURNED, split_axis=0, concat_axis=0, tiled=True)]
    another operation x2, local copies, waits for them, and re-layouts: 0.03 us -> 1.78 us  [on_device(): mine = jnp.stack([up, down])]
  transfers between devices with their start and end apart: 3 -> 2, of which waited for: 2 -> 1; matrix products, arithmetic and copies ran while one was open for 7% -> 6% of each run, Pallas kernels for 0% -> 4%
where the time goes in v10:
time: 166 us
  blocking collectives  111 us (67%)
  Pallas kernels  15.6 us (9%)
  between operations  13.6 us (8%)
  local copies, waits for them, and re-layouts  7.34 us (4%)
  matrix products  6.21 us (4%)
  starting transfers between devices  5.93 us (4%)
  waiting for transfers between devices  3.64 us (2%)
  other arithmetic  2.45 us (1%)
    all_to_all x1, blocking collectives, on_device(): lax.all_to_all(pieces, TURNED + GRP, split_axis=0, concat_axis=0, tiled=T...  43.4 us
    all_to_all x1, blocking collectives, on_device(): lax.all_to_all(result, TURNED, split_axis=0, concat_axis=0, tiled=True)  37.3 us
    all_to_all x1, blocking collectives, on_device(): rows = lax.all_to_all(rollout, GRP, split_axis=0, concat_axis=0, tiled=True)  30.5 us
    pallas_call x1, Pallas kernels, time_block(): pl.pallas_call(functools.partial(time_kernel, sizes), out_shape=jax.Shape...  7.4 us
    pallas_call x1, Pallas kernels, ff_block(): pl.pallas_call(ff_kernel, grid=(halves * n,), out_shape=jax.ShapeDtypeStr...  6.53 us
    ppermute x1, starting transfers between devices, other_half(): return lax.ppermute(block, ('zl', 'h'), mirror)  5.93 us
    unnamed x22, local copies, waits for them, and re-layouts  3.78 us
    ppermute x1, waiting for transfers between devices, other_half(): return lax.ppermute(block, ('zl', 'h'), mirror)  3.61 us
  transfers between devices with their start and end apart: 2, of which 1 were waited for; matrix products, arithmetic and copies ran while one was open for 6% of the time, Pallas kernels for 4%

profile of v10, /device:TPU:32, one launch (start us, length us, event | category | flops | bytes accessed | tf_op | source)
XLA Modules:
  0.0 166.0 jit_solution(9714259873609110029)
XLA Ops:
  6.5 0.9 dynamic-slice_bitcast_fusion
  7.5 0.8 dynamic-slice_bitcast_fusion.1
  8.3 5.9 %collective-permute-start = (bf16[2,32,1024]{2,1,0:T(8,128)(2,1)S(1)}, bf16[2,32,1024]{2,1,0:T(8,128)(2,1)S(1)}, u32[]{:S(2)}, u32[]{:S(2)}) collective-permute-start(bf16[2,32,1024]{2,1,0:T(8,128)(2,1)S(1)} %pad_maximum_fusion), channel_id=1, source_target_pairs={{0,193},{64,129},{128,65},{192,1},{1,192},{65,128},{129,64},{193,0... | collective-permute-start | bytes 393224 | tf_op jit(solution)/shard_map/ppermute | solution.py:186
  14.3 3.6 %collective-permute-done = bf16[2,32,1024]{2,1,0:T(8,128)(2,1)S(1)} collective-permute-done((bf16[2,32,1024]{2,1,0:T(8,128)(2,1)S(1)}, bf16[2,32,1024]{2,1,0:T(8,128)(2,1)S(1)}, u32[]{:S(2)}, u32[]{:S(2)}) %collective-permute-start) | collective-permute-done | bytes 131104 | tf_op jit(solution)/shard_map/ppermute | solution.py:186
  17.9 0.8 maximum_select_fusion
  18.6 0.0 all-gather.2.cloned.1.call-update
  18.7 30.5 %all_to_all.15 = bf16[8,64,1024]{2,1,0:T(8,128)(2,1)S(1)} all-to-all(bf16[8,64,1024]{2,1,0:T(8,128)(2,1)} %param.13), channel_id=1, replica_groups=mesh['zl'=4,'c'=2,'x'=4,'y'=4,'h'=2] {'zl','c'}, dimensions={0} | all-to-all | bytes 2097152 | tf_op jit(solution)/shard_map/all_to_all | solution.py:214
  49.2 0.3 fusion.6
  49.5 0.9 convolution_convert_fusion.1
  50.3 0.0 copy-start.9
  50.3 0.9 convolution_convert_fusion
  51.2 0.3 copy-done.9
  51.6 0.9 convolution_convert_fusion.2
  52.4 1.3 multiply_reduce_fusion
  53.7 1.4 fusion
  55.1 1.6 divide_convert_fusion
  56.7 0.7 fusion.9
  57.5 0.4 reshape.41
  57.9 1.1 copy.17
  59.0 0.0 copy-start.6
  59.0 0.0 copy-start.3
  59.0 0.0 copy-start.4
  59.0 0.0 copy-start.5
  59.1 0.0 copy-start.7
  59.1 43.4 %all_to_all.16 = bf16[256,2,1024]{2,1,0:T(2,128)(2,1)S(1)} all-to-all(bf16[256,2,1024]{2,1,0:T(2,128)(2,1)S(1)} %bitcast.49), channel_id=1, replica_groups=mesh['zl'=4,'c'=2,'x'=4,'y'=4,'h'=2] {'h','x','y','zl','c'}, dimensions={0} | all-to-all | bytes 2097152 | tf_op jit(solution)/shard_map/all_to_all | solution.py:237
  102.5 0.3 copy.21
  102.8 7.4 %time_attention.1 = bf16[2,256,1024]{2,1,0:T(8,128)(2,1)S(1)} custom-call(s32[2]{0:T(128)S(1)} %copy-done.7, bf16[2,256,1024]{2,1,0:T(8,128)(2,1)S(1)} %bitcast.40, f32[1,1024]{1,0:T(1,128)S(1)} %bitcast.42, bf16[2,1024,512]{2,1,0:T(8,128)(2,1)S(1)} %copy-done.3, bf16[1024,512]{1,0:T(8,128)(2,1)S(1)} %copy-done.4, bf16[512,1024]{1,0:T(8,128)(2,1)S(1)} %copy-done.5), custom_call_target="tpu_custom_call" | custom-call | flops 3221225472 | bytes 6291456 | tf_op jit(solution)/shard_map/time_attention/pallas_call | solution.py:91
  110.2 0.0 all-gather.2.cloned.1.call-done
  110.3 3.4 %copy-done.1 = bf16[2,2048,1024]{2,1,0:T(8,128)(2,1)S(1)} copy-done((bf16[2,2048,1024]{2,1,0:T(8,128)(2,1)S(1)}, bf16[2,2048,1024]{2,1,0:T(8,128)(2,1)}, u32[]{:S(2)}) %copy-start.1) | copy-done | bytes 8388632
  113.7 6.5 %feed_forward.1 = bf16[32,2,8,1024]{3,2,1,0:T(8,128)(2,1)S(1)} custom-call(bf16[512,1024]{1,0:T(8,128)(2,1)S(1)} %bitcast.39, f32[1,1024]{1,0:T(1,128)S(1)} %bitcast.41, bf16[2,2,1024,1024]{3,2,1,0:T(8,128)(2,1)S(1)} %bitcast.37, bf16[2,2,1024,1024]{3,2,1,0:T(8,128)(2,1)S(1)} %bitcast.38), custom_call_target="tpu_custom_call" | custom-call | flops 4294967296 | bytes 10485760 | tf_op jit(solution)/shard_map/feed_forward/pallas_call | solution.py:138
  120.2 37.3 %all_to_all.17.rows_ref = bf16[32,2,8,1024]{3,2,1,0:T(8,128)(2,1)S(1)} all-to-all(bf16[32,2,8,1024]{3,2,1,0:T(8,128)(2,1)S(1)} %feed_forward.1), channel_id=1, replica_groups=mesh['zl'=4,'c'=2,'x'=4,'y'=4,'h'=2] {'h','x','y'}, dimensions={0} | all-to-all | bytes 2097152 | tf_op jit(solution)/shard_map/all_to_all | solution.py:245
  157.5 1.7 %reorder.1 = bf16[8,64,1024]{2,1,0:T(8,128)(2,1)} custom-call(bf16[32,2,8,1024]{3,2,1,0:T(8,128)(2,1)S(1)} %all_to_all.17.rows_ref), custom_call_target="tpu_custom_call" | custom-call | flops 536870912 | bytes 2097152 | tf_op jit(solution)/shard_map/reorder/pallas_call | solution.py:171
  (17 shorter events, 0.1 us)
Async XLA Ops:
  6.5 50.2 %copy-start = (bf16[512,1024]{1,0:T(8,128)(2,1)S(1)}, bf16[512,1024]{1,0:T(8,128)(2,1)}, u32[]{:S(2)}) copy-start(bf16[512,1024]{1,0:T(8,128)(2,1)} %param.19) | copy-start | bytes 3145732
  6.5 103.7 %all-gather.2.cloned.1.call-start = ((), (), s32[]{:S(2)}) async-start(), calls=%async_computation.3 | async-start | bytes 8650752 | tf_op jit(solution)/shard_map/all_gather | solution.py:219
  8.3 41.1 %copy-start.8 = (bf16[2,1024,512]{2,1,0:T(8,128)(2,1)S(1)}, bf16[2,1024,512]{2,1,0:T(8,128)(2,1)}, u32[]{:S(2)}) copy-start(bf16[2,1024,512]{2,1,0:T(8,128)(2,1)} %param.17) | copy-start | bytes 6291460
  8.3 41.1 %copy-start.10 = (f32[1024]{0:T(1024)S(1)}, f32[1024]{0:T(1024)}, u32[]{:S(2)}) copy-start(f32[1024]{0:T(1024)} %param.14) | copy-start | bytes 12292
  8.3 9.5 %collective-permute-start = (bf16[2,32,1024]{2,1,0:T(8,128)(2,1)S(1)}, bf16[2,32,1024]{2,1,0:T(8,128)(2,1)S(1)}, u32[]{:S(2)}, u32[]{:S(2)}) collective-permute-start(bf16[2,32,1024]{2,1,0:T(8,128)(2,1)S(1)} %pad_maximum_fusion), channel_id=1, source_target_pairs={{0,193},{64,129},{128,65},{192,1},{1,192},{65,128},{129,64},{193,0... | collective-permute-start | bytes 393224 | tf_op jit(solution)/shard_map/ppermute | solution.py:186
  50.3 1.2 copy-start.9
  59.0 43.8 %copy-start.6 = (f32[1024]{0:T(1024)S(1)}, f32[1024]{0:T(1024)}, u32[]{:S(2)}) copy-start(f32[1024]{0:T(1024)} %param.15) | copy-start | bytes 12292
  59.0 43.8 %copy-start.3 = (bf16[2,1024,512]{2,1,0:T(8,128)(2,1)S(1)}, bf16[2,1024,512]{2,1,0:T(8,128)(2,1)}, u32[]{:S(2)}) copy-start(bf16[2,1024,512]{2,1,0:T(8,128)(2,1)} %qk_ref.1) | copy-start | bytes 6291460
  59.0 43.8 %copy-start.4 = (bf16[1024,512]{1,0:T(8,128)(2,1)S(1)}, bf16[1024,512]{1,0:T(8,128)(2,1)}, u32[]{:S(2)}) copy-start(bf16[1024,512]{1,0:T(8,128)(2,1)} %v_ref.1) | copy-start | bytes 3145732
  59.0 43.8 %copy-start.5 = (bf16[512,1024]{1,0:T(8,128)(2,1)S(1)}, bf16[512,1024]{1,0:T(8,128)(2,1)}, u32[]{:S(2)}) copy-start(bf16[512,1024]{1,0:T(8,128)(2,1)} %o_ref.1) | copy-start | bytes 3145732
  59.1 43.8 %copy-start.7 = (s32[2]{0:T(128)S(1)}, s32[2]{0:T(128)}, u32[]{:S(2)}) copy-start(s32[2]{0:T(128)} %start_ref.1) | copy-start | bytes 28
  102.8 7.4 %copy-start.2 = (f32[1024]{0:T(1024)S(1)}, f32[1024]{0:T(1024)}, u32[]{:S(2)}) copy-start(f32[1024]{0:T(1024)} %param.16) | copy-start | bytes 12292
  110.3 3.4 %copy-start.1 = (bf16[2,2048,1024]{2,1,0:T(8,128)(2,1)S(1)}, bf16[2,2048,1024]{2,1,0:T(8,128)(2,1)}, u32[]{:S(2)}) copy-start(bf16[2,2048,1024]{2,1,0:T(8,128)(2,1)} %all-gather.2.cloned.1.call-done) | copy-start | bytes 25165828
Sparse Core Ops, SparseCore 0:
  18.8 62.8 all-gather.1

commit v11 on v10

--- a/solution.py
+++ b/solution.py
@@ -104,48 +104,53 @@
     return (0.5 * x) * (1.0 + jnp.tanh(inner))
 
 
-def ff_kernel(rows_ref, gain_ref, up_ref, down_ref, out_ref, inner, total):
-    step, last = pl.program_id(0), pl.num_programs(0) - 1
-
-    @pl.when(step == 0)
-    def _():
-        rows = rows_ref[...].astype(F32)
-        inner[...] = rms_block(rows, gain_ref[...])
-        total[...] = rows
-
-    hidden = gelu(linear(inner[...], up_ref[0, 0])).astype(BF)
-    total[...] += lax.dot_general(
-        hidden, down_ref[0, 0], (((1,), (1,)), ((), ())), preferred_element_type=F32
-    )
-
-    @pl.when(step == last)
-    def _():
-        blocks, agents, block, width = out_ref.shape
-        for agent in range(agents):
-            part = total[agent * blocks * block : (agent + 1) * blocks * block]
-            out_ref[:, agent] = part.reshape(blocks, block, width).astype(BF)
+def ff_kernel(rows_ref, gain_ref, weights_ref, out_ref, held, arrived):
+    halves, width, half = weights_ref.shape[1:]
+    size = half // 2
+    parts = [(i, j) for i in range(halves) for j in range(half // size)]
+
+    def fetch(n, which):
+        i, j = parts[n]
+        source = weights_ref.at[which, i, :, pl.ds(j * size, size)]
+        return pltpu.make_async_copy(source, held.at[n, which], arrived.at[n, which])
+
+    fetch(0, 0).start()
+    fetch(0, 1).start()
+    total = rows_ref[...].astype(F32)
+    inner = rms_block(total, gain_ref[...])
+    for n in range(len(parts)):
+        fetch(n, 0).wait()
+        if n + 1 < len(parts):
+            fetch(n + 1, 0).start()
+            fetch(n + 1, 1).start()
+        hidden = gelu(linear(inner, held[n, 0])).astype(BF)
+        fetch(n, 1).wait()
+        total = total + lax.dot_general(
+            hidden, held[n, 1], (((1,), (1,)), ((), ())), preferred_element_type=F32
+        )
+    blocks, agents, block, _ = out_ref.shape
+    for agent in range(agents):
+        part = total[agent * blocks * block : (agent + 1) * blocks * block]
+        out_ref[:, agent] = part.reshape(blocks, block, width).astype(BF)
 
 
 def ff_block(rows, gain, weights, shape):
     rows = rows.reshape(-1, rows.shape[-1])
-    count, width = rows.shape
-    halves, half = weights.shape[1], weights.shape[3]
-    size = 512
-    n = half // size
-    whole = pl.BlockSpec((count, width), lambda i: (0, 0))
-    up = pl.BlockSpec((1, 1, width, size), lambda i: (0, i // n, 0, i % n))
-    down = pl.BlockSpec((1, 1, width, size), lambda i: (1, i // n, 0, i % n))
+    halves, width, half = weights.shape[1:]
+    vmem = pl.BlockSpec(memory_space=pltpu.VMEM)
     return pl.pallas_call(
         ff_kernel,
-        grid=(halves * n,),
         out_shape=jax.ShapeDtypeStruct(shape, BF),
-        in_specs=[whole, pl.BlockSpec((1, width), lambda i: (0, 0)), up, down],
-        out_specs=pl.BlockSpec(shape, lambda i: (0, 0, 0, 0)),
-        scratch_shapes=[pltpu.VMEM((count, width), BF), pltpu.VMEM((count, width), F32)],
-        compiler_params=pltpu.CompilerParams(vmem_limit_bytes=28 << 20),
+        in_specs=[vmem, vmem, pl.BlockSpec(memory_space=pltpu.HBM)],
+        out_specs=vmem,
+        scratch_shapes=[
+            pltpu.VMEM((2 * halves, 2, width, half // 2), BF),
+            pltpu.SemaphoreType.DMA((2 * halves, 2)),
+        ],
+        compiler_params=pltpu.CompilerParams(vmem_limit_bytes=50 << 20),
         cost_estimate=pl.CostEstimate(flops=4 << 30, bytes_accessed=10 << 20, transcendentals=1 << 20),
         name="feed_forward",
-    )(rows, gain[None, :], weights, weights)
+    )(rows, gain[None, :], weights)
 
 
 def pick(places, rows):
@@ -216,9 +221,9 @@
     pair = jnp.where(
         high == 0, jnp.concatenate([mine, other], 1), jnp.concatenate([other, mine], 1)
     )
+    rows, pair = lax.optimization_barrier((rows, pair))
     weights = lax.all_gather(pair, ("c", "x", "y"), axis=1, tiled=True)
     weights = weights.reshape(2, n_core, width, half)
-    rows, other = lax.optimization_barrier((rows, other))
 
     n_dev = lax.axis_size(DEV)
     agents_own = episode_start.shape[0]

time: 166 us -> 160 us (0.964)
  blocking collectives: 111 us -> 84.3 us
  waiting for transfers between devices: 3.64 us -> 21.3 us
  local copies, waits for them, and re-layouts: 7.34 us -> 2.24 us
  starting transfers between devices: 5.93 us -> 11 us
    all_to_all x1 -> x0, blocking collectives: 30.5 us -> none  [on_device(): rows = lax.all_to_all(rollout, GRP, split_axis=0, concat_axis=0, tiled=True)]
    ppermute x1, waiting for transfers between devices: 3.61 us -> 18 us  [other_half(): return lax.ppermute(block, ('zl', 'h'), mirror)]
    all_to_all x0 -> x1, starting transfers between devices: none -> 6.14 us  [on_device(): rows = lax.all_to_all(rollout, GRP, split_axis=0, concat_axis=0, tiled=True)]
    unnamed x22 -> x24, local copies, waits for them, and re-layouts: 3.78 us -> 0.43 us
    all_gather x1, waiting for transfers between devices: 0.02 us -> 3.28 us  [on_device(): weights = lax.all_gather(pair, ('c', 'x', 'y'), axis=1, tiled=True)]
    all_to_all x1, blocking collectives: 37.3 us -> 39.9 us  [on_device(): lax.all_to_all(result, TURNED, split_axis=0, concat_axis=0, tiled=True)]
    another operation x2, local copies, waits for them, and re-layouts: 1.78 us -> 0.03 us  [on_device(): mine = jnp.stack([up, down])]
  transfers between devices with their start and end apart: 2 -> 3, of which waited for: 1 -> 2; matrix products, arithmetic and copies ran while one was open for 6% -> 7% of each run, Pallas kernels for 4% -> 5%
where the time goes in v11:
time: 160 us
  blocking collectives  84.3 us (53%)
  waiting for transfers between devices  21.3 us (13%)
  Pallas kernels  17.1 us (11%)
  between operations  13.6 us (8%)
  starting transfers between devices  11 us (7%)
  matrix products  7.53 us (5%)
  other arithmetic  2.45 us (2%)
  local copies, waits for them, and re-layouts  2.24 us (1%)
    all_to_all x1, blocking collectives, on_device(): lax.all_to_all(pieces, TURNED + GRP, split_axis=0, concat_axis=0, tiled=T...  44.4 us
    all_to_all x1, blocking collectives, on_device(): lax.all_to_all(result, TURNED, split_axis=0, concat_axis=0, tiled=True)  39.9 us
    ppermute x1, waiting for transfers between devices, other_half(): return lax.ppermute(block, ('zl', 'h'), mirror)  18 us
    pallas_call x1, Pallas kernels, ff_block(): pl.pallas_call(ff_kernel, out_shape=jax.ShapeDtypeStruct(shape, BF), in_s...  7.91 us
    pallas_call x1, Pallas kernels, time_block(): pl.pallas_call(functools.partial(time_kernel, sizes), out_shape=jax.Shape...  7.47 us
    all_to_all x1, starting transfers between devices, on_device(): rows = lax.all_to_all(rollout, GRP, split_axis=0, concat_axis=0, tiled=True)  6.14 us
    ppermute x1, starting transfers between devices, other_half(): return lax.ppermute(block, ('zl', 'h'), mirror)  4.86 us
    dot_general x4, matrix products, linear(): return jnp.dot(rows, weight, preferred_element_type=F32)  4.65 us
  transfers between devices with their start and end apart: 3, of which 2 were waited for; matrix products, arithmetic and copies ran while one was open for 7% of the time, Pallas kernels for 5%

profile of v11, /device:TPU:32, one launch (start us, length us, event | category | flops | bytes accessed | tf_op | source)
XLA Modules:
  0.0 159.6 jit_solution(16633438431978153259)
XLA Ops:
  6.5 6.1 %all-to-all-start = ((bf16[8,64,1024]{2,1,0:T(8,128)(2,1)}), bf16[8,64,1024]{2,1,0:T(8,128)(2,1)S(1)}, u32[]{:S(2)}, u32[]{:S(2)}) async-start(bf16[8,64,1024]{2,1,0:T(8,128)(2,1)} %param.13), calls=%async_computation | async-start | bytes 2097152 | tf_op jit(solution)/shard_map/all_to_all | solution.py:219
  12.8 4.9 %collective-permute-start = (bf16[2,32,1024]{2,1,0:T(8,128)(2,1)S(1)}, bf16[2,32,1024]{2,1,0:T(8,128)(2,1)S(1)}, u32[]{:S(2)}, u32[]{:S(2)}) collective-permute-start(bf16[2,32,1024]{2,1,0:T(8,128)(2,1)S(1)} %pad_maximum_fusion), channel_id=1, source_target_pairs={{0,193},{64,129},{128,65},{192,1},{1,192},{65,128},{129,64},{193,0... | collective-permute-start | bytes 393224 | tf_op jit(solution)/shard_map/ppermute | solution.py:191
  17.6 18.0 %collective-permute-done = bf16[2,32,1024]{2,1,0:T(8,128)(2,1)S(1)} collective-permute-done((bf16[2,32,1024]{2,1,0:T(8,128)(2,1)S(1)}, bf16[2,32,1024]{2,1,0:T(8,128)(2,1)S(1)}, u32[]{:S(2)}, u32[]{:S(2)}) %collective-permute-start) | collective-permute-done | bytes 131104 | tf_op jit(solution)/shard_map/ppermute | solution.py:191
  35.7 0.8 maximum_select_fusion
  36.4 0.0 all-to-all-done
  36.4 0.0 all-gather.2.cloned.1.call-update
  36.4 0.3 fusion.6
  36.7 0.0 copy-start.9
  36.8 2.2 %convolution_convert_fusion = bf16[512,512]{0,1:T(8,128)(2,1)S(1)} fusion(bf16[2,1024,512]{2,1,0:T(8,128)(2,1)} %param.17, bf16[512,1024]{1,0:T(8,128)(2,1)S(1)} %bitcast.42, f32[1024]{0:T(1024)S(1)} %copy-done.11, f32[512]{0:T(512)S(1)} %add_rsqrt_fusion), kind=kOutput, calls=%fused_computation.15 | convolution fusion | flops 539230208 | bytes 2627584 | tf_op jit(solution)/shard_map/dot_general | solution.py:25
  39.0 0.0 copy-start.10
  39.0 0.8 convolution_convert_fusion.1
  39.9 0.4 copy-done.10
  40.2 0.8 convolution_convert_fusion.2
  41.1 1.3 multiply_reduce_fusion
  42.4 1.4 fusion
  43.8 1.6 divide_convert_fusion
  45.4 0.8 fusion.9
  46.1 0.4 reshape.41
  46.6 1.1 copy.17
  47.7 0.0 copy-start.4
  47.7 0.0 copy-start.1
  47.7 0.0 copy-start.2
  47.7 0.0 copy-start.3
  47.7 0.0 copy-start.6
  47.7 44.4 %all_to_all.15 = bf16[256,2,1024]{2,1,0:T(2,128)(2,1)S(1)} all-to-all(bf16[256,2,1024]{2,1,0:T(2,128)(2,1)S(1)} %bitcast.47), channel_id=1, replica_groups=mesh['zl'=4,'c'=2,'x'=4,'y'=4,'h'=2] {'h','x','y','zl','c'}, dimensions={0} | all-to-all | bytes 2097152 | tf_op jit(solution)/shard_map/all_to_all | solution.py:242
  92.1 0.3 copy.21
  92.4 0.0 copy-start.5
  92.5 7.5 %time_attention.1 = bf16[2,256,1024]{2,1,0:T(8,128)(2,1)S(1)} custom-call(s32[2]{0:T(128)S(1)} %copy-done.6, bf16[2,256,1024]{2,1,0:T(8,128)(2,1)S(1)} %bitcast.37, f32[1,1024]{1,0:T(1,128)S(1)} %bitcast.38, bf16[2,1024,512]{2,1,0:T(8,128)(2,1)S(1)} %copy-done.1, bf16[1024,512]{1,0:T(8,128)(2,1)S(1)} %copy-done.2, bf16[512,1024]{1,0:T(8,128)(2,1)S(1)} %copy-done.3), custom_call_target="tpu_custom_call" | custom-call | flops 3221225472 | bytes 6291456 | tf_op jit(solution)/shard_map/time_attention/pallas_call | solution.py:91
  99.9 3.3 %all-gather.2.cloned.1.call-done = bf16[2,2048,1024]{2,1,0:T(8,128)(2,1)} async-done(((bf16[2,64,1024]{2,1,0:T(8,128)(2,1)}), bf16[2,2048,1024]{2,1,0:T(8,128)(2,1)}) %all-gather.2.cloned.1.call-update) | async-done | bytes 8388624 | tf_op jit(solution)/shard_map/all_gather | solution.py:225
  103.2 7.9 %feed_forward.1 = bf16[32,2,8,1024]{3,2,1,0:T(8,128)(2,1)S(1)} custom-call(bf16[512,1024]{1,0:T(8,128)(2,1)S(1)} %bitcast.40, f32[1,1024]{1,0:T(1,128)S(1)} %bitcast.39, bf16[2,2,1024,1024]{3,2,1,0:T(8,128)(2,1)} %bitcast.51), custom_call_target="tpu_custom_call" | custom-call | flops 4294967296 | bytes 10485760 | tf_op jit(solution)/shard_map/feed_forward/pallas_call | solution.py:141
  111.1 39.9 %all_to_all.16.rows_ref = bf16[32,2,8,1024]{3,2,1,0:T(8,128)(2,1)S(1)} all-to-all(bf16[32,2,8,1024]{3,2,1,0:T(8,128)(2,1)S(1)} %feed_forward.1), channel_id=1, replica_groups=mesh['zl'=4,'c'=2,'x'=4,'y'=4,'h'=2] {'h','x','y'}, dimensions={0} | all-to-all | bytes 2097152 | tf_op jit(solution)/shard_map/all_to_all | solution.py:250
  151.1 1.7 %reorder.1 = bf16[8,64,1024]{2,1,0:T(8,128)(2,1)} custom-call(bf16[32,2,8,1024]{3,2,1,0:T(8,128)(2,1)S(1)} %all_to_all.16.rows_ref), custom_call_target="tpu_custom_call" | custom-call | flops 536870912 | bytes 2097152 | tf_op jit(solution)/shard_map/reorder/pallas_call | solution.py:176
  (20 shorter events, 0.1 us)
Async XLA Ops:
  6.5 38.8 %copy-start = (bf16[512,1024]{1,0:T(8,128)(2,1)S(1)}, bf16[512,1024]{1,0:T(8,128)(2,1)}, u32[]{:S(2)}) copy-start(bf16[512,1024]{1,0:T(8,128)(2,1)} %param.19) | copy-start | bytes 3145732
  6.5 6.2 %copy-start.7 = (bf16[2048,32]{0,1:T(8,128)(2,1)S(1)}, bf16[2048,32]{0,1:T(8,128)(2,1)}, u32[]{:S(2)}) copy-start(bf16[2048,32]{0,1:T(8,128)(2,1)} %param.24) | copy-start | bytes 393220
  6.5 6.2 %copy-start.8 = (bf16[32,2048]{1,0:T(8,128)(2,1)S(1)}, bf16[32,2048]{1,0:T(8,128)(2,1)}, u32[]{:S(2)}) copy-start(bf16[32,2048]{1,0:T(8,128)(2,1)} %param.23) | copy-start | bytes 393220
  6.5 30.2 %copy-start.11 = (f32[1024]{0:T(1024)S(1)}, f32[1024]{0:T(1024)}, u32[]{:S(2)}) copy-start(f32[1024]{0:T(1024)} %param.14) | copy-start | bytes 12292
  6.5 29.9 %all-to-all-start = ((bf16[8,64,1024]{2,1,0:T(8,128)(2,1)}), bf16[8,64,1024]{2,1,0:T(8,128)(2,1)S(1)}, u32[]{:S(2)}, u32[]{:S(2)}) async-start(bf16[8,64,1024]{2,1,0:T(8,128)(2,1)} %param.13), calls=%async_computation | async-start | bytes 2097152 | tf_op jit(solution)/shard_map/all_to_all | solution.py:219
  12.7 90.5 %all-gather.2.cloned.1.call-start = ((), (), s32[]{:S(2)}) async-start(), calls=%async_computation.3 | async-start | bytes 8650752 | tf_op jit(solution)/shard_map/all_gather | solution.py:225
  12.8 22.9 %collective-permute-start = (bf16[2,32,1024]{2,1,0:T(8,128)(2,1)S(1)}, bf16[2,32,1024]{2,1,0:T(8,128)(2,1)S(1)}, u32[]{:S(2)}, u32[]{:S(2)}) collective-permute-start(bf16[2,32,1024]{2,1,0:T(8,128)(2,1)S(1)} %pad_maximum_fusion), channel_id=1, source_target_pairs={{0,193},{64,129},{128,65},{192,1},{1,192},{65,128},{129,64},{193,0... | collective-permute-start | bytes 393224 | tf_op jit(solution)/shard_map/ppermute | solution.py:191
  36.7 2.2 %copy-start.9 = (bf16[2,1024,512]{2,1,0:T(8,128)(2,1)S(1)}, bf16[2,1024,512]{2,1,0:T(8,128)(2,1)}, u32[]{:S(2)}) copy-start(bf16[2,1024,512]{2,1,0:T(8,128)(2,1)} %param.17) | copy-start | bytes 6291460
  39.0 1.2 copy-start.10
  47.7 44.7 %copy-start.4 = (f32[1024]{0:T(1024)S(1)}, f32[1024]{0:T(1024)}, u32[]{:S(2)}) copy-start(f32[1024]{0:T(1024)} %param.15) | copy-start | bytes 12292
  47.7 44.7 %copy-start.1 = (bf16[2,1024,512]{2,1,0:T(8,128)(2,1)S(1)}, bf16[2,1024,512]{2,1,0:T(8,128)(2,1)}, u32[]{:S(2)}) copy-start(bf16[2,1024,512]{2,1,0:T(8,128)(2,1)} %qk_ref.1) | copy-start | bytes 6291460
  47.7 44.7 %copy-start.2 = (bf16[1024,512]{1,0:T(8,128)(2,1)S(1)}, bf16[1024,512]{1,0:T(8,128)(2,1)}, u32[]{:S(2)}) copy-start(bf16[1024,512]{1,0:T(8,128)(2,1)} %v_ref.1) | copy-start | bytes 3145732
  47.7 44.7 %copy-start.3 = (bf16[512,1024]{1,0:T(8,128)(2,1)S(1)}, bf16[512,1024]{1,0:T(8,128)(2,1)}, u32[]{:S(2)}) copy-start(bf16[512,1024]{1,0:T(8,128)(2,1)} %o_ref.1) | copy-start | bytes 3145732
  47.7 44.7 %copy-start.6 = (s32[2]{0:T(128)S(1)}, s32[2]{0:T(128)}, u32[]{:S(2)}) copy-start(s32[2]{0:T(128)} %start_ref.1) | copy-start | bytes 28
  92.4 10.8 %copy-start.5 = (f32[1024]{0:T(1024)S(1)}, f32[1024]{0:T(1024)}, u32[]{:S(2)}) copy-start(f32[1024]{0:T(1024)} %param.16) | copy-start | bytes 12292
Sparse Core Ops, SparseCore 0:
  36.6 66.5 all-gather.1

commit v12 on v11

--- a/solution.py
+++ b/solution.py
@@ -105,13 +105,13 @@
 
 
 def ff_kernel(rows_ref, gain_ref, weights_ref, out_ref, held, arrived):
-    halves, width, half = weights_ref.shape[1:]
-    size = half // 2
+    halves, shards, _, depth, half = weights_ref.shape
+    width, size = shards * depth, half // 2
     parts = [(i, j) for i in range(halves) for j in range(half // size)]
 
     def fetch(n, which):
         i, j = parts[n]
-        source = weights_ref.at[which, i, :, pl.ds(j * size, size)]
+        source = weights_ref.at[i, :, which, :, pl.ds(j * size, size)]
         return pltpu.make_async_copy(source, held.at[n, which], arrived.at[n, which])
 
     fetch(0, 0).start()
@@ -123,10 +123,13 @@
         if n + 1 < len(parts):
             fetch(n + 1, 0).start()
             fetch(n + 1, 1).start()
-        hidden = gelu(linear(inner, held[n, 0])).astype(BF)
+        hidden = gelu(linear(inner, held[n, 0].reshape(width, size))).astype(BF)
         fetch(n, 1).wait()
         total = total + lax.dot_general(
-            hidden, held[n, 1], (((1,), (1,)), ((), ())), preferred_element_type=F32
+            hidden,
+            held[n, 1].reshape(width, size),
+            (((1,), (1,)), ((), ())),
+            preferred_element_type=F32,
         )
     blocks, agents, block, _ = out_ref.shape
     for agent in range(agents):
@@ -136,7 +139,7 @@
 
 def ff_block(rows, gain, weights, shape):
     rows = rows.reshape(-1, rows.shape[-1])
-    halves, width, half = weights.shape[1:]
+    halves, shards, _, depth, half = weights.shape
     vmem = pl.BlockSpec(memory_space=pltpu.VMEM)
     return pl.pallas_call(
         ff_kernel,
@@ -144,7 +147,7 @@
         in_specs=[vmem, vmem, pl.BlockSpec(memory_space=pltpu.HBM)],
         out_specs=vmem,
         scratch_shapes=[
-            pltpu.VMEM((2 * halves, 2, width, half // 2), BF),
+            pltpu.VMEM((2 * halves, 2, shards, depth, half // 2), BF),
             pltpu.SemaphoreType.DMA((2 * halves, 2)),
         ],
         compiler_params=pltpu.CompilerParams(vmem_limit_bytes=50 << 20),
@@ -222,8 +225,8 @@
         high == 0, jnp.concatenate([mine, other], 1), jnp.concatenate([other, mine], 1)
     )
     rows, pair = lax.optimization_barrier((rows, pair))
-    weights = lax.all_gather(pair, ("c", "x", "y"), axis=1, tiled=True)
-    weights = weights.reshape(2, n_core, width, half)
+    weights = lax.all_gather(pair[None], ("c", "x", "y"), axis=0, tiled=True)
+    weights = weights.reshape(n_core, -1, 2, pair.shape[1], half)
 
     n_dev = lax.axis_size(DEV)
     agents_own = episode_start.shape[0]

time: 160 us -> 160 us (level)
  no operation moved by 1% of the time
where the time goes in v12:
time: 160 us
  blocking collectives  84.3 us (53%)
  waiting for transfers between devices  21.4 us (13%)
  Pallas kernels  17.1 us (11%)
  between operations  13.6 us (8%)
  starting transfers between devices  11 us (7%)
  matrix products  7.53 us (5%)
  other arithmetic  2.45 us (2%)
  local copies, waits for them, and re-layouts  2.24 us (1%)
    all_to_all x1, blocking collectives, on_device(): lax.all_to_all(pieces, TURNED + GRP, split_axis=0, concat_axis=0, tiled=T...  44.4 us
    all_to_all x1, blocking collectives, on_device(): lax.all_to_all(result, TURNED, split_axis=0, concat_axis=0, tiled=True)  39.9 us
    ppermute x1, waiting for transfers between devices, other_half(): return lax.ppermute(block, ('zl', 'h'), mirror)  18 us
    pallas_call x1, Pallas kernels, ff_block(): pl.pallas_call(ff_kernel, out_shape=jax.ShapeDtypeStruct(shape, BF), in_s...  7.92 us
    pallas_call x1, Pallas kernels, time_block(): pl.pallas_call(functools.partial(time_kernel, sizes), out_shape=jax.Shape...  7.45 us
    all_to_all x1, starting transfers between devices, on_device(): rows = lax.all_to_all(rollout, GRP, split_axis=0, concat_axis=0, tiled=True)  6.14 us
    ppermute x1, starting transfers between devices, other_half(): return lax.ppermute(block, ('zl', 'h'), mirror)  4.86 us
    dot_general x4, matrix products, linear(): return jnp.dot(rows, weight, preferred_element_type=F32)  4.65 us
  transfers between devices with their start and end apart: 3, of which 2 were waited for; matrix products, arithmetic and copies ran while one was open for 7% of the time, Pallas kernels for 5%

profile of v12, /device:TPU:32, one launch (start us, length us, event | category | flops | bytes accessed | tf_op | source)
XLA Modules:
  0.0 159.6 jit_solution(16115079517827515642)
XLA Ops:
  6.5 6.1 %all-to-all-start = ((bf16[8,64,1024]{2,1,0:T(8,128)(2,1)}), bf16[8,64,1024]{2,1,0:T(8,128)(2,1)S(1)}, u32[]{:S(2)}, u32[]{:S(2)}) async-start(bf16[8,64,1024]{2,1,0:T(8,128)(2,1)} %param.13), calls=%async_computation | async-start | bytes 2097152 | tf_op jit(solution)/shard_map/all_to_all | solution.py:222
  12.8 4.9 %collective-permute-start = (bf16[2,32,1024]{2,1,0:T(8,128)(2,1)S(1)}, bf16[2,32,1024]{2,1,0:T(8,128)(2,1)S(1)}, u32[]{:S(2)}, u32[]{:S(2)}) collective-permute-start(bf16[2,32,1024]{2,1,0:T(8,128)(2,1)S(1)} %pad_maximum_fusion), channel_id=1, source_target_pairs={{0,193},{64,129},{128,65},{192,1},{1,192},{65,128},{129,64},{193,0... | collective-permute-start | bytes 393224 | tf_op jit(solution)/shard_map/ppermute | solution.py:194
  17.6 18.0 %collective-permute-done = bf16[2,32,1024]{2,1,0:T(8,128)(2,1)S(1)} collective-permute-done((bf16[2,32,1024]{2,1,0:T(8,128)(2,1)S(1)}, bf16[2,32,1024]{2,1,0:T(8,128)(2,1)S(1)}, u32[]{:S(2)}, u32[]{:S(2)}) %collective-permute-start) | collective-permute-done | bytes 131104 | tf_op jit(solution)/shard_map/ppermute | solution.py:194
  35.7 0.8 maximum_select_fusion
  36.4 0.0 all-to-all-done
  36.4 0.0 all-gather.3.cloned.1.call-update
  36.4 0.3 fusion.6
  36.7 0.0 copy-start.9
  36.8 2.2 %convolution_convert_fusion = bf16[512,512]{0,1:T(8,128)(2,1)S(1)} fusion(bf16[2,1024,512]{2,1,0:T(8,128)(2,1)} %param.17, bf16[512,1024]{1,0:T(8,128)(2,1)S(1)} %bitcast.42, f32[1024]{0:T(1024)S(1)} %copy-done.11, f32[512]{0:T(512)S(1)} %add_rsqrt_fusion), kind=kOutput, calls=%fused_computation.15 | convolution fusion | flops 539230208 | bytes 2627584 | tf_op jit(solution)/shard_map/dot_general | solution.py:25
  39.0 0.0 copy-start.10
  39.0 0.8 convolution_convert_fusion.1
  39.9 0.4 copy-done.10
  40.2 0.8 convolution_convert_fusion.2
  41.1 1.3 multiply_reduce_fusion
  42.4 1.4 fusion
  43.8 1.6 divide_convert_fusion
  45.4 0.8 fusion.9
  46.1 0.4 reshape.41
  46.6 1.1 copy.17
  47.7 0.0 copy-start.4
  47.7 0.0 copy-start.1
  47.7 0.0 copy-start.2
  47.7 0.0 copy-start.3
  47.7 0.0 copy-start.6
  47.7 44.4 %all_to_all.15 = bf16[256,2,1024]{2,1,0:T(2,128)(2,1)S(1)} all-to-all(bf16[256,2,1024]{2,1,0:T(2,128)(2,1)S(1)} %bitcast.47), channel_id=1, replica_groups=mesh['zl'=4,'c'=2,'x'=4,'y'=4,'h'=2] {'h','x','y','zl','c'}, dimensions={0} | all-to-all | bytes 2097152 | tf_op jit(solution)/shard_map/all_to_all | solution.py:245
  92.1 0.3 copy.21
  92.4 0.0 copy-start.5
  92.5 7.4 %time_attention.1 = bf16[2,256,1024]{2,1,0:T(8,128)(2,1)S(1)} custom-call(s32[2]{0:T(128)S(1)} %copy-done.6, bf16[2,256,1024]{2,1,0:T(8,128)(2,1)S(1)} %bitcast.37, f32[1,1024]{1,0:T(1,128)S(1)} %bitcast.38, bf16[2,1024,512]{2,1,0:T(8,128)(2,1)S(1)} %copy-done.1, bf16[1024,512]{1,0:T(8,128)(2,1)S(1)} %copy-done.2, bf16[512,1024]{1,0:T(8,128)(2,1)S(1)} %copy-done.3), custom_call_target="tpu_custom_call" | custom-call | flops 3221225472 | bytes 6291456 | tf_op jit(solution)/shard_map/time_attention/pallas_call | solution.py:91
  99.9 3.3 %all-gather.3.cloned.1.call-done = bf16[64,64,1024]{2,1,0:T(8,128)(2,1)} async-done(((bf16[2,64,1024]{2,1,0:T(8,128)(2,1)}), bf16[64,64,1024]{2,1,0:T(8,128)(2,1)}) %all-gather.3.cloned.1.call-update) | async-done | bytes 8388624 | tf_op jit(solution)/shard_map/all_gather | solution.py:228
  103.2 7.9 %feed_forward.1 = bf16[32,2,8,1024]{3,2,1,0:T(8,128)(2,1)S(1)} custom-call(bf16[512,1024]{1,0:T(8,128)(2,1)S(1)} %bitcast.40, f32[1,1024]{1,0:T(1,128)S(1)} %bitcast.39, bf16[2,16,2,64,1024]{4,3,2,1,0:T(8,128)(2,1)} %bitcast.51), custom_call_target="tpu_custom_call" | custom-call | flops 4294967296 | bytes 10485760 | tf_op jit(solution)/shard_map/feed_forward/pallas_call | solution.py:144
  111.1 39.9 %all_to_all.16.rows_ref = bf16[32,2,8,1024]{3,2,1,0:T(8,128)(2,1)S(1)} all-to-all(bf16[32,2,8,1024]{3,2,1,0:T(8,128)(2,1)S(1)} %feed_forward.1), channel_id=1, replica_groups=mesh['zl'=4,'c'=2,'x'=4,'y'=4,'h'=2] {'h','x','y'}, dimensions={0} | all-to-all | bytes 2097152 | tf_op jit(solution)/shard_map/all_to_all | solution.py:253
  151.1 1.7 %reorder.1 = bf16[8,64,1024]{2,1,0:T(8,128)(2,1)} custom-call(bf16[32,2,8,1024]{3,2,1,0:T(8,128)(2,1)S(1)} %all_to_all.16.rows_ref), custom_call_target="tpu_custom_call" | custom-call | flops 536870912 | bytes 2097152 | tf_op jit(solution)/shard_map/reorder/pallas_call | solution.py:179
  (20 shorter events, 0.1 us)
Async XLA Ops:
  6.5 38.8 %copy-start = (bf16[512,1024]{1,0:T(8,128)(2,1)S(1)}, bf16[512,1024]{1,0:T(8,128)(2,1)}, u32[]{:S(2)}) copy-start(bf16[512,1024]{1,0:T(8,128)(2,1)} %param.19) | copy-start | bytes 3145732
  6.5 6.2 %copy-start.7 = (bf16[2048,32]{0,1:T(8,128)(2,1)S(1)}, bf16[2048,32]{0,1:T(8,128)(2,1)}, u32[]{:S(2)}) copy-start(bf16[2048,32]{0,1:T(8,128)(2,1)} %param.24) | copy-start | bytes 393220
  6.5 6.2 %copy-start.8 = (bf16[32,2048]{1,0:T(8,128)(2,1)S(1)}, bf16[32,2048]{1,0:T(8,128)(2,1)}, u32[]{:S(2)}) copy-start(bf16[32,2048]{1,0:T(8,128)(2,1)} %param.23) | copy-start | bytes 393220
  6.5 30.2 %copy-start.11 = (f32[1024]{0:T(1024)S(1)}, f32[1024]{0:T(1024)}, u32[]{:S(2)}) copy-start(f32[1024]{0:T(1024)} %param.14) | copy-start | bytes 12292
  6.5 29.9 %all-to-all-start = ((bf16[8,64,1024]{2,1,0:T(8,128)(2,1)}), bf16[8,64,1024]{2,1,0:T(8,128)(2,1)S(1)}, u32[]{:S(2)}, u32[]{:S(2)}) async-start(bf16[8,64,1024]{2,1,0:T(8,128)(2,1)} %param.13), calls=%async_computation | async-start | bytes 2097152 | tf_op jit(solution)/shard_map/all_to_all | solution.py:222
  12.7 90.5 %all-gather.3.cloned.1.call-start = ((), (), s32[]{:S(2)}) async-start(), calls=%async_computation.3 | async-start | bytes 8650752 | tf_op jit(solution)/shard_map/all_gather | solution.py:228
  12.8 22.9 %collective-permute-start = (bf16[2,32,1024]{2,1,0:T(8,128)(2,1)S(1)}, bf16[2,32,1024]{2,1,0:T(8,128)(2,1)S(1)}, u32[]{:S(2)}, u32[]{:S(2)}) collective-permute-start(bf16[2,32,1024]{2,1,0:T(8,128)(2,1)S(1)} %pad_maximum_fusion), channel_id=1, source_target_pairs={{0,193},{64,129},{128,65},{192,1},{1,192},{65,128},{129,64},{193,0... | collective-permute-start | bytes 393224 | tf_op jit(solution)/shard_map/ppermute | solution.py:194
  36.7 2.2 %copy-start.9 = (bf16[2,1024,512]{2,1,0:T(8,128)(2,1)S(1)}, bf16[2,1024,512]{2,1,0:T(8,128)(2,1)}, u32[]{:S(2)}) copy-start(bf16[2,1024,512]{2,1,0:T(8,128)(2,1)} %param.17) | copy-start | bytes 6291460
  39.0 1.2 copy-start.10
  47.7 44.7 %copy-start.4 = (f32[1024]{0:T(1024)S(1)}, f32[1024]{0:T(1024)}, u32[]{:S(2)}) copy-start(f32[1024]{0:T(1024)} %param.15) | copy-start | bytes 12292
  47.7 44.7 %copy-start.1 = (bf16[2,1024,512]{2,1,0:T(8,128)(2,1)S(1)}, bf16[2,1024,512]{2,1,0:T(8,128)(2,1)}, u32[]{:S(2)}) copy-start(bf16[2,1024,512]{2,1,0:T(8,128)(2,1)} %qk_ref.1) | copy-start | bytes 6291460
  47.7 44.7 %copy-start.2 = (bf16[1024,512]{1,0:T(8,128)(2,1)S(1)}, bf16[1024,512]{1,0:T(8,128)(2,1)}, u32[]{:S(2)}) copy-start(bf16[1024,512]{1,0:T(8,128)(2,1)} %v_ref.1) | copy-start | bytes 3145732
  47.7 44.7 %copy-start.3 = (bf16[512,1024]{1,0:T(8,128)(2,1)S(1)}, bf16[512,1024]{1,0:T(8,128)(2,1)}, u32[]{:S(2)}) copy-start(bf16[512,1024]{1,0:T(8,128)(2,1)} %o_ref.1) | copy-start | bytes 3145732
  47.7 44.7 %copy-start.6 = (s32[2]{0:T(128)S(1)}, s32[2]{0:T(128)}, u32[]{:S(2)}) copy-start(s32[2]{0:T(128)} %start_ref.1) | copy-start | bytes 28
  92.4 10.8 %copy-start.5 = (f32[1024]{0:T(1024)S(1)}, f32[1024]{0:T(1024)}, u32[]{:S(2)}) copy-start(f32[1024]{0:T(1024)} %param.16) | copy-start | bytes 12292
Sparse Core Ops, SparseCore 0:
  36.6 66.5 all-gather.2

commit v13 on v12

--- a/solution.py
+++ b/solution.py
@@ -104,7 +104,7 @@
     return (0.5 * x) * (1.0 + jnp.tanh(inner))
 
 
-def ff_kernel(rows_ref, gain_ref, weights_ref, out_ref, held, arrived):
+def ff_kernel(which_ref, rows_ref, gain_ref, weights_ref, out_ref, held, arrived):
     halves, shards, _, depth, half = weights_ref.shape
     width, size = shards * depth, half // 2
     parts = [(i, j) for i in range(halves) for j in range(half // size)]
@@ -116,7 +116,9 @@
 
     fetch(0, 0).start()
     fetch(0, 1).start()
-    total = rows_ref[...].astype(F32)
+    count = rows_ref.shape[1] // 2
+    here = pl.ds(pl.multiple_of(which_ref[0] * count, count), count)
+    total = jnp.concatenate([rows_ref[a, here].astype(F32) for a in range(rows_ref.shape[0])], 0)
     inner = rms_block(total, gain_ref[...])
     for n in range(len(parts)):
         fetch(n, 0).wait()
@@ -137,14 +139,13 @@
         out_ref[:, agent] = part.reshape(blocks, block, width).astype(BF)
 
 
-def ff_block(rows, gain, weights, shape):
-    rows = rows.reshape(-1, rows.shape[-1])
+def ff_block(rows, gain, weights, which, shape):
     halves, shards, _, depth, half = weights.shape
     vmem = pl.BlockSpec(memory_space=pltpu.VMEM)
     return pl.pallas_call(
         ff_kernel,
         out_shape=jax.ShapeDtypeStruct(shape, BF),
-        in_specs=[vmem, vmem, pl.BlockSpec(memory_space=pltpu.HBM)],
+        in_specs=[pl.BlockSpec(memory_space=pltpu.SMEM), vmem, vmem, pl.BlockSpec(memory_space=pltpu.HBM)],
         out_specs=vmem,
         scratch_shapes=[
             pltpu.VMEM((2 * halves, 2, shards, depth, half // 2), BF),
@@ -153,7 +154,7 @@
         compiler_params=pltpu.CompilerParams(vmem_limit_bytes=50 << 20),
         cost_estimate=pl.CostEstimate(flops=4 << 30, bytes_accessed=10 << 20, transcendentals=1 << 20),
         name="feed_forward",
-    )(rows, gain[None, :], weights)
+    )(which.reshape(1), rows, gain[None, :], weights)
 
 
 def pick(places, rows):
@@ -162,29 +163,31 @@
     return linear(jnp.where(spot == places, 1.0, 0.0).astype(BF), rows)
 
 
-def reorder_kernel(sizes, rows_ref, out_ref):
+def reorder_kernel(sizes, high_ref, own_ref, other_ref, out_ref):
     n_flat, n_high, own, steps = sizes
-    to = lax.broadcasted_iota(jnp.int32, (rows_ref.size // rows_ref.shape[-1], 1), 0)
+    to = lax.broadcasted_iota(jnp.int32, (2 * own_ref.size // own_ref.shape[-1], 1), 0)
     bits = lambda n: n.bit_length() - 1
     agent, to = to & (own - 1), to >> bits(own)
     high, to = to & (n_high - 1), to >> bits(n_high)
     flat, step = to & (n_flat - 1), to >> bits(n_flat)
-    place = ((high * n_flat + flat) * own + agent) * steps + step
-    rows = rows_ref[...].astype(F32).reshape(-1, rows_ref.shape[-1]).astype(BF)
+    place = (((high ^ high_ref[0]) * n_flat + flat) * own + agent) * steps + step
+    width = own_ref.shape[-1]
+    parts = [ref[...].astype(F32).reshape(-1, width) for ref in (own_ref, other_ref)]
+    rows = jnp.concatenate(parts, 0).astype(BF)
     out_ref[...] = pick(place, rows).reshape(out_ref.shape).astype(BF)
 
 
-def reorder(sizes, rows, shape):
+def reorder(sizes, high, own, other, shape):
     vmem = pl.BlockSpec(memory_space=pltpu.VMEM)
     return pl.pallas_call(
         functools.partial(reorder_kernel, sizes),
         out_shape=jax.ShapeDtypeStruct(shape, BF),
-        in_specs=[vmem],
+        in_specs=[pl.BlockSpec(memory_space=pltpu.SMEM), vmem, vmem],
         out_specs=vmem,
         compiler_params=pltpu.CompilerParams(vmem_limit_bytes=16 << 20),
         cost_estimate=pl.CostEstimate(flops=1 << 29, bytes_accessed=2 << 20, transcendentals=0),
         name="reorder",
-    )(rows)
+    )(high.reshape(1), own, other)
 
 
 def other_half(block):
@@ -248,10 +251,13 @@
     after_time = time_block(
         series, sizes, episode_start, time_gain, time_pair, time_value, time_out
     )
-    shape = (n_dev, agents_own, steps_here, width)
-    result = ff_block(after_time, inner_gain, weights, shape)
-    result = lax.all_to_all(result, TURNED, split_axis=0, concat_axis=0, tiled=True)
-    return reorder((n_flat, n_high, agents_own, steps_here), result, rollout.shape)
+    shape = (n_flat, agents_own, steps_here, width)
+    away = ff_block(after_time, inner_gain, weights, 1 - high, shape)
+    away = lax.ppermute(away, "h", [(0, 1), (1, 0)])
+    own = ff_block(after_time, inner_gain, weights, high, shape)
+    own = lax.all_to_all(own, ("x", "y"), split_axis=0, concat_axis=0, tiled=True)
+    away = lax.all_to_all(away, ("x", "y"), split_axis=0, concat_axis=0, tiled=True)
+    return reorder((n_flat, n_high, agents_own, steps_here), high, own, away, rollout.shape)
 
 
 def solution(mesh):

time: 160 us -> 165 us (1.031)
  blocking collectives: 84.3 us -> 31.9 us
  waiting for transfers between devices: 21.4 us -> 49.2 us
  starting transfers between devices: 11 us -> 31.3 us
  local copies, waits for them, and re-layouts: 2.24 us -> 7.12 us
  Pallas kernels: 17.1 us -> 21.6 us
    all_to_all x2, blocking collectives: 84.3 us -> 31.9 us  [the longest x1 16 us: on_device(): lax.all_to_all(own, ('x', 'y'), split_axis=0, concat_axis=0, tiled=True)]
    all_to_all x0 -> x1, waiting for transfers between devices: none -> 29 us  [on_device(): lax.all_to_all(pieces, TURNED + GRP, split_axis=0, concat_axis=0, tiled=T...]
    all_to_all x0 -> x1, starting transfers between devices: none -> 15.7 us  [on_device(): lax.all_to_all(pieces, TURNED + GRP, split_axis=0, concat_axis=0, tiled=T...]
    pallas_call x1 -> x2, Pallas kernels: 7.92 us -> 12.6 us  [ff_block(): pl.pallas_call(ff_kernel, out_shape=jax.ShapeDtypeStruct(shape, BF), in_s...]
    ppermute x0 -> x1, starting transfers between devices: none -> 4.55 us  [on_device(): away = lax.ppermute(away, 'h', [(0, 1), (1, 0)])]
    all_gather x1, waiting for transfers between devices: 3.31 us -> 0.08 us  [on_device(): weights = lax.all_gather(pair[None], ('c', 'x', 'y'), axis=0, tiled=True)]
    unnamed x24 -> x28, local copies, waits for them, and re-layouts: 0.43 us -> 2.92 us
    ppermute x0 -> x1, waiting for transfers between devices: none -> 2.14 us  [on_device(): away = lax.ppermute(away, 'h', [(0, 1), (1, 0)])]
  transfers between devices with their start and end apart: 3 -> 5, of which waited for: 2 -> 4; matrix products, arithmetic and copies ran while one was open for 7% -> 9% of each run, Pallas kernels for 5% -> 8%
where the time goes in v13:
time: 165 us
  waiting for transfers between devices  49.2 us (30%)
  blocking collectives  31.9 us (19%)
  starting transfers between devices  31.3 us (19%)
  Pallas kernels  21.6 us (13%)
  between operations  13.6 us (8%)
  matrix products  7.53 us (5%)
  local copies, waits for them, and re-layouts  7.12 us (4%)
  other arithmetic  2.46 us (1%)
    all_to_all x1, waiting for transfers between devices, on_device(): lax.all_to_all(pieces, TURNED + GRP, split_axis=0, concat_axis=0, tiled=T...  29 us
    ppermute x1, waiting for transfers between devices, other_half(): return lax.ppermute(block, ('zl', 'h'), mirror)  18 us
    all_to_all x1, blocking collectives, on_device(): lax.all_to_all(own, ('x', 'y'), split_axis=0, concat_axis=0, tiled=True)  16 us
    all_to_all x1, blocking collectives, on_device(): lax.all_to_all(away, ('x', 'y'), split_axis=0, concat_axis=0, tiled=True)  15.9 us
    all_to_all x1, starting transfers between devices, on_device(): lax.all_to_all(pieces, TURNED + GRP, split_axis=0, concat_axis=0, tiled=T...  15.7 us
    pallas_call x2, Pallas kernels, ff_block(): pl.pallas_call(ff_kernel, out_shape=jax.ShapeDtypeStruct(shape, BF), in_s...  12.6 us
    pallas_call x1, Pallas kernels, time_block(): pl.pallas_call(functools.partial(time_kernel, sizes), out_shape=jax.Shape...  7.37 us
    all_to_all x1, starting transfers between devices, on_device(): rows = lax.all_to_all(rollout, GRP, split_axis=0, concat_axis=0, tiled=True)  6.14 us
  transfers between devices with their start and end apart: 5, of which 4 were waited for; matrix products, arithmetic and copies ran while one was open for 9% of the time, Pallas kernels for 8%

profile of v13, /device:TPU:32, one launch (start us, length us, event | category | flops | bytes accessed | tf_op | source)
XLA Modules:
  0.0 164.8 jit_solution(3800415521340202047)
XLA Ops:
  6.5 6.1 %all-to-all-start = ((bf16[8,64,1024]{2,1,0:T(8,128)(2,1)}), bf16[8,64,1024]{2,1,0:T(8,128)(2,1)S(1)}, u32[]{:S(2)}, u32[]{:S(2)}) async-start(bf16[8,64,1024]{2,1,0:T(8,128)(2,1)} %param.13), calls=%async_computation | async-start | bytes 2097152 | tf_op jit(solution)/shard_map/all_to_all | solution.py:225
  12.8 4.9 %collective-permute-start = (bf16[2,32,1024]{2,1,0:T(8,128)(2,1)S(1)}, bf16[2,32,1024]{2,1,0:T(8,128)(2,1)S(1)}, u32[]{:S(2)}, u32[]{:S(2)}) collective-permute-start(bf16[2,32,1024]{2,1,0:T(8,128)(2,1)S(1)} %pad_maximum_fusion), channel_id=1, source_target_pairs={{0,193},{64,129},{128,65},{192,1},{1,192},{65,128},{129,64},{193,0... | collective-permute-start | bytes 393224 | tf_op jit(solution)/shard_map/ppermute | solution.py:197
  17.6 18.0 %collective-permute-done = bf16[2,32,1024]{2,1,0:T(8,128)(2,1)S(1)} collective-permute-done((bf16[2,32,1024]{2,1,0:T(8,128)(2,1)S(1)}, bf16[2,32,1024]{2,1,0:T(8,128)(2,1)S(1)}, u32[]{:S(2)}, u32[]{:S(2)}) %collective-permute-start) | collective-permute-done | bytes 131104 | tf_op jit(solution)/shard_map/ppermute | solution.py:197
  35.7 0.8 maximum_select_fusion
  36.4 0.0 all-gather.3.cloned.1.call-update
  36.5 0.3 fusion.6
  36.8 0.0 copy-start.11
  36.8 2.2 %convolution_convert_fusion = bf16[512,512]{0,1:T(8,128)(2,1)S(1)} fusion(bf16[2,1024,512]{2,1,0:T(8,128)(2,1)} %param.17, bf16[512,1024]{1,0:T(8,128)(2,1)S(1)} %bitcast.43, f32[1024]{0:T(1024)S(1)} %copy-done.13, f32[512]{0:T(512)S(1)} %add_rsqrt_fusion), kind=kOutput, calls=%fused_computation.15 | convolution fusion | flops 539230208 | bytes 2627584 | tf_op jit(solution)/shard_map/dot_general | solution.py:25
  39.0 0.8 convolution_convert_fusion.1
  39.9 0.4 copy-done.12
  40.2 0.8 convolution_convert_fusion.2
  41.1 1.3 multiply_reduce_fusion
  42.4 1.4 fusion
  43.8 1.6 divide_convert_fusion
  45.4 0.8 fusion.9
  46.1 0.4 reshape.46
  46.6 2.1 %copy.17 = bf16[2,16,8,2,1024]{4,3,2,1,0:T(2,128)(2,1)} copy(bf16[2,16,8,2,1024]{4,3,0,1,2:T(2,128)(2,1)S(1)} %bitcast.48) | data formatting | bytes 2097152 | tf_op jit(solution)/shard_map/transpose | solution.py:247
  48.7 15.7 %all-to-all-start.1 = ((bf16[256,2,1024]{2,1,0:T(2,128)(2,1)}), bf16[256,2,1024]{2,1,0:T(2,128)(2,1)}, u32[]{:S(2)}, u32[]{:S(2)}) async-start(bf16[256,2,1024]{2,1,0:T(2,128)(2,1)} %bitcast.47), calls=%async_computation.1 | async-start | bytes 2097152 | tf_op jit(solution)/shard_map/all_to_all | solution.py:248
  64.4 29.0 %all-to-all-done.1 = bf16[256,2,1024]{2,1,0:T(2,128)(2,1)} async-done(((bf16[256,2,1024]{2,1,0:T(2,128)(2,1)}), bf16[256,2,1024]{2,1,0:T(2,128)(2,1)}, u32[]{:S(2)}, u32[]{:S(2)}) %all-to-all-start.1) | async-done | bytes 1048608 | tf_op jit(solution)/shard_map/all_to_all | solution.py:248
  93.4 1.6 copy.21
  95.1 0.3 copy-done.3
  95.4 7.4 %time_attention.1.rows_ref = bf16[2,256,1024]{2,1,0:T(8,128)(2,1)S(1)} custom-call(s32[2]{0:T(128)S(1)} %copy-done.6, bf16[2,256,1024]{2,1,0:T(8,128)(2,1)S(1)} %bitcast.38, f32[1,1024]{1,0:T(1,128)S(1)} %bitcast.39, bf16[2,1024,512]{2,1,0:T(8,128)(2,1)S(1)} %copy-done.1, bf16[1024,512]{1,0:T(8,128)(2,1)S(1)} %copy-done.2, bf16[512,1024]{1,0:T(8,128)(2,1)S(1)} %copy-done.3), custom_call_target="tpu_custom_call" | custom-call | flops 3221225472 | bytes 6291456 | tf_op jit(solution)/shard_map/time_attention/pallas_call | solution.py:91
  102.8 1.0 copy-done.7
  103.7 0.1 all-gather.3.cloned.1.call-done
  103.8 1.2 copy-done.8
  105.0 6.3 %feed_forward.3 = bf16[16,2,8,1024]{3,2,1,0:T(8,128)(2,1)S(1)} custom-call(s32[1]{0:T(128)} %bitcast.19.which_ref, bf16[2,256,1024]{2,1,0:T(8,128)(2,1)S(1)} %copy-done.8, f32[1,1024]{1,0:T(1,128)S(1)} %bitcast.40, bf16[2,16,2,64,1024]{4,3,2,1,0:T(8,128)(2,1)} %bitcast.52), custom_call_target="tpu_custom_call" | custom-call | flops 4294967296 | bytes 10485760 | tf_op jit(solution)/shard_map/feed_forward/pallas_call | solution.py:145
  111.3 4.6 %collective-permute-start.1 = (bf16[16,2,8,1024]{3,2,1,0:T(8,128)(2,1)S(1)}, bf16[16,2,8,1024]{3,2,1,0:T(8,128)(2,1)S(1)}, u32[]{:S(2)}, u32[]{:S(2)}) collective-permute-start(bf16[16,2,8,1024]{3,2,1,0:T(8,128)(2,1)S(1)} %feed_forward.3), channel_id=1, source_target_pairs={{0,1},{1,0},{2,3},{3,2},{4,5},{5,4},{6,7},{7,6},{8,9},{9,8},{10,11... | collective-permute-start | bytes 1572872 | tf_op jit(solution)/shard_map/ppermute | solution.py:256
  115.9 6.3 %feed_forward.2 = bf16[16,2,8,1024]{3,2,1,0:T(8,128)(2,1)S(1)} custom-call(s32[1]{0:T(128)} %bitcast.which_ref.high_ref, bf16[2,256,1024]{2,1,0:T(8,128)(2,1)S(1)} %copy-done.8, f32[1,1024]{1,0:T(1,128)S(1)} %bitcast.41, bf16[2,16,2,64,1024]{4,3,2,1,0:T(8,128)(2,1)} %bitcast.53), custom_call_target="tpu_custom_call" | custom-call | flops 4294967296 | bytes 10485760 | tf_op jit(solution)/shard_map/feed_forward/pallas_call | solution.py:145
  122.2 16.0 %all_to_all.20.own_ref = bf16[16,2,8,1024]{3,2,1,0:T(8,128)(2,1)S(1)} all-to-all(bf16[16,2,8,1024]{3,2,1,0:T(8,128)(2,1)S(1)} %feed_forward.2), channel_id=1, replica_groups=mesh['zl'=4,'c'=2,'x'=4,'y'=4,'h'=2] {'x','y'}, dimensions={0} | all-to-all | bytes 1048576 | tf_op jit(solution)/shard_map/all_to_all | solution.py:258
  138.1 2.1 %collective-permute-done.1 = bf16[16,2,8,1024]{3,2,1,0:T(8,128)(2,1)S(1)} collective-permute-done((bf16[16,2,8,1024]{3,2,1,0:T(8,128)(2,1)S(1)}, bf16[16,2,8,1024]{3,2,1,0:T(8,128)(2,1)S(1)}, u32[]{:S(2)}, u32[]{:S(2)}) %collective-permute-start.1) | collective-permute-done | bytes 524320 | tf_op jit(solution)/shard_map/ppermute | solution.py:256
  140.3 15.9 %all_to_all.21.other_ref = bf16[16,2,8,1024]{3,2,1,0:T(8,128)(2,1)S(1)} all-to-all(bf16[16,2,8,1024]{3,2,1,0:T(8,128)(2,1)S(1)} %collective-permute-done.1), channel_id=1, replica_groups=mesh['zl'=4,'c'=2,'x'=4,'y'=4,'h'=2] {'x','y'}, dimensions={0} | all-to-all | bytes 1048576 | tf_op jit(solution)/shard_map/all_to_all | solution.py:259
  156.2 1.7 %reorder.1 = bf16[8,64,1024]{2,1,0:T(8,128)(2,1)} custom-call(s32[1]{0:T(128)} %bitcast.which_ref.high_ref, bf16[16,2,8,1024]{3,2,1,0:T(8,128)(2,1)S(1)} %all_to_all.20.own_ref, bf16[16,2,8,1024]{3,2,1,0:T(8,128)(2,1)S(1)} %all_to_all.21.other_ref), custom_call_target="tpu_custom_call" | custom-call | flops 536870912 | bytes 2097152 | tf_op jit(solution)/shard_map/reorder/pallas_call | solution.py:182
  (29 shorter events, 0.1 us)
Async XLA Ops:
  6.5 38.8 %copy-start = (bf16[512,1024]{1,0:T(8,128)(2,1)S(1)}, bf16[512,1024]{1,0:T(8,128)(2,1)}, u32[]{:S(2)}) copy-start(bf16[512,1024]{1,0:T(8,128)(2,1)} %param.19) | copy-start | bytes 3145732
  6.5 6.2 %copy-start.9 = (bf16[2048,32]{0,1:T(8,128)(2,1)S(1)}, bf16[2048,32]{0,1:T(8,128)(2,1)}, u32[]{:S(2)}) copy-start(bf16[2048,32]{0,1:T(8,128)(2,1)} %param.24) | copy-start | bytes 393220
  6.5 6.2 %copy-start.10 = (bf16[32,2048]{1,0:T(8,128)(2,1)S(1)}, bf16[32,2048]{1,0:T(8,128)(2,1)}, u32[]{:S(2)}) copy-start(bf16[32,2048]{1,0:T(8,128)(2,1)} %param.23) | copy-start | bytes 393220
  6.5 30.2 %copy-start.13 = (f32[1024]{0:T(1024)S(1)}, f32[1024]{0:T(1024)}, u32[]{:S(2)}) copy-start(f32[1024]{0:T(1024)} %param.14) | copy-start | bytes 12292
  6.5 29.9 %all-to-all-start = ((bf16[8,64,1024]{2,1,0:T(8,128)(2,1)}), bf16[8,64,1024]{2,1,0:T(8,128)(2,1)S(1)}, u32[]{:S(2)}, u32[]{:S(2)}) async-start(bf16[8,64,1024]{2,1,0:T(8,128)(2,1)} %param.13), calls=%async_computation | async-start | bytes 2097152 | tf_op jit(solution)/shard_map/all_to_all | solution.py:225
  12.7 91.1 %all-gather.3.cloned.1.call-start = ((), (), s32[]{:S(2)}) async-start(), calls=%async_computation.4 | async-start | bytes 8650752 | tf_op jit(solution)/shard_map/all_gather | solution.py:231
  12.8 22.9 %collective-permute-start = (bf16[2,32,1024]{2,1,0:T(8,128)(2,1)S(1)}, bf16[2,32,1024]{2,1,0:T(8,128)(2,1)S(1)}, u32[]{:S(2)}, u32[]{:S(2)}) collective-permute-start(bf16[2,32,1024]{2,1,0:T(8,128)(2,1)S(1)} %pad_maximum_fusion), channel_id=1, source_target_pairs={{0,193},{64,129},{128,65},{192,1},{1,192},{65,128},{129,64},{193,0... | collective-permute-start | bytes 393224 | tf_op jit(solution)/shard_map/ppermute | solution.py:197
  36.8 2.2 %copy-start.11 = (bf16[2,1024,512]{2,1,0:T(8,128)(2,1)S(1)}, bf16[2,1024,512]{2,1,0:T(8,128)(2,1)}, u32[]{:S(2)}) copy-start(bf16[2,1024,512]{2,1,0:T(8,128)(2,1)} %param.17) | copy-start | bytes 6291460
  39.0 1.2 copy-start.12
  48.7 46.4 %copy-start.1 = (bf16[2,1024,512]{2,1,0:T(8,128)(2,1)S(1)}, bf16[2,1024,512]{2,1,0:T(8,128)(2,1)}, u32[]{:S(2)}) copy-start(bf16[2,1024,512]{2,1,0:T(8,128)(2,1)} %qk_ref.1) | copy-start | bytes 6291460
  48.7 46.4 %copy-start.4 = (f32[1024]{0:T(1024)S(1)}, f32[1024]{0:T(1024)}, u32[]{:S(2)}) copy-start(f32[1024]{0:T(1024)} %param.15) | copy-start | bytes 12292
  48.7 46.4 %copy-start.6 = (s32[2]{0:T(128)S(1)}, s32[2]{0:T(128)}, u32[]{:S(2)}) copy-start(s32[2]{0:T(128)} %start_ref.1) | copy-start | bytes 28
  48.7 44.7 %all-to-all-start.1 = ((bf16[256,2,1024]{2,1,0:T(2,128)(2,1)}), bf16[256,2,1024]{2,1,0:T(2,128)(2,1)}, u32[]{:S(2)}, u32[]{:S(2)}) async-start(bf16[256,2,1024]{2,1,0:T(2,128)(2,1)} %bitcast.47), calls=%async_computation.1 | async-start | bytes 2097152 | tf_op jit(solution)/shard_map/all_to_all | solution.py:248
  93.4 1.7 %copy-start.2 = (bf16[1024,512]{1,0:T(8,128)(2,1)S(1)}, bf16[1024,512]{1,0:T(8,128)(2,1)}, u32[]{:S(2)}) copy-start(bf16[1024,512]{1,0:T(8,128)(2,1)} %v_ref.1) | copy-start | bytes 3145732
  93.4 2.0 %copy-start.3 = (bf16[512,1024]{1,0:T(8,128)(2,1)S(1)}, bf16[512,1024]{1,0:T(8,128)(2,1)}, u32[]{:S(2)}) copy-start(bf16[512,1024]{1,0:T(8,128)(2,1)} %o_ref.1) | copy-start | bytes 3145732
  95.4 8.4 %copy-start.5 = (f32[1024]{0:T(1024)S(1)}, f32[1024]{0:T(1024)}, u32[]{:S(2)}) copy-start(f32[1024]{0:T(1024)} %param.16) | copy-start | bytes 12292
  102.8 1.0 copy-start.7
  103.8 1.2 copy-start.8
  111.3 28.9 %collective-permute-start.1 = (bf16[16,2,8,1024]{3,2,1,0:T(8,128)(2,1)S(1)}, bf16[16,2,8,1024]{3,2,1,0:T(8,128)(2,1)S(1)}, u32[]{:S(2)}, u32[]{:S(2)}) collective-permute-start(bf16[16,2,8,1024]{3,2,1,0:T(8,128)(2,1)S(1)} %feed_forward.3), channel_id=1, source_target_pairs={{0,1},{1,0},{2,3},{3,2},{4,5},{5,4},{6,7},{7,6},{8,9},{9,8},{10,11... | collective-permute-start | bytes 1572872 | tf_op jit(solution)/shard_map/ppermute | solution.py:256
Sparse Core Ops, SparseCore 0:
  36.6 67.1 all-gather.2
